TPU v7x, 128 devices: a whole 4x4x4 slice. The times are simulated.
128 devices in a mesh: tm: 32 (over z, x_hi, y), rows: 4 (over x_lo, core).
Axes of the slice: x: 4 (x_hi: 2, x_lo: 2; x = x_hi * 2 + x_lo), y: 4, z: 4, core: 2. Of those that a mesh axis runs over, the one named last changes fastest.
Arguments:
- video_clip: bfloat16 [256, 56, 7, 512], P('tm', 'rows'), may hold values from -6 to 6
- cotangent: bfloat16 [256, 56, 7, 512], P('tm', 'rows'), may hold values from -6 to 6
- gain_first: float32 [512], replicated, may hold values from 0.1 to 1.9
- bias_first: float32 [512], replicated, may hold values from -3 to 3
- qkv_first: bfloat16 [512, 1536], replicated
- out_first: bfloat16 [512, 512], replicated, may hold values from -0.25 to 0.25
- gain_second: float32 [512], replicated, may hold values from 0.1 to 1.9
- bias_second: float32 [512], replicated, may hold values from -3 to 3
- qkv_second: bfloat16 [512, 1536], replicated
- out_second: bfloat16 [512, 512], replicated, may hold values from -0.25 to 0.25
Outputs:
- grad_clip: bfloat16 [256, 56, 7, 512], P('tm', 'rows')
- grad_qkv_first: float32 [512, 1536], P(('tm', 'rows'))
- grad_out_first: float32 [512, 512], P(('tm', 'rows'))
- grad_qkv_second: float32 [512, 1536], P(('tm', 'rows'))
- grad_out_second: float32 [512, 512], P(('tm', 'rows'))
All inputs are finite; a program needn't handle non-finite values.
Results may differ from a plain program's by a relative error of at most 0.03.
Values may be sent and summed in bfloat16 or wider, within the bound.
A program may use at most 256 MiB of HBM per device.

v0:
```python
import math

import jax
import jax.numpy as jnp
from jax import lax
from jax.sharding import PartitionSpec as P

HEADS = 16
WT = 8
WH = 7
WW = 7


def from_behind_2(block, axis, distance):
    devices = range(lax.axis_size(axis))
    route = [((i - distance) % len(devices), i) for i in devices]
    return lax.ppermute(block, axis, route)


def to_windows(volume):
    frames, rows_here, columns, channels = volume.shape
    blocked = volume.reshape(frames // WT, WT, rows_here // WH, WH, columns // WW, WW, channels)
    blocked = blocked.transpose(0, 2, 4, 1, 3, 5, 6)
    return blocked.reshape(-1, WT * WH * WW, channels)


def from_windows(windowed, frames, rows_here, columns):
    channels = windowed.shape[-1]
    blocked = windowed.reshape(frames // WT, rows_here // WH, columns // WW, WT, WH, WW, channels)
    return blocked.transpose(0, 3, 1, 4, 2, 5, 6).reshape(frames, rows_here, columns, channels)


def region(position, length, extent):
    return jnp.where(
        position < length - extent, 0, jnp.where(position < length - extent // 2, 1, 2)
    ).astype(jnp.int32)


def region_labels(time_pos, time_len, row_pos, row_len, columns):
    col_pos = jnp.arange(columns, dtype=jnp.int32)
    labels = (
        region(time_pos, time_len, WT)[:, None, None] * 9
        + region(row_pos, row_len, WH)[None, :, None] * 3
        + region(col_pos, columns, WW)[None, None, :]
    )
    return to_windows(labels[..., None])[..., 0]


def normalize(values_in, norm_gain, norm_bias):
    center = values_in - jnp.mean(values_in, axis=-1, keepdims=True)
    spread = jnp.mean(center * center, axis=-1, keepdims=True)
    return (center * lax.rsqrt(spread + 1e-05) * norm_gain + norm_bias).astype(jnp.bfloat16)


def attend(projected, same_region):
    windows, length, triple = projected.shape
    channels = triple // 3
    head_size = channels // HEADS
    packed = lax.optimization_barrier(projected.astype(jnp.bfloat16))
    packed = packed.astype(jnp.float32).reshape(windows, length, 3, HEADS, head_size)
    query_rows = packed[:, :, 0]
    key_rows = packed[:, :, 1]
    value_rows = packed[:, :, 2]
    scores = jnp.einsum("nqhd,nkhd->nhqk", query_rows, key_rows) * head_size ** (-0.5)
    scores = jnp.where(same_region[:, None], scores, -1000000000.0)
    weights = lax.optimization_barrier(jax.nn.softmax(scores, axis=-1).astype(jnp.bfloat16))
    mixed = jnp.einsum("nhqk,nkhd->nqhd", weights.astype(jnp.float32), value_rows)
    return mixed.astype(jnp.bfloat16).reshape(windows, length, channels)


def forward_block(windows_in, norm_gain, norm_bias, w_qkv, same_region):
    windows, length, channels = windows_in.shape
    input_float = windows_in.astype(jnp.float32)
    normed, pull_norm = jax.vjp(
        lambda values_in: normalize(values_in, norm_gain, norm_bias), input_float
    )
    normed_rows = normed.reshape(-1, channels)
    projected = jnp.dot(normed_rows, w_qkv, preferred_element_type=jnp.float32).reshape(
        windows, length, 3 * channels
    )
    mixed, pull_attend = jax.vjp(lambda inner: attend(inner, same_region), projected)
    return (input_float, normed_rows, mixed, pull_norm, pull_attend)


def block_output(saved, w_out):
    input_float, normed_rows, mixed, pull_norm, pull_attend = saved
    channels = mixed.shape[-1]
    added = jnp.dot(mixed.reshape(-1, channels), w_out, preferred_element_type=jnp.float32)
    return (input_float + added.reshape(input_float.shape)).astype(jnp.bfloat16)


def backward_block(saved, grads_in, w_qkv, w_out):
    input_float, normed_rows, mixed, pull_norm, pull_attend = saved
    channels = mixed.shape[-1]
    grad_rows = grads_in.reshape(-1, channels)
    mixed_rows = mixed.reshape(-1, channels)
    grad_out = jnp.dot(mixed_rows.T, grad_rows, preferred_element_type=jnp.float32)
    d_mixed = jnp.dot(grad_rows, w_out.T, preferred_element_type=jnp.float32).astype(jnp.bfloat16)
    (d_projected,) = pull_attend(d_mixed.reshape(mixed.shape))
    d_projected = d_projected.astype(jnp.bfloat16).reshape(-1, 3 * channels)
    grad_qkv = jnp.dot(normed_rows.T, d_projected, preferred_element_type=jnp.float32)
    d_normed = jnp.dot(d_projected, w_qkv.T, preferred_element_type=jnp.float32).astype(
        jnp.bfloat16
    )
    (d_input,) = pull_norm(d_normed.reshape(input_float.shape))
    d_total = (grads_in.astype(jnp.float32) + d_input).astype(jnp.bfloat16)
    return (d_total, grad_qkv, grad_out)


def shift_in(volume):
    time_axis = volume.ndim - 4
    half_frames = WT // 2
    band = WH // 2
    from_ahead = from_behind_2(lax.slice_in_dim(volume, 0, half_frames, axis=time_axis), "tm", -1)
    volume = jnp.concatenate(
        [
            lax.slice_in_dim(volume, half_frames, volume.shape[time_axis], axis=time_axis),
            from_ahead,
        ],
        axis=time_axis,
    )
    row_axis = time_axis + 1
    from_below = from_behind_2(lax.slice_in_dim(volume, 0, band, axis=row_axis), "rows", -1)
    volume = jnp.concatenate(
        [lax.slice_in_dim(volume, band, volume.shape[row_axis], axis=row_axis), from_below],
        axis=row_axis,
    )
    return jnp.roll(volume, -(WW // 2), axis=time_axis + 2)


def shift_out(volume):
    half_frames = WT // 2
    band = WH // 2
    volume = jnp.roll(volume, WW // 2, axis=2)
    row_count = volume.shape[1]
    from_above = from_behind_2(
        lax.slice_in_dim(volume, row_count - band, row_count, axis=1), "rows", 1
    )
    volume = jnp.concatenate(
        [from_above, lax.slice_in_dim(volume, 0, row_count - band, axis=1)], axis=1
    )
    frame_count = volume.shape[0]
    from_behind = from_behind_2(
        lax.slice_in_dim(volume, frame_count - half_frames, frame_count, axis=0), "tm", 1
    )
    return jnp.concatenate(
        [from_behind, lax.slice_in_dim(volume, 0, frame_count - half_frames, axis=0)], axis=0
    )


def per_device(
    video_clip,
    cotangent,
    gain_first,
    bias_first,
    qkv_first,
    out_first,
    gain_second,
    bias_second,
    qkv_second,
    out_second,
):
    frames, rows_here, columns, channels = video_clip.shape
    time_count = lax.axis_size("tm")
    band_count = lax.axis_size("rows")
    grad_scale = 1.0 / math.sqrt(frames * time_count * rows_here * band_count * columns)
    cot_second = shift_in(cotangent)
    clip_windows = to_windows(video_clip)
    window_count, length, unused_channels = clip_windows.shape
    open_mask = jnp.ones((window_count, length, length), bool)
    saved_first = forward_block(clip_windows, gain_first, bias_first, qkv_first, open_mask)
    first_out = from_windows(block_output(saved_first, out_first), frames, rows_here, columns)
    input_second = shift_in(first_out)
    time_pos = lax.axis_index("tm") * frames + jnp.arange(frames, dtype=jnp.int32)
    row_pos = lax.axis_index("rows") * rows_here + jnp.arange(rows_here, dtype=jnp.int32)
    labels = region_labels(time_pos, frames * time_count, row_pos, rows_here * band_count, columns)
    same_region = labels[:, :, None] == labels[:, None, :]
    saved_second = forward_block(
        to_windows(input_second), gain_second, bias_second, qkv_second, same_region
    )
    d_second, grad_qkv_second, grad_out_second = backward_block(
        saved_second, to_windows(cot_second), qkv_second, out_second
    )
    cot_first = shift_out(from_windows(d_second, frames, rows_here, columns))
    d_first, grad_qkv_first, grad_out_first = backward_block(
        saved_first, to_windows(cot_first), qkv_first, out_first
    )
    grad_qkv_first, grad_out_first, grad_qkv_second, grad_out_second = (
        lax.psum_scatter(
            grad_qkv_first * grad_scale, ("tm", "rows"), scatter_dimension=0, tiled=True
        ),
        lax.psum_scatter(
            grad_out_first * grad_scale, ("tm", "rows"), scatter_dimension=0, tiled=True
        ),
        lax.psum_scatter(
            grad_qkv_second * grad_scale, ("tm", "rows"), scatter_dimension=0, tiled=True
        ),
        lax.psum_scatter(
            grad_out_second * grad_scale, ("tm", "rows"), scatter_dimension=0, tiled=True
        ),
    )
    grad_clip = from_windows(d_first, frames, rows_here, columns)
    return (grad_clip, grad_qkv_first, grad_out_first, grad_qkv_second, grad_out_second)


def solution(mesh):
    placed = (
        P("tm", "rows", None, None),
        P("tm", "rows", None, None),
        P(),
        P(),
        P(),
        P(),
        P(),
        P(),
        P(),
        P(),
    )
    return jax.shard_map(
        per_device,
        mesh=mesh,
        in_specs=placed,
        out_specs=(
            P("tm", "rows", None, None),
            P(("tm", "rows"), None),
            P(("tm", "rows"), None),
            P(("tm", "rows"), None),
            P(("tm", "rows"), None),
        ),
        check_vma=False,
    )
```

profile of v0, /device:TPU:0, one launch (start us, length us, event | category | flops | bytes accessed | tf_op | source)
XLA Modules:
  0.0 513.6 jit_solution(1771419617128690461)
XLA Ops:
  16.2 4.4 convolution_convert_fusion.3
  20.6 4.5 copy.234
  25.1 14.1 %fusion.77 = (f32[2,16,392]{2,1,0:T(8,128)S(1)}, f32[2,16,392,392]{2,3,1,0:T(8,128)}) fusion(bf16[2,392,3,16,32]{1,4,3,2,0:T(8,128)(2,1)} %bitcast.214), kind=kOutput, calls=%fused_computation.158 | convolution fusion | flops 329456000 | bytes 21816320 | tf_op jit(solution)/shard_map/jvp()/sub | solution.py:66
  39.2 11.1 %divide_convert_fusion.1 = bf16[2,16,392,392]{2,3,1,0:T(8,128)(2,1)S(1)} fusion(f32[2,16,392,392]{2,3,1,0:T(8,128)} %get-tuple-element.26, f32[2,16,392]{2,1,0:T(8,128)S(1)} %get-tuple-element.25), kind=kLoop, calls=%fused_computation.20 | loop fusion | flops 9834496 | bytes 29553664 | tf_op jit(solution)/shard_map/jvp()/convert_element_type | solution.py:66
  58.1 9.5 %collective-permute-start.2 = (bf16[4,14,7,512]{3,0,2,1:T(4,128)(2,1)}, bf16[4,14,7,512]{3,0,2,1:T(4,128)(2,1)}, u32[]{:S(2)}, u32[]{:S(2)}) collective-permute-start(bf16[4,14,7,512]{3,0,2,1:T(4,128)(2,1)} %bitcast.21), channel_id=1, source_target_pairs={{4,0},{8,4},{12,8},{16,12},{20,16},{24,20},{28,24},{32,28},{36,32}... | collective-permute-start | bytes 1204232 | tf_op jit(solution)/shard_map/ppermute | solution.py:17
  79.4 7.0 %collective-permute-done = bf16[4,14,7,512]{3,2,1,0:T(8,128)(2,1)} collective-permute-done((bf16[4,14,7,512]{3,2,1,0:T(8,128)(2,1)}, bf16[4,14,7,512]{3,2,1,0:T(8,128)(2,1)}, u32[]{:S(2)}, u32[]{:S(2)}) %collective-permute-start) | collective-permute-done | bytes 401440 | tf_op jit(solution)/shard_map/ppermute | solution.py:17
  96.0 4.4 convolution_convert_fusion.2
  100.4 4.7 copy.248
  105.2 15.3 %fusion.78 = (f32[2,16,392]{2,1,0:T(8,128)S(1)}, f32[2,16,392,392]{2,3,1,0:T(8,128)}) fusion(pred[2,392,392]{1,2,0:T(8,128)(4,1)} %broadcast_compare_fusion, bf16[2,392,3,16,32]{1,4,3,2,0:T(8,128)(2,1)} %bitcast.219), kind=kOutput, calls=%fused_computation.159 | convolution fusion | flops 334373248 | bytes 22217728 | tf_op jit(solution)/shard_map/jvp()/sub | solution.py:66
  133.9 7.7 %convolution_convert_fusion.1 = bf16[2,16,392,392]{2,3,1,0:T(8,128)(2,1)} fusion(bf16[2,392,3,16,32]{1,4,3,2,0:T(8,128)(2,1)} %bitcast.220, bf16[2,16,32,392]{3,0,2,1:T(2,128)(2,1)S(1)} %bitcast.224), kind=kOutput, calls=%fused_computation.26 | convolution fusion | flops 319621120 | bytes 11685888 | tf_op jit(solution)/shard_map/transpose(jvp(nhqk,nkhd->nqhd))/dot_general | solution.py:67
  141.6 21.3 %divide_convert_fusion = (bf16[2,16,392,392]{2,3,1,0:T(8,128)(2,1)}, f32[2,16,392]{2,1,0:T(8,128)S(1)}) fusion(f32[2,16,392,392]{2,3,1,0:T(8,128)} %get-tuple-element.28, f32[2,16,392]{2,1,0:T(8,128)S(1)} %copy-done.43, f32[2,16,392]{2,1,0:T(8,128)S(1)} %copy-done.44, bf16[2,16,392,392]{2,3,1,0:T(8,128)(2,1)} %convolution_convert_fusion.1), kind=kLoop, calls=%fused_computation.17 | loop fusion | flops 29490944 | bytes 39488512 | tf_op jit(solution)/shard_map/jvp()/convert_element_type | solution.py:66
  163.6 17.2 %convolution_bitcast_fusion.6 = f32[2,392,1,16,32]{1,4,3,0,2:T(8,128)} fusion(bf16[2,392,3,16,32]{1,4,3,2,0:T(8,128)(2,1)} %bitcast.221, f32[2,16,392,392]{2,3,1,0:T(8,128)} %get-tuple-element.28, bf16[2,16,392,392]{2,3,1,0:T(8,128)(2,1)} %convolution_convert_fusion.1, f32[2,16,392]{2,1,0:T(8,128)} %neg.18, f32[2,16,392]{2,1,0:T(8,128)} %copy-done.42, ...), kind=kOutput, calls=%fused_computation.49 | convolution fusion | flops 344207360 | bytes 41721856 | tf_op jit(solution)/shard_map/transpose(jvp(nqhd,nkhd->nhqk))/dot_general | solution.py:64
  180.7 17.0 %convolution_bitcast_fusion.5 = f32[2,392,1,16,32]{1,4,3,0,2:T(8,128)} fusion(bf16[2,392,3,16,32]{1,4,3,2,0:T(8,128)(2,1)} %bitcast.222, f32[2,16,392,392]{2,3,1,0:T(8,128)} %get-tuple-element.28, bf16[2,16,392,392]{2,3,1,0:T(8,128)(2,1)} %convolution_convert_fusion.1, f32[2,16,392]{2,1,0:T(8,128)} %neg.18, f32[2,16,392]{2,1,0:T(8,128)} %copy-done.42, ...), kind=kOutput, calls=%fused_computation.48 | convolution fusion | flops 344207360 | bytes 41721856 | tf_op jit(solution)/shard_map/transpose(jvp(nqhd,nkhd->nhqk))/dot_general | solution.py:64
  197.7 8.4 %convolution_bitcast_fusion.7 = f32[2,392,1,16,32]{1,4,3,0,2:T(8,128)S(1)} fusion(bf16[2,16,392,392]{2,3,1,0:T(8,128)(2,1)} %get-tuple-element.9, bf16[2,16,32,392]{3,0,2,1:T(2,128)(2,1)S(1)} %bitcast.225), kind=kOutput, calls=%fused_computation.50 | convolution fusion | flops 314703872 | bytes 12242944 | tf_op jit(solution)/shard_map/transpose(jvp(nhqk,nkhd->nqhd))/dot_general | solution.py:67
  208.9 4.5 copy.259
  236.6 7.1 %fusion.45 = bf16[2,392,16,32]{1,3,2,0:T(8,128)(2,1)S(1)} fusion(bf16[2,16,392,392]{2,3,1,0:T(8,128)(2,1)} %get-tuple-element.9, bf16[2,392,3,16,32]{1,4,3,2,0:T(8,128)(2,1)S(1)} %bitcast.223), kind=kOutput, calls=%fused_computation.86 | convolution fusion | flops 315105280 | bytes 11685888 | tf_op jit(solution)/shard_map/jvp(nhqk,nkhd->nqhd)/dot_general | solution.py:67
  253.5 9.9 %collective-permute-done.5 = bf16[4,14,7,512]{3,0,2,1:T(4,128)(2,1)} collective-permute-done((bf16[4,14,7,512]{3,0,2,1:T(4,128)(2,1)}, bf16[4,14,7,512]{3,0,2,1:T(4,128)(2,1)}, u32[]{:S(2)}, u32[]{:S(2)}) %collective-permute-start.5) | collective-permute-done | bytes 401440 | tf_op jit(solution)/shard_map/ppermute | solution.py:17
  270.4 9.6 %convolution_bitcast_fusion.4 = f32[2,392,1,16,32]{1,4,3,0,2:T(8,128)} fusion(bf16[2,16,392,392]{2,3,1,0:T(8,128)(2,1)} %copy-done.2, bf16[2,16,32,392]{3,0,2,1:T(2,128)(2,1)S(1)} %bitcast.226), kind=kOutput, calls=%fused_computation.47 | convolution fusion | flops 314703872 | bytes 12242944 | tf_op jit(solution)/shard_map/transpose(jvp(nhqk,nkhd->nqhd))/dot_general | solution.py:67
  280.0 7.8 %convolution_convert_fusion = bf16[2,16,392,392]{2,3,1,0:T(8,128)(2,1)} fusion(bf16[2,392,3,16,32]{1,4,3,2,0:T(8,128)(2,1)} %bitcast.215, bf16[2,16,32,392]{3,0,2,1:T(2,128)(2,1)S(1)} %bitcast.227), kind=kOutput, calls=%fused_computation.25 | convolution fusion | flops 319621120 | bytes 11685888 | tf_op jit(solution)/shard_map/transpose(jvp(nhqk,nkhd->nqhd))/dot_general | solution.py:67
  287.8 14.2 %fusion.12 = f32[2,16,392]{2,1,0:T(8,128)S(1)} fusion(f32[2,16,392,392]{2,3,1,0:T(8,128)} %get-tuple-element.26, bf16[2,16,392,392]{2,3,1,0:T(8,128)(2,1)} %convolution_convert_fusion, f32[2,16,392]{2,1,0:T(8,128)S(1)} %copy-done.41), kind=kLoop, calls=%fused_computation.16 | loop fusion | flops 19656448 | bytes 29603840 | tf_op jit(solution)/shard_map/transpose(jvp())/reduce_sum | solution.py:66
  302.1 16.3 %convolution_bitcast_fusion.3 = f32[2,392,1,16,32]{1,4,3,0,2:T(8,128)} fusion(bf16[2,392,3,16,32]{1,4,3,2,0:T(8,128)(2,1)} %bitcast.216, f32[2,16,392,392]{2,3,1,0:T(8,128)} %get-tuple-element.26, bf16[2,16,392,392]{2,3,1,0:T(8,128)(2,1)} %convolution_convert_fusion, f32[2,16,392]{2,1,0:T(8,128)S(1)} %neg.20, f32[2,16,392]{2,1,0:T(8,128)S(1)} %copy-done.40), kind=kOutput, calls=%fused_computation.46 | convolution fusion | flops 339290112 | bytes 41289728 | tf_op jit(solution)/shard_map/transpose(jvp(nqhd,nkhd->nhqk))/dot_general | solution.py:64
  318.3 16.5 %convolution_bitcast_fusion.2 = f32[2,392,1,16,32]{1,4,3,0,2:T(8,128)} fusion(bf16[2,392,3,16,32]{1,4,3,2,0:T(8,128)(2,1)} %bitcast.217, f32[2,16,392,392]{2,3,1,0:T(8,128)} %get-tuple-element.26, bf16[2,16,392,392]{2,3,1,0:T(8,128)(2,1)} %convolution_convert_fusion, f32[2,16,392]{2,1,0:T(8,128)S(1)} %neg.20, f32[2,16,392]{2,1,0:T(8,128)S(1)} %copy-done.40), kind=kOutput, calls=%fused_computation.45 | convolution fusion | flops 339290112 | bytes 41289728 | tf_op jit(solution)/shard_map/transpose(jvp(nqhd,nkhd->nhqk))/dot_general | solution.py:64
  351.9 4.7 copy.275
  373.6 129.9 %all-reduce.13.cloned.1.call-done = (f32[512,1536]{1,0:T(8,128)}, f32[512,512]{1,0:T(8,128)}, f32[512,1536]{1,0:T(8,128)}, f32[512,512]{1,0:T(8,128)}) async-done(((f32[512,1536]{1,0:T(8,128)}, f32[512,512]{1,0:T(8,128)}, f32[512,1536]{1,0:T(8,128)}, f32[512,512]{1,0:T(8,128)}), (f32[512,1536]{1,0:T(8,128)}, f32[512,512]{1,0:T(8,128)}, f32[512,1536]{1,0:T(8,128)}, ...) | async-done | bytes 8388624
  (247 shorter events, 131.1 us)
Async XLA Ops:
  7.2 88.8 %copy-start = (bf16[512,1536]{1,0:T(8,128)(2,1)S(1)}, bf16[512,1536]{1,0:T(8,128)(2,1)}, u32[]{:S(2)}) copy-start(bf16[512,1536]{1,0:T(8,128)(2,1)} %param.18) | copy-start | bytes 4718596
  7.2 496.3 %all-reduce.13.cloned.1.call-start = ((), (), s32[]{:S(2)}) async-start(), calls=%async_computation | async-start | bytes 16777216
  11.9 8.7 %copy-start.31 = (f32[2,8,7,7]{1,3,2,0:T(8,128)}, f32[2,8,7,7]{1,3,2,0:T(8,128)S(1)}, u32[]{:S(2)}) copy-start(f32[2,8,7,7]{1,3,2,0:T(8,128)S(1)} %fusion.64) | copy-start | bytes 9412
  12.2 8.4 %copy-start.48 = (f32[2,392]{1,0:T(2,128)}, f32[2,392]{1,0:T(2,128)S(1)}, u32[]{:S(2)}) copy-start(f32[2,392]{1,0:T(2,128)S(1)} %rsqrt.39) | copy-start | bytes 9412
  12.3 8.3 %copy-start.50 = (f32[2,392]{1,0:T(2,128)}, f32[2,392]{1,0:T(2,128)S(1)}, u32[]{:S(2)}) copy-start(f32[2,392]{1,0:T(2,128)S(1)} %div.105) | copy-start | bytes 9412
  39.2 32.4 %copy-start.39 = (f32[2,16,392]{2,1,0:T(8,128)}, f32[2,16,392]{2,1,0:T(8,128)S(1)}, u32[]{:S(2)}) copy-start(f32[2,16,392]{2,1,0:T(8,128)S(1)} %get-tuple-element.25) | copy-start | bytes 150532
  39.2 11.1 %copy-start.8 = (bf16[2,392,1536]{1,2,0:T(8,128)(2,1)S(1)}, bf16[2,392,1536]{1,2,0:T(8,128)(2,1)}, u32[]{:S(2)}) copy-start(bf16[2,392,1536]{1,2,0:T(8,128)(2,1)} %copy.234) | copy-start | bytes 7225348
  56.0 11.6 %copy-start.25 = (bf16[8,14,7,512]{3,0,2,1:T(8,128)(2,1)S(1)}, bf16[8,14,7,512]{3,0,2,1:T(8,128)(2,1)}, u32[]{:S(2)}) copy-start(bf16[8,14,7,512]{3,0,2,1:T(8,128)(2,1)} %param.11) | copy-start | bytes 2408452
  58.1 20.2 %collective-permute-start.2 = (bf16[4,14,7,512]{3,0,2,1:T(4,128)(2,1)}, bf16[4,14,7,512]{3,0,2,1:T(4,128)(2,1)}, u32[]{:S(2)}, u32[]{:S(2)}) collective-permute-start(bf16[4,14,7,512]{3,0,2,1:T(4,128)(2,1)} %bitcast.21), channel_id=1, source_target_pairs={{4,0},{8,4},{12,8},{16,12},{20,16},{24,20},{28,24},{32,28},{36,32}... | collective-permute-start | bytes 1204232 | tf_op jit(solution)/shard_map/ppermute | solution.py:17
  69.5 16.8 %collective-permute-start = (bf16[4,14,7,512]{3,2,1,0:T(8,128)(2,1)}, bf16[4,14,7,512]{3,2,1,0:T(8,128)(2,1)}, u32[]{:S(2)}, u32[]{:S(2)}) collective-permute-start(bf16[4,14,7,512]{3,2,1,0:T(8,128)(2,1)} %copy.301), channel_id=1, source_target_pairs={{4,0},{8,4},{12,8},{16,12},{20,16},{24,20},{28,24},{32,28},{36,32}... | collective-permute-start | bytes 1204232 | tf_op jit(solution)/shard_map/ppermute | solution.py:17
  79.3 10.1 %collective-permute-start.3 = (bf16[8,3,7,512]{3,0,2,1:T(8,128)(2,1)S(1)}, bf16[8,3,7,512]{3,0,2,1:T(8,128)(2,1)S(1)}, u32[]{:S(2)}, u32[]{:S(2)}) collective-permute-start(bf16[8,3,7,512]{3,0,2,1:T(8,128)(2,1)S(1)} %pad_maximum_fusion.5), channel_id=1, source_target_pairs={{1,0},{2,1},{3,2},{0,3},{5,4},{6,5},{7,6},{4,7},{9,8},{10,9},{11,1... | collective-permute-start | bytes 516104 | tf_op jit(solution)/shard_map/ppermute | solution.py:17
  88.1 33.0 %collective-permute-start.1 = (bf16[8,3,7,512]{3,2,1,0:T(8,128)(2,1)}, bf16[8,3,7,512]{3,2,1,0:T(8,128)(2,1)}, u32[]{:S(2)}, u32[]{:S(2)}) collective-permute-start(bf16[8,3,7,512]{3,2,1,0:T(8,128)(2,1)} %slice.109), channel_id=1, source_target_pairs={{1,0},{2,1},{3,2},{0,3},{5,4},{6,5},{7,6},{4,7},{9,8},{10,9},{11,1... | collective-permute-start | bytes 516104 | tf_op jit(solution)/shard_map/ppermute | solution.py:17
  91.5 8.9 %copy-start.37 = (f32[2,8,7,7]{1,3,2,0:T(8,128)}, f32[2,8,7,7]{1,3,2,0:T(8,128)S(1)}, u32[]{:S(2)}) copy-start(f32[2,8,7,7]{1,3,2,0:T(8,128)S(1)} %multiply_reduce_fusion.3) | copy-start | bytes 9412
  91.7 8.7 %copy-start.33 = (f32[2,8,7,7]{1,3,2,0:T(8,128)}, f32[2,8,7,7]{1,3,2,0:T(8,128)S(1)}, u32[]{:S(2)}) copy-start(f32[2,8,7,7]{1,3,2,0:T(8,128)S(1)} %fusion.65) | copy-start | bytes 9412
  92.0 8.4 %copy-start.52 = (f32[2,392]{1,0:T(2,128)}, f32[2,392]{1,0:T(2,128)S(1)}, u32[]{:S(2)}) copy-start(f32[2,392]{1,0:T(2,128)S(1)} %rsqrt.41) | copy-start | bytes 9412
  197.7 8.4 %copy-start.18 = (f32[2,392,1,16,32]{1,4,3,0,2:T(8,128)S(1)}, f32[2,392,1,16,32]{1,4,3,0,2:T(8,128)}, u32[]{:S(2)}) copy-start(f32[2,392,1,16,32]{1,4,3,0,2:T(8,128)} %convolution_bitcast_fusion.6) | copy-start | bytes 4816900
  197.7 8.4 %copy-start.19 = (f32[2,392,1,16,32]{1,4,3,0,2:T(8,128)S(1)}, f32[2,392,1,16,32]{1,4,3,0,2:T(8,128)}, u32[]{:S(2)}) copy-start(f32[2,392,1,16,32]{1,4,3,0,2:T(8,128)} %convolution_bitcast_fusion.5) | copy-start | bytes 4816900
  236.0 7.7 %collective-permute-start.4 = (bf16[8,3,7,512]{3,0,2,1:T(8,128)(2,1)S(1)}, bf16[8,3,7,512]{3,0,2,1:T(8,128)(2,1)S(1)}, u32[]{:S(2)}, u32[]{:S(2)}) collective-permute-start(bf16[8,3,7,512]{3,0,2,1:T(8,128)(2,1)S(1)} %pad_maximum_fusion.4), channel_id=1, source_target_pairs={{3,0},{0,1},{1,2},{2,3},{7,4},{4,5},{5,6},{6,7},{11,8},{8,9},{9,10... | collective-permute-start | bytes 516104 | tf_op jit(solution)/shard_map/ppermute | solution.py:17
  236.6 8.3 %copy-start.20 = (f32[1,2,1,8,7,7,512]{6,1,5,4,3,2,0:T(2,128)S(1)}, f32[1,2,1,8,7,7,512]{6,1,5,4,3,2,0:T(2,128)}, u32[]{:S(2)}) copy-start(f32[1,2,1,8,7,7,512]{6,1,5,4,3,2,0:T(2,128)} %copy.244) | copy-start | bytes 4816900
  244.9 18.5 %collective-permute-start.5 = (bf16[4,14,7,512]{3,0,2,1:T(4,128)(2,1)}, bf16[4,14,7,512]{3,0,2,1:T(4,128)(2,1)}, u32[]{:S(2)}, u32[]{:S(2)}) collective-permute-start(bf16[4,14,7,512]{3,0,2,1:T(4,128)(2,1)} %get-tuple-element.11), channel_id=1, source_target_pairs={{124,0},{0,4},{4,8},{8,12},{12,16},{16,20},{20,24},{24,28},{28,32}... | collective-permute-start | bytes 1204232 | tf_op jit(solution)/shard_map/ppermute | solution.py:17
  280.0 7.8 %copy-start.41 = (f32[2,16,392]{2,1,0:T(8,128)S(1)}, f32[2,16,392]{2,1,0:T(8,128)}, u32[]{:S(2)}) copy-start(f32[2,16,392]{2,1,0:T(8,128)} %multiply_divide_fusion) | copy-start | bytes 150532
  287.8 14.2 %copy-start.40 = (f32[2,16,392]{2,1,0:T(8,128)S(1)}, f32[2,16,392]{2,1,0:T(8,128)}, u32[]{:S(2)}) copy-start(f32[2,16,392]{2,1,0:T(8,128)} %copy-done.39) | copy-start | bytes 150532
  318.3 16.5 %copy-start.24 = (bf16[784,512]{0,1:T(8,128)(2,1)S(1)}, bf16[784,512]{0,1:T(8,128)(2,1)}, u32[]{:S(2)}) copy-start(bf16[784,512]{0,1:T(8,128)(2,1)} %reshape.431) | copy-start | bytes 2408452
  370.0 136.3 %copy-start.1 = (bf16[512,1536]{1,0:T(8,128)(2,1)S(1)}, bf16[512,1536]{1,0:T(8,128)(2,1)}, u32[]{:S(2)}) copy-start(bf16[512,1536]{1,0:T(8,128)(2,1)} %param.18) | copy-start | bytes 4718596
  (44 other events, 147.0 us)
Sparse Core Ops, SparseCore 0:
  345.7 157.7 all-reduce.12
where the time goes:
time: 524 us; the launch traced here: 514 us
  matrix products  172 us (33%)
  waiting for transfers between devices  147 us (28%)
  local copies, waits for them, and re-layouts  85.2 us (16%)
  other arithmetic  82.8 us (16%)
  between operations  15.4 us (3%)
  starting transfers between devices  11 us (2%)
    unnamed x2, waiting for transfers between devices  130 us
    dot_general x4, matrix products, attend(): jnp.einsum('nqhd,nkhd->nhqk', query_rows, key_rows) * head_size ** (-0.5)  66.9 us
    dot_general x6, matrix products, attend(): jnp.einsum('nhqk,nkhd->nqhd', weights.astype(jnp.float32), value_rows)  43 us
    convert_element_type x2, other arithmetic, attend(): jax.nn.softmax(scores, axis=-1).astype(jnp.bfloat16)  32.4 us
    sub x2, matrix products, attend(): jax.nn.softmax(scores, axis=-1).astype(jnp.bfloat16)  29.4 us
    optimization_barrier x4, local copies, waits for them, and re-layouts, attend(): packed = lax.optimization_barrier(projected.astype(jnp.bfloat16))  18.5 us
    convert_element_type x6, local copies, waits for them, and re-layouts, forward_block(): input_float = windows_in.astype(jnp.float32)  17.6 us
    ppermute x6, waiting for transfers between devices, from_behind_2(): return lax.ppermute(block, axis, route)  16.9 us
  transfers between devices with their start and end apart: 7, of which 3 were waited for; matrix products, arithmetic and copies ran while one was open for 17% of the time, Pallas kernels for 0%

commit v1 on v0

v1 whole, which is shorter than its diff:
```python
import functools
import math

import jax
import jax.numpy as jnp
from jax import lax
from jax.experimental import pallas as pl
from jax.experimental.pallas import tpu as pltpu
from jax.sharding import PartitionSpec as P

F32, BF16 = jnp.float32, jnp.bfloat16
C, HEADS, HD = 512, 16, 32
TOK = 392
GROUP = 4
VROWS = 48
LOG2E = math.log2(math.e)
QSCALE = HD ** (-0.5) * LOG2E
MASKED = -1000000000.0 * LOG2E
LOW, HIGH = 2.0**-60, 2.0**100
WHOLE = ((0, 392, 0),)
SPLIT = ((0, 224, 0), (224, 392, 256))
VMEM_LIMIT = 56 * 1024 * 1024


def mm(a, b):
    return lax.dot_general(a, b, (((1,), (0,)), ((), ())), preferred_element_type=F32)


def mm_nt(a, b):
    return lax.dot_general(a, b, (((1,), (1,)), ((), ())), preferred_element_type=F32)


def mm_tn(a, b):
    return lax.dot_general(a, b, (((0,), (0,)), ((), ())), preferred_element_type=F32)


def standardized(values):
    center = values - jnp.mean(values, axis=-1, keepdims=True)
    rstd = lax.rsqrt(jnp.mean(center * center, axis=-1, keepdims=True) + 1e-05)
    return center * rstd, rstd


def tiles(block):
    return block.astype(F32).reshape(-1, C)


def head_rows(j, block):
    row = lax.broadcasted_iota(jnp.int32, block.shape, 0) // HD
    return jnp.where(row == j, block, jnp.zeros_like(block))


def head_lanes(j, block):
    lane = lax.broadcasted_iota(jnp.int32, block.shape, 1) // HD
    return jnp.where(lane == j, block, jnp.zeros_like(block))


def store_transposed(ref, block, segments, row0=0):
    for start, stop, lane in segments:
        ref[row0 : row0 + block.shape[1], lane : lane + stop - start] = block[start:stop].T


def store_values(vt, block, segments):
    for start, stop, lane in segments:
        turned = block[start:stop].T
        count = stop - start
        for head in range(HEADS):
            vt[VROWS * head : VROWS * head + HD, lane : lane + count] = turned[
                HD * head : HD * (head + 1)
            ]
            vt[VROWS * head + HD : VROWS * (head + 1), lane : lane + count] = jnp.ones(
                (VROWS - HD, count), BF16
            )


def out_of_range(sums):
    return jnp.where((sums > LOW) & (sums < HIGH), 0.0, 1.0)


def forward_kernel(
    x_ref, gain_ref, bias_ref, wqkv_ref, wout_ref,
    e_ref, mixt_ref, inv_ref, own_ref, row_ref, tm_ref, corner_ref,
    qt, k, vt,
):
    w, g = pl.program_id(0), pl.program_id(1)

    @pl.when(g == 0)
    def _():
        xhat, _ = standardized(tiles(x_ref[...]))
        normed = (xhat * gain_ref[...] + bias_ref[...]).astype(BF16)
        store_transposed(qt, (mm(normed, wqkv_ref[:, 0:C]) * QSCALE).astype(BF16), WHOLE)
        k[...] = mm(normed, wqkv_ref[:, C : 2 * C]).astype(BF16)
        store_values(vt, mm(normed, wqkv_ref[:, 2 * C :]).astype(BF16), WHOLE)

    base = pl.multiple_of(g * 128, 128)
    kg = k[:, pl.ds(base, 128)]
    qtg = qt[pl.ds(base, 128), :]

    def head(j, shifted):
        scores = mm(kg, head_rows(j, qtg))
        if shifted:
            scores = scores - jnp.max(scores, axis=0, keepdims=True)
        e = jnp.exp2(scores).astype(BF16)
        e_ref[0, j] = e
        mixed = mm(vt[pl.ds(pl.multiple_of(g * 4 * VROWS + j * VROWS, 16), VROWS), :], e)
        sums = mixed[HD : HD + 1]
        inv = 1.0 / sums
        inv_ref[0, 0, pl.ds(j, 1), :] = inv
        mixt_ref[0, pl.ds(pl.multiple_of(base + j * HD, HD), HD), :] = (mixed[:HD] * inv).astype(BF16)
        return out_of_range(sums)

    bad = head(0, False)
    for j in range(1, GROUP):
        bad = bad + head(j, False)

    @pl.when(jnp.max(bad) > 0.0)
    def _():
        def step(j, carry):
            head(j, True)
            return carry

        lax.fori_loop(0, GROUP, step, 0)

    @pl.when(g == GROUP - 1)
    def _():
        y = tiles(x_ref[...]) + mm_tn(mixt_ref[0], wout_ref[...])
        y = y.reshape(7, 7, 8, C).astype(BF16)
        low = y.astype(F32)[:, :, 0:4].astype(BF16)
        own_ref[...] = y

        @pl.when(w == 0)
        def _():
            row_ref[...] = y[0:3]
            corner_ref[...] = low[0:3]
            tm_ref[0:4] = low[3:7]

        @pl.when(w == 1)
        def _():
            tm_ref[4:11] = low


def norm_backward(dnormed, xhat, rstd, gain):
    d = dnormed.astype(BF16).astype(F32) * gain
    return rstd * (
        d
        - jnp.mean(d, axis=-1, keepdims=True)
        - xhat * jnp.mean(d * xhat, axis=-1, keepdims=True)
    )


def backward_first_kernel(
    scale,
    x_ref, gain_ref, bias_ref, wqkv_ref, wout_ref, e_ref, mixt_ref, inv_ref,
    own_ref, row_ref, tm_ref, corner_ref,
    grad_ref, gqkv_ref, gout_ref,
    xhat_s, rstd_s, normed_s, cot_s, q, kt, v, dot_s, dopt, dqt, dproj,
):
    w, g = pl.program_id(0), pl.program_id(1)

    @pl.when(g == 0)
    def _():
        xhat, rstd = standardized(tiles(x_ref[...]))
        xhat_s[...] = xhat
        rstd_s[...] = rstd
        normed = (xhat * gain_ref[...] + bias_ref[...]).astype(BF16)
        normed_s[...] = normed
        q[...] = mm(normed, wqkv_ref[:, 0:C]).astype(BF16)
        store_transposed(kt, mm(normed, wqkv_ref[:, C : 2 * C]).astype(BF16), WHOLE)
        v[...] = mm(normed, wqkv_ref[:, 2 * C :]).astype(BF16)

        def put(row, count, low, high):
            whole = jnp.concatenate([low.astype(F32), high.astype(F32)[:, :, 4:8]], axis=2)
            cot_s[56 * row : 56 * (row + count)] = whole.reshape(-1, C)

        @pl.when(w == 0)
        def _():
            put(0, 3, corner_ref[...], row_ref[...])
            put(3, 4, tm_ref[0:4], own_ref[3:7])

        @pl.when(w == 1)
        def _():
            put(0, 7, tm_ref[4:11], own_ref[7:14])

        dot_s[...] = mm_nt(wout_ref[...], cot_s[...].astype(BF16)).astype(BF16)

    base = pl.multiple_of(g * 128, 128)
    vg = v[:, pl.ds(base, 128)]
    qg = q[:, pl.ds(base, 128)]
    ds_all = []
    for j in range(GROUP):
        rows = pl.ds(pl.multiple_of(base + HD * j, HD), HD)
        inv = inv_ref[0, 0, j : j + 1, :]
        do = dot_s[rows, :].astype(F32) * inv
        dsum = jnp.sum(mixt_ref[0, rows, :].astype(F32) * do, axis=0, keepdims=True)
        dopt[HD * j : HD * (j + 1), :] = do.astype(BF16)
        ds_all.append(dsum)
    dopg = dopt[...]
    dopn = dopg.T
    dv = dk = None
    for j in range(GROUP):
        e = e_ref[0, j]
        dp = mm(vg, head_rows(j, dopg)) - ds_all[j]
        ds = (e.astype(F32) * dp).astype(BF16)
        rows = pl.ds(pl.multiple_of(base + HD * j, HD), HD)
        dqt[HD * j : HD * (j + 1), :] = (mm(kt[rows, :], ds) * HD ** (-0.5)).astype(BF16)
        dv_j = mm(e, head_lanes(j, dopn))
        dk_j = mm(ds, head_lanes(j, qg))
        dv = dv_j if dv is None else dv + dv_j
        dk = dk_j if dk is None else dk + dk_j
    dproj[:, pl.ds(base, 128)] = dqt[...].T
    dproj[:, pl.ds(pl.multiple_of(base + C, 128), 128)] = (dk * HD ** (-0.5)).astype(BF16)
    dproj[:, pl.ds(pl.multiple_of(base + 2 * C, 128), 128)] = dv.astype(BF16)

    @pl.when(g == GROUP - 1)
    def _():
        gout = mm(mixt_ref[0], cot_s[...].astype(BF16)) * scale
        gqkv = mm_tn(normed_s[...], dproj[...]) * scale

        @pl.when(w == 0)
        def _():
            gout_ref[...] = gout
            gqkv_ref[...] = gqkv

        @pl.when(w == 1)
        def _():
            gout_ref[...] += gout
            gqkv_ref[...] += gqkv

        dnormed = mm_nt(dproj[...], wqkv_ref[...])
        total = cot_s[...] + norm_backward(dnormed, xhat_s[...], rstd_s[...], gain_ref[...])
        grad_ref[...] = total.reshape(7, 7, 8, C).astype(BF16)


def second_kernel(
    scale,
    y_own, y_row, y_tm, y_corner, c_own, c_row, c_tm, c_corner,
    gain_ref, bias_ref, wqkv_ref, wout_ref,
    own_ref, row_ref, tm_ref, corner_ref, gqkv_ref, gout_ref,
    x_s, rstd_s, normed_s, cot_s, q, qt, k, kt, v, vt, dot_s, mixt, dopt, dqt, dproj, pen, e_s, dk_s, dv_s,
):
    w, g = pl.program_id(0), pl.program_id(1)
    last_frames = lax.axis_index("tm") == lax.axis_size("tm") - 1
    last_rows = (lax.axis_index("rows") == lax.axis_size("rows") - 1) & (w == 1)

    def region_of(token, segment):
        columns = 4 if segment == 0 else 3
        late = jnp.where(last_frames & (token % 8 < 4), 1, 0)
        below = jnp.where(last_rows & (token // 8 // columns >= 4), 2, 0)
        return late + below

    @pl.when(g == 0)
    def _():
        def gather(into, own, row, tm, corner):
            def put(rho, count, low, high):
                whole = jnp.concatenate([low.astype(F32), high.astype(F32)[:, :, 4:8]], axis=2)
                into[32 * rho : 32 * (rho + count)] = whole[:, 3:7].reshape(-1, C)
                into[224 + 24 * rho : 224 + 24 * (rho + count)] = whole[:, 0:3].reshape(-1, C)

            @pl.when(w == 0)
            def _():
                put(0, 7, tm[0:7], own[3:10])

            @pl.when(w == 1)
            def _():
                put(0, 4, tm[7:11], own[10:14])
                put(4, 3, corner[...], row[...])

        gather(x_s, y_own, y_row, y_tm, y_corner)
        gather(cot_s, c_own, c_row, c_tm, c_corner)
        xhat, rstd = standardized(x_s[...])
        x_s[...] = xhat
        rstd_s[...] = rstd
        normed = (xhat * gain_ref[...] + bias_ref[...]).astype(BF16)
        normed_s[...] = normed
        queries = mm(normed, wqkv_ref[:, 0:C])
        q[...] = queries.astype(BF16)
        store_transposed(qt, (queries * QSCALE).astype(BF16), SPLIT)
        keys = mm(normed, wqkv_ref[:, C : 2 * C]).astype(BF16)
        k[...] = keys
        store_transposed(kt, keys, SPLIT)
        values = mm(normed, wqkv_ref[:, 2 * C :]).astype(BF16)
        v[...] = values
        store_values(vt, values, SPLIT)
        for s, (start, stop, lane) in enumerate(SPLIT):
            dot_s[:, lane : lane + stop - start] = mm_nt(
                wout_ref[...], cot_s[start:stop].astype(BF16)
            ).astype(BF16)
            shape = (stop - start, stop - start)
            key = region_of(lax.broadcasted_iota(jnp.int32, shape, 0), s)
            query = region_of(lax.broadcasted_iota(jnp.int32, shape, 1), s)
            pen[start:stop, 0 : stop - start] = jnp.where(key == query, 0.0, MASKED)

    base = pl.multiple_of(g * 128, 128)

    def head(j, s, general):
        start, stop, lane = SPLIT[s]
        count = stop - start
        keys = slice(0, TOK) if general else slice(start, stop)
        lanes = slice(lane, lane + count)
        qtg = qt[pl.ds(base, 128), lanes]
        scores = mm(k[keys, pl.ds(base, 128)], head_rows(j, qtg))
        if general:
            shape = (TOK, count)
            token = lax.broadcasted_iota(jnp.int32, shape, 0)
            key = jnp.where(token < 224, region_of(token, 0), region_of(token - 224, 1) + 4)
            query = region_of(lax.broadcasted_iota(jnp.int32, shape, 1), s) + 4 * s
            same = key == query
            scores = jnp.where(same, scores, MASKED)
            scores = scores - jnp.max(scores, axis=0, keepdims=True)
        else:
            scores = scores + pen[start:stop, 0:count]
        e = jnp.exp2(scores).astype(BF16)
        e_s[0 if general else start : TOK if general else stop, 0:count] = e
        vrows = pl.ds(pl.multiple_of(g * 4 * VROWS + j * VROWS, 16), VROWS)
        if general:
            mixed = mm(vt[vrows, 0:224], e[0:224]) + mm(vt[vrows, 256:424], e[224:392])
        else:
            mixed = mm(vt[vrows, lanes], e)
        sums = mixed[HD : HD + 1]
        inv = 1.0 / sums
        mixed = mixed[:HD] * inv
        rows = pl.ds(pl.multiple_of(base + j * HD, HD), HD)
        mixt[rows, lanes] = mixed.astype(BF16)
        do = dot_s[rows, lanes].astype(F32) * inv
        dsum = jnp.sum(mixed * do, axis=0, keepdims=True)
        do = do.astype(BF16)
        jrow = j * HD if isinstance(j, int) else pl.multiple_of(j * HD, HD)
        dopt[...] = jnp.zeros_like(dopt)
        dopt[pl.ds(jrow, HD), lanes] = do
        dop = dopt[:, lanes]
        dp = mm(v[keys, pl.ds(base, 128)], dop) - dsum
        ds = e.astype(F32) * dp
        if general:
            ds = jnp.where(same, ds, 0.0)
        ds = ds.astype(BF16)
        if general:
            dq = mm(kt[rows, 0:224], ds[0:224]) + mm(kt[rows, 256:424], ds[224:392])
        else:
            dq = mm(kt[rows, lanes], ds)
        dqt[pl.ds(jrow, HD), lanes] = (dq * HD ** (-0.5)).astype(BF16)
        dv_s[keys] += mm(e, dop.T)
        dk_s[keys] += mm(ds, head_lanes(j, q[start:stop, pl.ds(base, 128)]))
        return out_of_range(sums)

    dv_s[...] = jnp.zeros_like(dv_s)
    dk_s[...] = jnp.zeros_like(dk_s)
    bad = jnp.zeros((), F32)
    for s in range(2):
        for j in range(GROUP):
            bad = bad + jnp.max(head(j, s, False))

    @pl.when(bad > 0.0)
    def _():
        dv_s[...] = jnp.zeros_like(dv_s)
        dk_s[...] = jnp.zeros_like(dk_s)

        def step(j, carry):
            head(j, 0, True)
            head(j, 1, True)
            return carry

        lax.fori_loop(0, GROUP, step, 0)

    for start, stop, lane in SPLIT:
        dproj[start:stop, pl.ds(base, 128)] = dqt[:, lane : lane + stop - start].T
    dproj[:, pl.ds(pl.multiple_of(base + C, 128), 128)] = (dk_s[...] * HD ** (-0.5)).astype(BF16)
    dproj[:, pl.ds(pl.multiple_of(base + 2 * C, 128), 128)] = dv_s[...].astype(BF16)

    @pl.when(g == GROUP - 1)
    def _():
        gout = None
        for start, stop, lane in SPLIT:
            part = mm(mixt[:, lane : lane + stop - start], cot_s[start:stop].astype(BF16))
            gout = part if gout is None else gout + part
        gout = gout * scale
        gqkv = mm_tn(normed_s[...], dproj[...]) * scale

        @pl.when(w == 0)
        def _():
            gout_ref[...] = gout
            gqkv_ref[...] = gqkv

        @pl.when(w == 1)
        def _():
            gout_ref[...] += gout
            gqkv_ref[...] += gqkv

        dnormed = mm_nt(dproj[...], wqkv_ref[...])
        total = cot_s[...] + norm_backward(dnormed, x_s[...], rstd_s[...], gain_ref[...])
        first = total[0:224].reshape(7, 4, 8, C)
        second = total[224:392].reshape(7, 3, 8, C)
        whole = jnp.concatenate([second, first], axis=1)
        low = whole[:, :, 0:4].astype(BF16)
        whole = whole.astype(BF16)

        @pl.when(w == 0)
        def _():
            own_ref[0:3] = whole[0:3]
            own_ref[3:10] = whole
            tm_ref[0:7] = low

        @pl.when(w == 1)
        def _():
            own_ref[10:14] = whole[0:4]
            tm_ref[7:11] = low[0:4]
            row_ref[...] = whole[4:7]
            corner_ref[...] = low[4:7]


def whole_block(shape):
    zeros = (0,) * len(shape)
    return pl.BlockSpec(shape, lambda w, g: zeros)


def piece_shapes():
    return [(14, 7, 8, C), (3, 7, 8, C), (11, 7, 4, C), (3, 7, 4, C)]


WINDOW = pl.BlockSpec((7, 7, 8, C), lambda w, g: (w, 0, 0, 0))
WEIGHTS = [(1, C), (1, C), (C, 3 * C), (C, C)]
SAVED = [
    pl.BlockSpec((1, GROUP, TOK, TOK), lambda w, g: (w, g, 0, 0)),
    pl.BlockSpec((1, C, TOK), lambda w, g: (w, 0, 0)),
    pl.BlockSpec((1, 1, GROUP, TOK), lambda w, g: (w, g, 0, 0)),
]
SAVED_SHAPES = [
    jax.ShapeDtypeStruct((2, HEADS, TOK, TOK), BF16),
    jax.ShapeDtypeStruct((2, C, TOK), BF16),
    jax.ShapeDtypeStruct((2, HEADS // GROUP, GROUP, TOK), F32),
]


def params():
    return pltpu.CompilerParams(
        dimension_semantics=("arbitrary", "arbitrary"), vmem_limit_bytes=VMEM_LIMIT
    )


def forward_first(x, weights):
    pieces = piece_shapes()
    return pl.pallas_call(
        forward_kernel,
        grid=(2, GROUP),
        in_specs=[WINDOW] + [whole_block(s) for s in WEIGHTS],
        out_specs=SAVED + [WINDOW] + [whole_block(s) for s in pieces[1:]],
        out_shape=SAVED_SHAPES + [jax.ShapeDtypeStruct(s, BF16) for s in pieces],
        scratch_shapes=[
            pltpu.VMEM((C, TOK), BF16),
            pltpu.VMEM((TOK, C), BF16),
            pltpu.VMEM((HEADS * VROWS, TOK), BF16),
        ],
        compiler_params=params(),
        name="forward_first",
    )(x, *weights)


def backward_first(scale, x, weights, saved, pieces):
    return pl.pallas_call(
        functools.partial(backward_first_kernel, scale),
        grid=(2, GROUP),
        in_specs=[WINDOW]
        + [whole_block(s) for s in WEIGHTS]
        + SAVED
        + [whole_block(s) for s in piece_shapes()],
        out_specs=[WINDOW, whole_block((C, 3 * C)), whole_block((C, C))],
        out_shape=[
            jax.ShapeDtypeStruct((14, 7, 8, C), BF16),
            jax.ShapeDtypeStruct((C, 3 * C), F32),
            jax.ShapeDtypeStruct((C, C), F32),
        ],
        scratch_shapes=[
            pltpu.VMEM((TOK, C), F32),
            pltpu.VMEM((TOK, 1), F32),
            pltpu.VMEM((TOK, C), BF16),
            pltpu.VMEM((TOK, C), F32),
            pltpu.VMEM((TOK, C), BF16),
            pltpu.VMEM((C, TOK), BF16),
            pltpu.VMEM((TOK, C), BF16),
            pltpu.VMEM((C, TOK), BF16),
            pltpu.VMEM((128, TOK), BF16),
            pltpu.VMEM((128, TOK), BF16),
            pltpu.VMEM((TOK, 3 * C), BF16),
        ],
        compiler_params=params(),
        name="backward_first",
    )(x, *weights, *saved, *pieces)


def second_block(scale, y_pieces, c_pieces, weights):
    pieces = piece_shapes()
    return pl.pallas_call(
        functools.partial(second_kernel, scale),
        grid=(2, GROUP),
        in_specs=[whole_block(s) for s in pieces + pieces + WEIGHTS],
        out_specs=[whole_block(s) for s in pieces + [(C, 3 * C), (C, C)]],
        out_shape=[jax.ShapeDtypeStruct(s, BF16) for s in pieces]
        + [jax.ShapeDtypeStruct((C, 3 * C), F32), jax.ShapeDtypeStruct((C, C), F32)],
        scratch_shapes=[
            pltpu.VMEM((TOK, C), F32),
            pltpu.VMEM((TOK, 1), F32),
            pltpu.VMEM((TOK, C), BF16),
            pltpu.VMEM((TOK, C), F32),
            pltpu.VMEM((TOK, C), BF16),
            pltpu.VMEM((C, 512), BF16),
            pltpu.VMEM((TOK, C), BF16),
            pltpu.VMEM((C, 512), BF16),
            pltpu.VMEM((TOK, C), BF16),
            pltpu.VMEM((HEADS * VROWS, 512), BF16),
            pltpu.VMEM((C, 512), BF16),
            pltpu.VMEM((C, 512), BF16),
            pltpu.VMEM((128, 512), BF16),
            pltpu.VMEM((128, 512), BF16),
            pltpu.VMEM((TOK, 3 * C), BF16),
            pltpu.VMEM((TOK, 256), F32),
            pltpu.VMEM((TOK, 256), BF16),
            pltpu.VMEM((TOK, 128), F32),
            pltpu.VMEM((TOK, 128), F32),
        ],
        compiler_params=params(),
        name="second_block",
    )(*y_pieces, *c_pieces, *weights)


def moved(block, axes, steps):
    sizes = [lax.axis_size(a) for a in axes]
    total = math.prod(sizes)

    def place(index):
        out = []
        for size in reversed(sizes):
            out.append(index % size)
            index //= size
        return out[::-1]

    def number(places):
        index = 0
        for p, size in zip(places, sizes):
            index = index * size + p % size
        return index

    route = [
        (number([p + s for p, s in zip(place(i), steps)]), i) for i in range(total)
    ]
    return lax.ppermute(block, axes if len(axes) > 1 else axes[0], route)


def exchanged(row, tm, corner, step):
    return (
        moved(row, ("rows",), (step,)),
        moved(tm, ("tm",), (step,)),
        moved(corner, ("tm", "rows"), (step, step)),
    )


def per_device(
    video_clip, cotangent,
    gain_first, bias_first, qkv_first, out_first,
    gain_second, bias_second, qkv_second, out_second,
):
    frames, rows_here, columns, channels = video_clip.shape
    devices = lax.axis_size("tm") * lax.axis_size("rows")
    scale = 1.0 / math.sqrt(frames * rows_here * columns * devices)
    x = video_clip.transpose(1, 2, 0, 3)
    cot = cotangent.transpose(1, 2, 0, 3)
    first = (gain_first.reshape(1, C), bias_first.reshape(1, C), qkv_first, out_first)
    second = (gain_second.reshape(1, C), bias_second.reshape(1, C), qkv_second, out_second)
    c_pieces = (cot,) + exchanged(cot[0:3], cot[3:14, :, 0:4], cot[0:3, :, 0:4], 1)
    *saved, own, row, tm, corner = forward_first(x, first)
    y_pieces = (own,) + exchanged(row, tm, corner, 1)
    own, row, tm, corner, gqkv2, gout2 = second_block(scale, y_pieces, c_pieces, second)
    d_pieces = (own,) + exchanged(row, tm, corner, -1)
    grad, gqkv1, gout1 = backward_first(scale, x, first, saved, d_pieces)

    def scattered(block):
        return lax.psum_scatter(block, ("tm", "rows"), scatter_dimension=0, tiled=True)

    return (
        grad.transpose(2, 0, 1, 3),
        scattered(gqkv1), scattered(gout1), scattered(gqkv2), scattered(gout2),
    )


def solution(mesh):
    clip = P("tm", "rows", None, None)
    scattered = P(("tm", "rows"), None)
    return jax.shard_map(
        per_device,
        mesh=mesh,
        in_specs=(clip, clip) + (P(),) * 8,
        out_specs=(clip,) + (scattered,) * 4,
        check_vma=False,
    )
```

time: 524 us -> 328 us (0.63); the launches traced: 514 us -> 327 us
  matrix products: 172 us -> 0 us
  Pallas kernels: 0 us -> 98.4 us
  other arithmetic: 82.8 us -> 0 us
  local copies, waits for them, and re-layouts: 85.2 us -> 7.52 us
  waiting for transfers between devices: 147 us -> 188 us
  starting transfers between devices: 11 us -> 18.4 us
    dot_general x21 -> x0, matrix products: 143 us -> none  [the longest x4 66.9 us: attend(): jnp.einsum('nqhd,nkhd->nhqk', query_rows, key_rows) * head_size ** (-0.5)]
    pallas_call x0 -> x3, Pallas kernels: none -> 98.4 us  [the longest x1 48.2 us: second_block(): pl.pallas_call(functools.partial(second_kernel, scale), grid=(2, GROUP),...]
    convert_element_type x8 -> x0, other arithmetic: 44.7 us -> none  [the longest x2 32.4 us: attend(): jax.nn.softmax(scores, axis=-1).astype(jnp.bfloat16)]
    convert_element_type x15 -> x0, local copies, waits for them, and re-layouts: 32.4 us -> none  [the longest x6 17.6 us: forward_block(): input_float = windows_in.astype(jnp.float32)]
    unnamed x2, waiting for transfers between devices: 130 us -> 159 us
    sub x2 -> x0, matrix products: 29.4 us -> none  [attend(): jax.nn.softmax(scores, axis=-1).astype(jnp.bfloat16)]
    reduce_sum x9 -> x0, other arithmetic: 28.2 us -> none  [the longest x1 14.2 us: attend(): jax.nn.softmax(scores, axis=-1).astype(jnp.bfloat16)]
    optimization_barrier x4 -> x0, local copies, waits for them, and re-layouts: 18.5 us -> none  [attend(): packed = lax.optimization_barrier(projected.astype(jnp.bfloat16))]
  transfers between devices with their start and end apart: 7 -> 10, of which waited for: 3 -> 5; matrix products, arithmetic and copies ran while one was open for 17% -> 1% of each run, Pallas kernels for 0% -> 0%
where the time goes in v1:
time: 328 us; the launch traced here: 327 us
  waiting for transfers between devices  188 us (57%)
  Pallas kernels  98.4 us (30%)
  starting transfers between devices  18.4 us (6%)
  between operations  14.1 us (4%)
  local copies, waits for them, and re-layouts  7.52 us (2%)
    unnamed x2, waiting for transfers between devices  159 us
    pallas_call x1, Pallas kernels, second_block(): pl.pallas_call(functools.partial(second_kernel, scale), grid=(2, GROUP),...  48.2 us
    pallas_call x1, Pallas kernels, backward_first(): pl.pallas_call(functools.partial(backward_first_kernel, scale), grid=(2,...  32.1 us
    ppermute x9, waiting for transfers between devices, moved(): return lax.ppermute(block, axes if len(axes) > 1 else axes[0], route)  29.1 us
    ppermute x9, starting transfers between devices, moved(): return lax.ppermute(block, axes if len(axes) > 1 else axes[0], route)  18.3 us
    pallas_call x1, Pallas kernels, forward_first(): pl.pallas_call(forward_kernel, grid=(2, GROUP), in_specs=[WINDOW] + [whol...  18 us
  transfers between devices with their start and end apart: 10, of which 5 were waited for; matrix products, arithmetic and copies ran while one was open for 1% of the time, Pallas kernels for 0%

profile of v1, /device:TPU:0, one launch (start us, length us, event | category | flops | bytes accessed | tf_op | source)
XLA Modules:
  0.0 326.9 jit_solution(14945016884844567960)
XLA Ops:
  7.2 18.0 %forward_first.1 = (bf16[2,16,392,392]{3,2,1,0:T(8,128)(2,1)}, bf16[2,512,392]{2,1,0:T(8,128)(2,1)}, f32[2,4,4,392]{3,2,1,0:T(4,128)}, bf16[14,7,8,512]{3,2,1,0:...) custom-call(bf16[14,7,8,512]{3,2,1,0:T(8,128)(2,1)} %bitcast.7, ...), custom_call_target="tpu_custom_call" | custom-call | tf_op jit(solution)/shard_map/forward_first/pallas_call | solution.py:440
  25.3 9.1 %collective-permute-start.1 = (bf16[11,7,4,512]{3,2,1,0:T(4,128)(2,1)}, bf16[11,7,4,512]{3,2,1,0:T(4,128)(2,1)S(1)}, u32[]{:S(2)}, u32[]{:S(2)}) collective-permute-start(bf16[11,7,4,512]{3,2,1,0:T(4,128)(2,1)} %get-tuple-element.26), channel_id=1, source_target_pairs={{4,0},{8,4},{12,8},{16,12},{20,16},{24,20},{28,24},{32,28},{36,32}... | collective-permute-start | bytes 946184 | tf_op jit(solution)/shard_map/ppermute | solution.py:543
  34.4 1.2 slice.13
  35.5 0.8 collective-permute-start.4
  36.3 0.8 collective-permute-start
  37.1 0.9 slice.12
  38.1 0.9 slice.14
  39.1 11.0 %collective-permute-done.2.y_corner = bf16[3,7,4,512]{3,2,1,0:T(4,128)(2,1)S(1)} collective-permute-done((bf16[3,7,4,512]{3,2,1,0:T(4,128)(2,1)}, bf16[3,7,4,512]{3,2,1,0:T(4,128)(2,1)S(1)}, u32[]{:S(2)}, u32[]{:S(2)}) %collective-permute-start.2) | collective-permute-done | bytes 86048 | tf_op jit(solution)/shard_map/ppermute | solution.py:543
  50.0 7.2 %collective-permute-start.5 = (bf16[3,7,4,512]{3,2,1,0:T(4,128)(2,1)S(1)}, bf16[3,7,4,512]{3,2,1,0:T(4,128)(2,1)S(1)}, u32[]{:S(2)}, u32[]{:S(2)}) collective-permute-start(bf16[3,7,4,512]{3,2,1,0:T(4,128)(2,1)S(1)} %slice.14), channel_id=1, source_target_pairs={{5,0},{6,1},{7,2},{4,3},{9,4},{10,5},{11,6},{8,7},{13,8},{14,9},{1... | collective-permute-start | bytes 258056 | tf_op jit(solution)/shard_map/ppermute | solution.py:543
  57.2 2.2 collective-permute-done.5.c_corner
  59.5 0.6 copy-done.8
  60.1 0.1 copy-done.3
  60.2 0.1 copy-done
  60.3 0.1 copy-done.1
  60.4 48.2 %second_block.1 = (bf16[14,7,8,512]{3,2,1,0:T(8,128)(2,1)}, bf16[3,7,8,512]{3,2,1,0:T(8,128)(2,1)}, bf16[11,7,4,512]{3,2,1,0:T(4,128)(2,1)}, bf16[3,7,4,512]{3,2...) custom-call(bf16[14,7,8,512]{3,2,1,0:T(8,128)(2,1)} %get-tuple-element.24.y_own, ...), custom_call_target="tpu_custom_call" | custom-call | tf_op jit(solution)/shard_map/second_block/pallas_call | solution.py:490
  108.8 0.3 collective-permute-start.8
  109.1 15.8 %collective-permute-done.8.corner_ref = bf16[3,7,4,512]{3,2,1,0:T(4,128)(2,1)S(1)} collective-permute-done((bf16[3,7,4,512]{3,2,1,0:T(4,128)(2,1)}, bf16[3,7,4,512]{3,2,1,0:T(4,128)(2,1)S(1)}, u32[]{:S(2)}, u32[]{:S(2)}) %collective-permute-start.8) | collective-permute-done | bytes 86048 | tf_op jit(solution)/shard_map/ppermute | solution.py:543
  124.9 0.1 collective-permute-done.7.tm_ref
  125.0 0.5 copy-done.6
  125.6 0.2 copy-done.2
  125.7 32.1 %backward_first.1 = (bf16[14,7,8,512]{3,2,1,0:T(8,128)(2,1)}, f32[512,1536]{1,0:T(8,128)}, f32[512,512]{1,0:T(8,128)}) custom-call(bf16[14,7,8,512]{3,2,1,0:T(8,128)(2,1)} %bitcast.8, f32[1,512]{1,0:T(1,128)} %bitcast.14, f32[1,512]{1,0:T(1,128)} %bitcast.16, bf16[512,1536]{1,0:T(8,128)(2,1)} %wqkv_ref.5, bf16[512,512]{1,0:T(8,128)(2,1)} %wout_ref.5, ...), custom_call_target="tpu_custom_call" | custom-call | tf_op jit(solution)/shard_map/backward_first/pallas_call | solution.py:457
  157.9 159.4 %all-reduce.7.cloned.1.call-done = (f32[512,1536]{1,0:T(8,128)}, f32[512,512]{1,0:T(8,128)}, f32[512,1536]{1,0:T(8,128)}, f32[512,512]{1,0:T(8,128)}) async-done(((f32[512,1536]{1,0:T(8,128)}, f32[512,512]{1,0:T(8,128)}, f32[512,1536]{1,0:T(8,128)}, f32[512,512]{1,0:T(8,128)}), (f32[512,1536]{1,0:T(8,128)}, f32[512,512]{1,0:T(8,128)}, f32[512,1536]{1,0:T(8,128)}, ...) | async-done | bytes 8388624
  317.2 1.3 constant_dynamic-slice_fusion
  318.6 1.4 constant_dynamic-slice_fusion.1
  (23 shorter events, 0.4 us)
Async XLA Ops:
  7.2 310.1 %all-reduce.7.cloned.1.call-start = ((), (), s32[]{:S(2)}) async-start(), calls=%async_computation | async-start | bytes 16777216
  25.3 34.2 %collective-permute-start.1 = (bf16[11,7,4,512]{3,2,1,0:T(4,128)(2,1)}, bf16[11,7,4,512]{3,2,1,0:T(4,128)(2,1)S(1)}, u32[]{:S(2)}, u32[]{:S(2)}) collective-permute-start(bf16[11,7,4,512]{3,2,1,0:T(4,128)(2,1)} %get-tuple-element.26), channel_id=1, source_target_pairs={{4,0},{8,4},{12,8},{16,12},{20,16},{24,20},{28,24},{32,28},{36,32}... | collective-permute-start | bytes 946184 | tf_op jit(solution)/shard_map/ppermute | solution.py:543
  35.5 24.0 %collective-permute-start.4 = (bf16[11,7,4,512]{3,2,1,0:T(4,128)(2,1)S(1)}, bf16[11,7,4,512]{3,2,1,0:T(4,128)(2,1)S(1)}, u32[]{:S(2)}, u32[]{:S(2)}) collective-permute-start(bf16[11,7,4,512]{3,2,1,0:T(4,128)(2,1)S(1)} %slice.13), channel_id=1, source_target_pairs={{4,0},{8,4},{12,8},{16,12},{20,16},{24,20},{28,24},{32,28},{36,32}... | collective-permute-start | bytes 946184 | tf_op jit(solution)/shard_map/ppermute | solution.py:543
  36.3 13.7 %collective-permute-start.2 = (bf16[3,7,4,512]{3,2,1,0:T(4,128)(2,1)}, bf16[3,7,4,512]{3,2,1,0:T(4,128)(2,1)S(1)}, u32[]{:S(2)}, u32[]{:S(2)}) collective-permute-start(bf16[3,7,4,512]{3,2,1,0:T(4,128)(2,1)} %get-tuple-element.27), channel_id=1, source_target_pairs={{5,0},{6,1},{7,2},{4,3},{9,4},{10,5},{11,6},{8,7},{13,8},{14,9},{1... | collective-permute-start | bytes 258056 | tf_op jit(solution)/shard_map/ppermute | solution.py:543
  36.3 23.1 %collective-permute-start = (bf16[3,7,8,512]{3,2,1,0:T(8,128)(2,1)}, bf16[3,7,8,512]{3,2,1,0:T(8,128)(2,1)S(1)}, u32[]{:S(2)}, u32[]{:S(2)}) collective-permute-start(bf16[3,7,8,512]{3,2,1,0:T(8,128)(2,1)} %get-tuple-element.25), channel_id=1, source_target_pairs={{1,0},{2,1},{3,2},{0,3},{5,4},{6,5},{7,6},{4,7},{9,8},{10,9},{11,1... | collective-permute-start | bytes 516104 | tf_op jit(solution)/shard_map/ppermute | solution.py:543
  38.0 21.4 %collective-permute-start.3 = (bf16[3,7,8,512]{3,2,1,0:T(8,128)(2,1)S(1)}, bf16[3,7,8,512]{3,2,1,0:T(8,128)(2,1)S(1)}, u32[]{:S(2)}, u32[]{:S(2)}) collective-permute-start(bf16[3,7,8,512]{3,2,1,0:T(8,128)(2,1)S(1)} %slice.12), channel_id=1, source_target_pairs={{1,0},{2,1},{3,2},{0,3},{5,4},{6,5},{7,6},{4,7},{9,8},{10,9},{11,1... | collective-permute-start | bytes 516104 | tf_op jit(solution)/shard_map/ppermute | solution.py:543
  50.0 9.5 %copy-start.7 = (bf16[3,7,4,512]{3,2,1,0:T(4,128)(2,1)}, bf16[3,7,4,512]{3,2,1,0:T(4,128)(2,1)S(1)}, u32[]{:S(2)}) copy-start(bf16[3,7,4,512]{3,2,1,0:T(4,128)(2,1)S(1)} %collective-permute-done.2.y_corner) | copy-start | bytes 258052
  50.0 9.4 %collective-permute-start.5 = (bf16[3,7,4,512]{3,2,1,0:T(4,128)(2,1)S(1)}, bf16[3,7,4,512]{3,2,1,0:T(4,128)(2,1)S(1)}, u32[]{:S(2)}, u32[]{:S(2)}) collective-permute-start(bf16[3,7,4,512]{3,2,1,0:T(4,128)(2,1)S(1)} %slice.14), channel_id=1, source_target_pairs={{5,0},{6,1},{7,2},{4,3},{9,4},{10,5},{11,6},{8,7},{13,8},{14,9},{1... | collective-permute-start | bytes 258056 | tf_op jit(solution)/shard_map/ppermute | solution.py:543
  59.4 0.6 copy-start.8
  59.4 0.7 copy-start.3
  59.4 0.8 copy-start.4
  59.5 0.8 copy-start
  59.5 0.9 copy-start.1
  108.7 16.3 %collective-permute-start.7 = (bf16[11,7,4,512]{3,2,1,0:T(4,128)(2,1)}, bf16[11,7,4,512]{3,2,1,0:T(4,128)(2,1)S(1)}, u32[]{:S(2)}, u32[]{:S(2)}) collective-permute-start(bf16[11,7,4,512]{3,2,1,0:T(4,128)(2,1)} %get-tuple-element.30), channel_id=1, source_target_pairs={{124,0},{0,4},{4,8},{8,12},{12,16},{16,20},{20,24},{24,28},{28,32}... | collective-permute-start | bytes 946184 | tf_op jit(solution)/shard_map/ppermute | solution.py:543
  108.7 16.2 %collective-permute-start.6 = (bf16[3,7,8,512]{3,2,1,0:T(8,128)(2,1)}, bf16[3,7,8,512]{3,2,1,0:T(8,128)(2,1)S(1)}, u32[]{:S(2)}, u32[]{:S(2)}) collective-permute-start(bf16[3,7,8,512]{3,2,1,0:T(8,128)(2,1)} %get-tuple-element.29), channel_id=1, source_target_pairs={{3,0},{0,1},{1,2},{2,3},{7,4},{4,5},{5,6},{6,7},{11,8},{8,9},{9,10... | collective-permute-start | bytes 516104 | tf_op jit(solution)/shard_map/ppermute | solution.py:543
  108.8 16.1 %collective-permute-start.8 = (bf16[3,7,4,512]{3,2,1,0:T(4,128)(2,1)}, bf16[3,7,4,512]{3,2,1,0:T(4,128)(2,1)S(1)}, u32[]{:S(2)}, u32[]{:S(2)}) collective-permute-start(bf16[3,7,4,512]{3,2,1,0:T(4,128)(2,1)} %get-tuple-element.31), channel_id=1, source_target_pairs={{127,0},{124,1},{125,2},{126,3},{3,4},{0,5},{1,6},{2,7},{7,8},{4,9... | collective-permute-start | bytes 258056 | tf_op jit(solution)/shard_map/ppermute | solution.py:543
  124.9 0.6 copy-start.6
  124.9 0.7 copy-start.5
  125.0 0.8 copy-start.2
Sparse Core Ops, SparseCore 0:
  158.0 159.1 all-reduce.6

commit v2 on v1

--- a/solution.py
+++ b/solution.py
@@ -138,6 +138,24 @@
             tm_ref[4:11] = low
 
 
+def write_parts(gqkv, gout, parts):
+    def layer(z, carry):
+        for xy in range(16):
+            x, y = xy // 4, xy % 4
+            rows = pl.ds(pl.multiple_of((z * 16 + x // 2 * 8 + y * 2 + x % 2) * 8, 8), 8)
+            blocks = (
+                gqkv[rows, 0:640],
+                gqkv[rows, 640:1280],
+                jnp.concatenate([gqkv[rows, 1280:1536], gout[rows, :]], axis=1),
+            )
+            for part, block, place in zip(parts, blocks, ((x, y, z), (y, z, x), (z, x, y))):
+                part[(0,) + place] = block[0:4].astype(BF16)
+                part[(1,) + place] = block[4:8].astype(BF16)
+        return carry
+
+    lax.fori_loop(0, 4, layer, 0)
+
+
 def norm_backward(dnormed, xhat, rstd, gain):
     d = dnormed.astype(BF16).astype(F32) * gain
     return rstd * (
@@ -151,9 +169,10 @@
     scale,
     x_ref, gain_ref, bias_ref, wqkv_ref, wout_ref, e_ref, mixt_ref, inv_ref,
     own_ref, row_ref, tm_ref, corner_ref,
-    grad_ref, gqkv_ref, gout_ref,
-    xhat_s, rstd_s, normed_s, cot_s, q, kt, v, dot_s, dopt, dqt, dproj,
+    grad_ref, part0_ref, part1_ref, part2_ref,
+    xhat_s, rstd_s, normed_s, cot_s, q, kt, v, dot_s, dopt, dqt, dproj, gqkv_s, gout_s,
 ):
+    part_refs = (part0_ref, part1_ref, part2_ref)
     w, g = pl.program_id(0), pl.program_id(1)
 
     @pl.when(g == 0)
@@ -217,13 +236,14 @@
 
         @pl.when(w == 0)
         def _():
-            gout_ref[...] = gout
-            gqkv_ref[...] = gqkv
+            gout_s[...] = gout
+            gqkv_s[...] = gqkv
 
         @pl.when(w == 1)
         def _():
-            gout_ref[...] += gout
-            gqkv_ref[...] += gqkv
+            gout_s[...] += gout
+            gqkv_s[...] += gqkv
+            write_parts(gqkv_s, gout_s, part_refs)
 
         dnormed = mm_nt(dproj[...], wqkv_ref[...])
         total = cot_s[...] + norm_backward(dnormed, xhat_s[...], rstd_s[...], gain_ref[...])
@@ -234,9 +254,11 @@
     scale,
     y_own, y_row, y_tm, y_corner, c_own, c_row, c_tm, c_corner,
     gain_ref, bias_ref, wqkv_ref, wout_ref,
-    own_ref, row_ref, tm_ref, corner_ref, gqkv_ref, gout_ref,
+    own_ref, row_ref, tm_ref, corner_ref, part0_ref, part1_ref, part2_ref,
     x_s, rstd_s, normed_s, cot_s, q, qt, k, kt, v, vt, dot_s, mixt, dopt, dqt, dproj, pen, e_s, dk_s, dv_s,
+    gqkv_s, gout_s,
 ):
+    part_refs = (part0_ref, part1_ref, part2_ref)
     w, g = pl.program_id(0), pl.program_id(1)
     last_frames = lax.axis_index("tm") == lax.axis_size("tm") - 1
     last_rows = (lax.axis_index("rows") == lax.axis_size("rows") - 1) & (w == 1)
@@ -376,13 +398,14 @@
 
         @pl.when(w == 0)
         def _():
-            gout_ref[...] = gout
-            gqkv_ref[...] = gqkv
+            gout_s[...] = gout
+            gqkv_s[...] = gqkv
 
         @pl.when(w == 1)
         def _():
-            gout_ref[...] += gout
-            gqkv_ref[...] += gqkv
+            gout_s[...] += gout
+            gqkv_s[...] += gqkv
+            write_parts(gqkv_s, gout_s, part_refs)
 
         dnormed = mm_nt(dproj[...], wqkv_ref[...])
         total = cot_s[...] + norm_backward(dnormed, x_s[...], rstd_s[...], gain_ref[...])
@@ -415,6 +438,8 @@
     return [(14, 7, 8, C), (3, 7, 8, C), (11, 7, 4, C), (3, 7, 4, C)]
 
 
+WIDTHS = (640, 640, 768)
+PARTS = [(2, 4, 4, 4, 4, width) for width in WIDTHS]
 WINDOW = pl.BlockSpec((7, 7, 8, C), lambda w, g: (w, 0, 0, 0))
 WEIGHTS = [(1, C), (1, C), (C, 3 * C), (C, C)]
 SAVED = [
@@ -461,12 +486,8 @@
         + [whole_block(s) for s in WEIGHTS]
         + SAVED
         + [whole_block(s) for s in piece_shapes()],
-        out_specs=[WINDOW, whole_block((C, 3 * C)), whole_block((C, C))],
-        out_shape=[
-            jax.ShapeDtypeStruct((14, 7, 8, C), BF16),
-            jax.ShapeDtypeStruct((C, 3 * C), F32),
-            jax.ShapeDtypeStruct((C, C), F32),
-        ],
+        out_specs=[WINDOW] + [whole_block(s) for s in PARTS],
+        out_shape=[jax.ShapeDtypeStruct(s, BF16) for s in [(14, 7, 8, C)] + PARTS],
         scratch_shapes=[
             pltpu.VMEM((TOK, C), F32),
             pltpu.VMEM((TOK, 1), F32),
@@ -479,6 +500,8 @@
             pltpu.VMEM((128, TOK), BF16),
             pltpu.VMEM((128, TOK), BF16),
             pltpu.VMEM((TOK, 3 * C), BF16),
+            pltpu.VMEM((C, 3 * C), F32),
+            pltpu.VMEM((C, C), F32),
         ],
         compiler_params=params(),
         name="backward_first",
@@ -491,9 +514,8 @@
         functools.partial(second_kernel, scale),
         grid=(2, GROUP),
         in_specs=[whole_block(s) for s in pieces + pieces + WEIGHTS],
-        out_specs=[whole_block(s) for s in pieces + [(C, 3 * C), (C, C)]],
-        out_shape=[jax.ShapeDtypeStruct(s, BF16) for s in pieces]
-        + [jax.ShapeDtypeStruct((C, 3 * C), F32), jax.ShapeDtypeStruct((C, C), F32)],
+        out_specs=[whole_block(s) for s in pieces + PARTS],
+        out_shape=[jax.ShapeDtypeStruct(s, BF16) for s in pieces + PARTS],
         scratch_shapes=[
             pltpu.VMEM((TOK, C), F32),
             pltpu.VMEM((TOK, 1), F32),
@@ -514,10 +536,142 @@
             pltpu.VMEM((TOK, 256), BF16),
             pltpu.VMEM((TOK, 128), F32),
             pltpu.VMEM((TOK, 128), F32),
+            pltpu.VMEM((C, 3 * C), F32),
+            pltpu.VMEM((C, C), F32),
         ],
         compiler_params=params(),
         name="second_block",
     )(*y_pieces, *c_pieces, *weights)
+
+
+def coordinates():
+    tm, rows = lax.axis_index("tm"), lax.axis_index("rows")
+    return {
+        "x": tm // 4 % 2 * 2 + rows // 2,
+        "y": tm % 4,
+        "z": tm // 8,
+        "core": rows % 2,
+    }
+
+
+def device_at(place):
+    tm = place["z"] * 8 + place["x"] // 2 * 4 + place["y"]
+    return (tm, place["x"] % 2 * 2 + place["core"])
+
+
+def beside(here, axis, steps):
+    return device_at({**here, axis: (here[axis] + steps) % (2 if axis == "core" else 4)})
+
+
+ORDERS = ("xyz", "yzx", "zxy")
+MESH = pl.DeviceIdType.MESH
+
+
+def reduce_kernel(jobs, *refs):
+    parts, outs = refs[:jobs], refs[jobs : 2 * jobs]
+    scratch = refs[2 * jobs : 7 * jobs]
+    held = [scratch[5 * i : 5 * i + 2] for i in range(jobs)]
+    slots = [scratch[5 * i + 2 : 5 * i + 5] for i in range(jobs)]
+    send_sem, recv_sem, local_sem = refs[7 * jobs :]
+    here = coordinates()
+    partners = [beside(here, "core", 1)] + [
+        beside(here, axis, steps) for axis in "xyz" for steps in (1, 2, 3)
+    ]
+    barrier = pltpu.get_barrier_semaphore()
+    for partner in partners:
+        pl.semaphore_signal(barrier, inc=1, device_id=partner, device_id_type=MESH)
+
+    local = []
+    for i in range(jobs):
+        copy = pltpu.make_async_copy(parts[i].at[here["core"]], held[i][0], local_sem.at[i])
+        copy.start()
+        local.append(copy)
+    pl.semaphore_wait(barrier, len(partners))
+
+    flying = []
+    for i in range(jobs):
+        copy = pltpu.make_async_remote_copy(
+            src_ref=parts[i].at[1 - here["core"]],
+            dst_ref=held[i][1],
+            send_sem=send_sem.at[i, 0],
+            recv_sem=recv_sem.at[i, 0],
+            device_id=partners[0],
+            device_id_type=MESH,
+        )
+        copy.start()
+        flying.append([copy])
+
+    sent = list(flying)
+    sums = [None] * jobs
+    for stage in range(4):
+        for i in range(jobs):
+            order = ORDERS[i % 3]
+            for copy in flying[i]:
+                copy.wait_recv()
+            if stage == 0:
+                local[i].wait()
+                for a in range(4):
+                    total = held[i][0][a].astype(F32) + held[i][1][a].astype(F32)
+                    held[i][0][a] = total.astype(BF16)
+                source = held[i][0]
+            else:
+                total = sums[i]
+                for slot in range(3):
+                    total = total + slots[i][stage - 1][slot].astype(F32)
+                if stage == 3:
+                    outs[i][...] = total
+                    continue
+                source = slots[i][stage - 1].at[3]
+                source[...] = total.astype(BF16)
+            axis = order[stage]
+            copies = []
+            for steps in (1, 2, 3):
+                copy = pltpu.make_async_remote_copy(
+                    src_ref=source.at[(here[axis] + steps) % 4],
+                    dst_ref=slots[i][stage].at[steps - 1],
+                    send_sem=send_sem.at[i, 3 * stage + steps],
+                    recv_sem=recv_sem.at[i, 3 * stage + steps],
+                    device_id=beside(here, axis, steps),
+                    device_id_type=MESH,
+                )
+                copy.start()
+                copies.append(copy)
+            sums[i] = source[here[axis]].astype(F32)
+            flying[i] = copies
+            sent.append(copies)
+    for copies in sent:
+        for copy in copies:
+            copy.wait_send()
+
+
+def reduced(parts):
+    jobs = len(parts)
+    scratch = []
+    for part in parts:
+        width = part.shape[-1]
+        scratch += [
+            pltpu.VMEM((4, 4, 4, 4, width), BF16),
+            pltpu.VMEM((4, 4, 4, 4, width), BF16),
+            pltpu.VMEM((4, 4, 4, 4, width), BF16),
+            pltpu.VMEM((4, 4, 4, width), BF16),
+            pltpu.VMEM((4, 4, width), BF16),
+        ]
+    return pl.pallas_call(
+        functools.partial(reduce_kernel, jobs),
+        in_specs=[pl.BlockSpec(memory_space=pl.ANY)] * jobs,
+        out_specs=[pl.BlockSpec(memory_space=pltpu.VMEM)] * jobs,
+        out_shape=[jax.ShapeDtypeStruct((4, part.shape[-1]), F32) for part in parts],
+        scratch_shapes=scratch
+        + [
+            pltpu.SemaphoreType.DMA((jobs, 10)),
+            pltpu.SemaphoreType.DMA((jobs, 10)),
+            pltpu.SemaphoreType.DMA((jobs,)),
+        ],
+        compiler_params=pltpu.CompilerParams(
+            collective_id=0, has_side_effects=True, vmem_limit_bytes=VMEM_LIMIT
+        ),
+        name="reduce_gradients",
+    )(*parts)
 
 
 def moved(block, axes, steps):
@@ -566,17 +720,16 @@
     c_pieces = (cot,) + exchanged(cot[0:3], cot[3:14, :, 0:4], cot[0:3, :, 0:4], 1)
     *saved, own, row, tm, corner = forward_first(x, first)
     y_pieces = (own,) + exchanged(row, tm, corner, 1)
-    own, row, tm, corner, gqkv2, gout2 = second_block(scale, y_pieces, c_pieces, second)
+    own, row, tm, corner, *parts2 = second_block(scale, y_pieces, c_pieces, second)
     d_pieces = (own,) + exchanged(row, tm, corner, -1)
-    grad, gqkv1, gout1 = backward_first(scale, x, first, saved, d_pieces)
-
-    def scattered(block):
-        return lax.psum_scatter(block, ("tm", "rows"), scatter_dimension=0, tiled=True)
-
-    return (
-        grad.transpose(2, 0, 1, 3),
-        scattered(gqkv1), scattered(gout1), scattered(gqkv2), scattered(gout2),
-    )
+    grad, *parts1 = backward_first(scale, x, first, saved, d_pieces)
+    sums = reduced(parts1 + parts2)
+
+    def matrices(sums):
+        gqkv = jnp.concatenate([sums[0], sums[1], sums[2][:, :256]], axis=1)
+        return gqkv, sums[2][:, 256:]
+
+    return (grad.transpose(2, 0, 1, 3), *matrices(sums[:3]), *matrices(sums[3:]))
 
 
 def solution(mesh):

time: 328 us -> 176 us (0.54)
  waiting for transfers between devices: 188 us -> 25.1 us
  Pallas kernels: 98.4 us -> 122 us
  between operations: 14.1 us -> 0.75 us
    unnamed x2 -> x0, waiting for transfers between devices: 159 us -> none
    pallas_call x0 -> x1, Pallas kernels: none -> 24 us  [reduced(): pl.pallas_call(functools.partial(reduce_kernel, jobs), in_specs=[pl.Block...]
    ppermute x9, waiting for transfers between devices: 29.1 us -> 25.1 us  [moved(): return lax.ppermute(block, axes if len(axes) > 1 else axes[0], route)]
    slice x0 -> x4, local copies, waits for them, and re-layouts: none -> 3.95 us  [the longest x2 2.59 us: matrices(): return (gqkv, sums[2][:, 256:])]
  transfers between devices with their start and end apart: 10 -> 9, of which waited for: 5 -> 4; matrix products, arithmetic and copies ran while one was open for 1% -> 1% of each run, Pallas kernels for 0% -> 10%
where the time goes in v2:
time: 176 us; the launch traced here: 175 us
  Pallas kernels  122 us (69%)
  waiting for transfers between devices  25.1 us (14%)
  starting transfers between devices  17.4 us (10%)
  local copies, waits for them, and re-layouts  8.69 us (5%)
    pallas_call x1, Pallas kernels, second_block(): pl.pallas_call(functools.partial(second_kernel, scale), grid=(2, GROUP),...  47.9 us
    pallas_call x1, Pallas kernels, backward_first(): pl.pallas_call(functools.partial(backward_first_kernel, scale), grid=(2,...  31.8 us
    ppermute x9, waiting for transfers between devices, moved(): return lax.ppermute(block, axes if len(axes) > 1 else axes[0], route)  25.1 us
    pallas_call x1, Pallas kernels, reduced(): pl.pallas_call(functools.partial(reduce_kernel, jobs), in_specs=[pl.Block...  24 us
    pallas_call x1, Pallas kernels, forward_first(): pl.pallas_call(forward_kernel, grid=(2, GROUP), in_specs=[WINDOW] + [whol...  18 us
    ppermute x9, starting transfers between devices, moved(): return lax.ppermute(block, axes if len(axes) > 1 else axes[0], route)  17.4 us
  transfers between devices with their start and end apart: 9, of which 4 were waited for; matrix products, arithmetic and copies ran while one was open for 1% of the time, Pallas kernels for 10%

profile of v2, /device:TPU:0, one launch (start us, length us, event | category | flops | bytes accessed | tf_op | source)
XLA Modules:
  0.0 175.0 jit_solution(13834032620457075700)
XLA Ops:
  0.6 1.2 slice.29
  1.8 9.1 %collective-permute-start.4 = (bf16[11,7,4,512]{3,2,1,0:T(4,128)(2,1)S(1)}, bf16[11,7,4,512]{3,2,1,0:T(4,128)(2,1)S(1)}, u32[]{:S(2)}, u32[]{:S(2)}) collective-permute-start(bf16[11,7,4,512]{3,2,1,0:T(4,128)(2,1)S(1)} %slice.29), channel_id=1, source_target_pairs={{4,0},{8,4},{12,8},{16,12},{20,16},{24,20},{28,24},{32,28},{36,32}... | collective-permute-start | bytes 946184 | tf_op jit(solution)/shard_map/ppermute | solution.py:697
  10.9 18.0 %forward_first.1 = (bf16[2,16,392,392]{3,2,1,0:T(8,128)(2,1)}, bf16[2,512,392]{2,1,0:T(8,128)(2,1)}, f32[2,4,4,392]{3,2,1,0:T(4,128)}, bf16[14,7,8,512]{3,2,1,0:...) custom-call(bf16[14,7,8,512]{3,2,1,0:T(8,128)(2,1)} %bitcast.7, ...), custom_call_target="tpu_custom_call" | custom-call | tf_op jit(solution)/shard_map/forward_first/pallas_call | solution.py:465
  28.9 0.8 collective-permute-start.1
  29.7 0.9 slice.30
  30.7 0.9 slice.28
  31.6 0.8 collective-permute-start.3
  32.5 6.8 %collective-permute-done.5.c_corner = bf16[3,7,4,512]{3,2,1,0:T(4,128)(2,1)S(1)} collective-permute-done((bf16[3,7,4,512]{3,2,1,0:T(4,128)(2,1)S(1)}, bf16[3,7,4,512]{3,2,1,0:T(4,128)(2,1)S(1)}, u32[]{:S(2)}, u32[]{:S(2)}) %collective-permute-start.5) | collective-permute-done | bytes 86048 | tf_op jit(solution)/shard_map/ppermute | solution.py:697
  39.4 6.2 %collective-permute-start.2 = (bf16[3,7,4,512]{3,2,1,0:T(4,128)(2,1)}, bf16[3,7,4,512]{3,2,1,0:T(4,128)(2,1)S(1)}, u32[]{:S(2)}, u32[]{:S(2)}) collective-permute-start(bf16[3,7,4,512]{3,2,1,0:T(4,128)(2,1)} %get-tuple-element.35), channel_id=1, source_target_pairs={{5,0},{6,1},{7,2},{4,3},{9,4},{10,5},{11,6},{8,7},{13,8},{14,9},{1... | collective-permute-start | bytes 258056 | tf_op jit(solution)/shard_map/ppermute | solution.py:697
  45.5 2.4 %collective-permute-done.2.y_corner = bf16[3,7,4,512]{3,2,1,0:T(4,128)(2,1)S(1)} collective-permute-done((bf16[3,7,4,512]{3,2,1,0:T(4,128)(2,1)}, bf16[3,7,4,512]{3,2,1,0:T(4,128)(2,1)S(1)}, u32[]{:S(2)}, u32[]{:S(2)}) %collective-permute-start.2) | collective-permute-done | bytes 86048 | tf_op jit(solution)/shard_map/ppermute | solution.py:697
  48.0 0.6 copy-done.8
  48.7 0.1 copy-done
  48.9 47.9 %second_block.1 = (bf16[14,7,8,512]{3,2,1,0:T(8,128)(2,1)}, bf16[3,7,8,512]{3,2,1,0:T(8,128)(2,1)}, bf16[11,7,4,512]{3,2,1,0:T(4,128)(2,1)}, bf16[3,7,4,512]{3,2...) custom-call(bf16[14,7,8,512]{3,2,1,0:T(8,128)(2,1)} %get-tuple-eleme, ...), custom_call_target="tpu_custom_call" | custom-call | tf_op jit(solution)/shard_map/second_block/pallas_call | solution.py:513
  96.9 0.3 collective-permute-start.8
  97.2 15.8 %collective-permute-done.8.corner_ref = bf16[3,7,4,512]{3,2,1,0:T(4,128)(2,1)S(1)} collective-permute-done((bf16[3,7,4,512]{3,2,1,0:T(4,128)(2,1)}, bf16[3,7,4,512]{3,2,1,0:T(4,128)(2,1)S(1)}, u32[]{:S(2)}, u32[]{:S(2)}) %collective-permute-start.8) | collective-permute-done | bytes 86048 | tf_op jit(solution)/shard_map/ppermute | solution.py:697
  113.1 0.5 copy-done.6
  113.7 0.1 copy-done.2
  113.9 31.8 %backward_first.1 = (bf16[14,7,8,512]{3,2,1,0:T(8,128)(2,1)}, bf16[2,4,4,4,4,640]{5,4,3,2,1,0:T(4,128)(2,1)}, bf16[2,4,4,4,4,640]{5,4,3,2,1,0:T(4,128)(2,1)}, bf16[2,4,4,4,4,768]{5,4,3,2,1,0:T(4,128)(2,1)}) custom-call(bf16[14,7,8,512]{3,2,1,0:T(8,128)(2,1)} %bitcast.8, f32[1,512]{1,0:T(1,128)} %bitcast.14, f32[1,512]{1,0:T(1,128)} %bitcast.16, ...), custom_call_target="tpu_custom_call" | custom-call | tf_op jit(solution)/shard_map/backward_first/pallas_call | solution.py:482
  145.6 24.0 %reduce_gradients.1 = (f32[4,640]{1,0:T(4,128)}, f32[4,640]{1,0:T(4,128)}, f32[4,768]{1,0:T(4,128)}, f32[4,640]{1,0:T(4,128)}, f32[4,640]{1,0:T(4,128)}, /*index=5*/f32[4,768]{1,0:T(4,128)}) custom-call(bf16[2,4,4,4,4,640]{5,4,3,2,1,0:T(4,128)(2,1)} %get-tuple-element.41.refs_0_, bf16[2,4,4,4,4,640]{5,4,3,2,1,0:T(4,128)(2,1)} %get-tuple-element.42.refs_1_, ...), custom_call_target="tpu_custom_call" | custom-call | tf_op jit(solution)/shard_map/reduce_gradients/pallas_call | solution.py:659
  169.7 0.7 slice.24
  170.4 1.3 slice.25
  171.7 0.7 slice.26
  172.3 1.3 slice.27
  173.6 1.4 pad_maximum_fusion
  (24 shorter events, 0.6 us)
Async XLA Ops:
  1.8 46.2 %collective-permute-start.4 = (bf16[11,7,4,512]{3,2,1,0:T(4,128)(2,1)S(1)}, bf16[11,7,4,512]{3,2,1,0:T(4,128)(2,1)S(1)}, u32[]{:S(2)}, u32[]{:S(2)}) collective-permute-start(bf16[11,7,4,512]{3,2,1,0:T(4,128)(2,1)S(1)} %slice.29), channel_id=1, source_target_pairs={{4,0},{8,4},{12,8},{16,12},{20,16},{24,20},{28,24},{32,28},{36,32}... | collective-permute-start | bytes 946184 | tf_op jit(solution)/shard_map/ppermute | solution.py:697
  28.9 19.1 %collective-permute-start.1 = (bf16[11,7,4,512]{3,2,1,0:T(4,128)(2,1)}, bf16[11,7,4,512]{3,2,1,0:T(4,128)(2,1)S(1)}, u32[]{:S(2)}, u32[]{:S(2)}) collective-permute-start(bf16[11,7,4,512]{3,2,1,0:T(4,128)(2,1)} %get-tuple-element.34), channel_id=1, source_target_pairs={{4,0},{8,4},{12,8},{16,12},{20,16},{24,20},{28,24},{32,28},{36,32}... | collective-permute-start | bytes 946184 | tf_op jit(solution)/shard_map/ppermute | solution.py:697
  30.6 8.7 %collective-permute-start.5 = (bf16[3,7,4,512]{3,2,1,0:T(4,128)(2,1)S(1)}, bf16[3,7,4,512]{3,2,1,0:T(4,128)(2,1)S(1)}, u32[]{:S(2)}, u32[]{:S(2)}) collective-permute-start(bf16[3,7,4,512]{3,2,1,0:T(4,128)(2,1)S(1)} %slice.30), channel_id=1, source_target_pairs={{5,0},{6,1},{7,2},{4,3},{9,4},{10,5},{11,6},{8,7},{13,8},{14,9},{1... | collective-permute-start | bytes 258056 | tf_op jit(solution)/shard_map/ppermute | solution.py:697
  31.6 16.3 %collective-permute-start.3 = (bf16[3,7,8,512]{3,2,1,0:T(8,128)(2,1)S(1)}, bf16[3,7,8,512]{3,2,1,0:T(8,128)(2,1)S(1)}, u32[]{:S(2)}, u32[]{:S(2)}) collective-permute-start(bf16[3,7,8,512]{3,2,1,0:T(8,128)(2,1)S(1)} %slice.28), channel_id=1, source_target_pairs={{1,0},{2,1},{3,2},{0,3},{5,4},{6,5},{7,6},{4,7},{9,8},{10,9},{11,1... | collective-permute-start | bytes 516104 | tf_op jit(solution)/shard_map/ppermute | solution.py:697
  32.5 15.5 %collective-permute-start = (bf16[3,7,8,512]{3,2,1,0:T(8,128)(2,1)}, bf16[3,7,8,512]{3,2,1,0:T(8,128)(2,1)S(1)}, u32[]{:S(2)}, u32[]{:S(2)}) collective-permute-start(bf16[3,7,8,512]{3,2,1,0:T(8,128)(2,1)} %get-tuple-element.33), channel_id=1, source_target_pairs={{1,0},{2,1},{3,2},{0,3},{5,4},{6,5},{7,6},{4,7},{9,8},{10,9},{11,1... | collective-permute-start | bytes 516104 | tf_op jit(solution)/shard_map/ppermute | solution.py:697
  39.4 8.7 %copy-start.7 = (bf16[3,7,4,512]{3,2,1,0:T(4,128)(2,1)}, bf16[3,7,4,512]{3,2,1,0:T(4,128)(2,1)S(1)}, u32[]{:S(2)}) copy-start(bf16[3,7,4,512]{3,2,1,0:T(4,128)(2,1)S(1)} %collective-permute-done.5.c_corner) | copy-start | bytes 258052
  39.4 8.6 %collective-permute-start.2 = (bf16[3,7,4,512]{3,2,1,0:T(4,128)(2,1)}, bf16[3,7,4,512]{3,2,1,0:T(4,128)(2,1)S(1)}, u32[]{:S(2)}, u32[]{:S(2)}) collective-permute-start(bf16[3,7,4,512]{3,2,1,0:T(4,128)(2,1)} %get-tuple-element.35), channel_id=1, source_target_pairs={{5,0},{6,1},{7,2},{4,3},{9,4},{10,5},{11,6},{8,7},{13,8},{14,9},{1... | collective-permute-start | bytes 258056 | tf_op jit(solution)/shard_map/ppermute | solution.py:697
  47.9 0.6 copy-start.8
  47.9 0.7 copy-start.3
  48.0 0.7 copy-start.4
  48.0 0.9 copy-start
  48.0 1.0 copy-start.1
  96.8 16.3 %collective-permute-start.7 = (bf16[11,7,4,512]{3,2,1,0:T(4,128)(2,1)}, bf16[11,7,4,512]{3,2,1,0:T(4,128)(2,1)S(1)}, u32[]{:S(2)}, u32[]{:S(2)}) collective-permute-start(bf16[11,7,4,512]{3,2,1,0:T(4,128)(2,1)} %get-tuple-element.38), channel_id=1, source_target_pairs={{124,0},{0,4},{4,8},{8,12},{12,16},{16,20},{20,24},{24,28},{28,32}... | collective-permute-start | bytes 946184 | tf_op jit(solution)/shard_map/ppermute | solution.py:697
  96.8 16.2 %collective-permute-start.6 = (bf16[3,7,8,512]{3,2,1,0:T(8,128)(2,1)}, bf16[3,7,8,512]{3,2,1,0:T(8,128)(2,1)S(1)}, u32[]{:S(2)}, u32[]{:S(2)}) collective-permute-start(bf16[3,7,8,512]{3,2,1,0:T(8,128)(2,1)} %get-tuple-element.37), channel_id=1, source_target_pairs={{3,0},{0,1},{1,2},{2,3},{7,4},{4,5},{5,6},{6,7},{11,8},{8,9},{9,10... | collective-permute-start | bytes 516104 | tf_op jit(solution)/shard_map/ppermute | solution.py:697
  96.9 16.1 %collective-permute-start.8 = (bf16[3,7,4,512]{3,2,1,0:T(4,128)(2,1)}, bf16[3,7,4,512]{3,2,1,0:T(4,128)(2,1)S(1)}, u32[]{:S(2)}, u32[]{:S(2)}) collective-permute-start(bf16[3,7,4,512]{3,2,1,0:T(4,128)(2,1)} %get-tuple-element.39), channel_id=1, source_target_pairs={{127,0},{124,1},{125,2},{126,3},{3,4},{0,5},{1,6},{2,7},{7,8},{4,9... | collective-permute-start | bytes 258056 | tf_op jit(solution)/shard_map/ppermute | solution.py:697
  113.0 0.6 copy-start.6
  113.0 0.7 copy-start.5
  113.1 0.8 copy-start.2

commit v3 on v2

--- a/solution.py
+++ b/solution.py
@@ -77,10 +77,10 @@
 
 
 def forward_kernel(
-    x_ref, gain_ref, bias_ref, wqkv_ref, wout_ref,
-    e_ref, mixt_ref, inv_ref, own_ref, row_ref, tm_ref, corner_ref,
-    qt, k, vt,
+    x_ref, cot_ref, gain_ref, bias_ref, wqkv_ref, wout_ref,
+    e_ref, mixt_ref, inv_ref, *refs,
 ):
+    y_pieces, c_pieces, (qt, k, vt) = refs[0:5], refs[5:10], refs[10:]
     w, g = pl.program_id(0), pl.program_id(1)
 
     @pl.when(g == 0)
@@ -123,19 +123,25 @@
     @pl.when(g == GROUP - 1)
     def _():
         y = tiles(x_ref[...]) + mm_tn(mixt_ref[0], wout_ref[...])
-        y = y.reshape(7, 7, 8, C).astype(BF16)
-        low = y.astype(F32)[:, :, 0:4].astype(BF16)
-        own_ref[...] = y
-
-        @pl.when(w == 0)
-        def _():
-            row_ref[...] = y[0:3]
-            corner_ref[...] = low[0:3]
-            tm_ref[0:4] = low[3:7]
-
-        @pl.when(w == 1)
-        def _():
-            tm_ref[4:11] = low
+        for whole, pieces in (
+            (y.reshape(7, 7, 8, C), y_pieces),
+            (cot_ref[...].astype(F32), c_pieces),
+        ):
+            own, ahead, behind, above, corner = pieces
+
+            @pl.when(w == 0)
+            def _():
+                above[...] = whole[0:3, :, 0:4].astype(BF16)
+                corner[...] = whole[0:3, :, 4:8].astype(BF16)
+                ahead[0:4] = whole[3:7, :, 0:4].astype(BF16)
+                own[0:4] = whole[3:7, :, 4:8].astype(BF16)
+
+            @pl.when(w == 1)
+            def _():
+                ahead[4:7] = whole[0:3, :, 0:4].astype(BF16)
+                own[4:7] = whole[0:3, :, 4:8].astype(BF16)
+                behind[...] = whole[3:7, :, 4:8].astype(BF16)
+                own[7:11] = whole[3:7, :, 0:4].astype(BF16)
 
 
 def write_parts(gqkv, gout, parts):
@@ -168,7 +174,7 @@
 def backward_first_kernel(
     scale,
     x_ref, gain_ref, bias_ref, wqkv_ref, wout_ref, e_ref, mixt_ref, inv_ref,
-    own_ref, row_ref, tm_ref, corner_ref,
+    own, ahead, behind, above, corner,
     grad_ref, part0_ref, part1_ref, part2_ref,
     xhat_s, rstd_s, normed_s, cot_s, q, kt, v, dot_s, dopt, dqt, dproj, gqkv_s, gout_s,
 ):
@@ -187,17 +193,18 @@
         v[...] = mm(normed, wqkv_ref[:, 2 * C :]).astype(BF16)
 
         def put(row, count, low, high):
-            whole = jnp.concatenate([low.astype(F32), high.astype(F32)[:, :, 4:8]], axis=2)
+            whole = jnp.concatenate([low.astype(F32), high.astype(F32)], axis=2)
             cot_s[56 * row : 56 * (row + count)] = whole.reshape(-1, C)
 
         @pl.when(w == 0)
         def _():
-            put(0, 3, corner_ref[...], row_ref[...])
-            put(3, 4, tm_ref[0:4], own_ref[3:7])
+            put(0, 3, above[...], corner[...])
+            put(3, 4, ahead[0:4], own[0:4])
 
         @pl.when(w == 1)
         def _():
-            put(0, 7, tm_ref[4:11], own_ref[7:14])
+            put(0, 3, ahead[4:7], own[4:7])
+            put(3, 4, own[7:11], behind[...])
 
         dot_s[...] = mm_nt(wout_ref[...], cot_s[...].astype(BF16)).astype(BF16)
 
@@ -252,15 +259,15 @@
 
 def second_kernel(
     scale,
-    y_own, y_row, y_tm, y_corner, c_own, c_row, c_tm, c_corner,
+    y_own, y_ahead, y_behind, y_above, y_corner, c_own, c_ahead, c_behind, c_above, c_corner,
     gain_ref, bias_ref, wqkv_ref, wout_ref,
-    own_ref, row_ref, tm_ref, corner_ref, part0_ref, part1_ref, part2_ref,
+    own, ahead, behind, above, corner, part0_ref, part1_ref, part2_ref,
     x_s, rstd_s, normed_s, cot_s, q, qt, k, kt, v, vt, dot_s, mixt, dopt, dqt, dproj, pen, e_s, dk_s, dv_s,
     gqkv_s, gout_s,
 ):
     part_refs = (part0_ref, part1_ref, part2_ref)
     w, g = pl.program_id(0), pl.program_id(1)
-    last_frames = lax.axis_index("tm") == lax.axis_size("tm") - 1
+    last_frames = lax.axis_index("tm") == jnp.where(w == 0, lax.axis_size("tm") - 1, 0)
     last_rows = (lax.axis_index("rows") == lax.axis_size("rows") - 1) & (w == 1)
 
     def region_of(token, segment):
@@ -271,23 +278,23 @@
 
     @pl.when(g == 0)
     def _():
-        def gather(into, own, row, tm, corner):
+        def gather(into, own, ahead, behind, above, corner):
             def put(rho, count, low, high):
-                whole = jnp.concatenate([low.astype(F32), high.astype(F32)[:, :, 4:8]], axis=2)
+                whole = jnp.concatenate([low.astype(F32), high.astype(F32)], axis=2)
                 into[32 * rho : 32 * (rho + count)] = whole[:, 3:7].reshape(-1, C)
                 into[224 + 24 * rho : 224 + 24 * (rho + count)] = whole[:, 0:3].reshape(-1, C)
 
             @pl.when(w == 0)
             def _():
-                put(0, 7, tm[0:7], own[3:10])
+                put(0, 7, ahead[...], own[0:7])
 
             @pl.when(w == 1)
             def _():
-                put(0, 4, tm[7:11], own[10:14])
-                put(4, 3, corner[...], row[...])
-
-        gather(x_s, y_own, y_row, y_tm, y_corner)
-        gather(cot_s, c_own, c_row, c_tm, c_corner)
+                put(0, 4, own[7:11], behind[...])
+                put(4, 3, above[...], corner[...])
+
+        gather(x_s, y_own, y_ahead, y_behind, y_above, y_corner)
+        gather(cot_s, c_own, c_ahead, c_behind, c_above, c_corner)
         xhat, rstd = standardized(x_s[...])
         x_s[...] = xhat
         rstd_s[...] = rstd
@@ -413,20 +420,19 @@
         second = total[224:392].reshape(7, 3, 8, C)
         whole = jnp.concatenate([second, first], axis=1)
         low = whole[:, :, 0:4].astype(BF16)
-        whole = whole.astype(BF16)
+        high = whole[:, :, 4:8].astype(BF16)
 
         @pl.when(w == 0)
         def _():
-            own_ref[0:3] = whole[0:3]
-            own_ref[3:10] = whole
-            tm_ref[0:7] = low
+            ahead[...] = low
+            own[0:7] = high
 
         @pl.when(w == 1)
         def _():
-            own_ref[10:14] = whole[0:4]
-            tm_ref[7:11] = low[0:4]
-            row_ref[...] = whole[4:7]
-            corner_ref[...] = low[4:7]
+            own[7:11] = low[0:4]
+            behind[...] = high[0:4]
+            above[...] = low[4:7]
+            corner[...] = high[4:7]
 
 
 def whole_block(shape):
@@ -435,7 +441,7 @@
 
 
 def piece_shapes():
-    return [(14, 7, 8, C), (3, 7, 8, C), (11, 7, 4, C), (3, 7, 4, C)]
+    return [(rows, 7, 4, C) for rows in (11, 7, 4, 3, 3)]
 
 
 WIDTHS = (640, 640, 768)
@@ -460,13 +466,13 @@
     )
 
 
-def forward_first(x, weights):
-    pieces = piece_shapes()
-    return pl.pallas_call(
+def forward_first(x, cot, weights):
+    pieces = piece_shapes() * 2
+    outs = pl.pallas_call(
         forward_kernel,
         grid=(2, GROUP),
-        in_specs=[WINDOW] + [whole_block(s) for s in WEIGHTS],
-        out_specs=SAVED + [WINDOW] + [whole_block(s) for s in pieces[1:]],
+        in_specs=[WINDOW, WINDOW] + [whole_block(s) for s in WEIGHTS],
+        out_specs=SAVED + [whole_block(s) for s in pieces],
         out_shape=SAVED_SHAPES + [jax.ShapeDtypeStruct(s, BF16) for s in pieces],
         scratch_shapes=[
             pltpu.VMEM((C, TOK), BF16),
@@ -475,7 +481,8 @@
         ],
         compiler_params=params(),
         name="forward_first",
-    )(x, *weights)
+    )(x, cot, *weights)
+    return outs[:3], outs[3:8], outs[8:]
 
 
 def backward_first(scale, x, weights, saved, pieces):
@@ -567,12 +574,63 @@
 MESH = pl.DeviceIdType.MESH
 
 
+ROUTES = ((-1, 0), (1, 0), (0, -1), (1, -1))
+
+
+def exchange_kernel(way, *refs):
+    count = (len(refs) - 2) // 2
+    sent, received, (send_sem, recv_sem) = refs[:count], refs[count : 2 * count], refs[2 * count :]
+    tm, rows = lax.axis_index("tm"), lax.axis_index("rows")
+    tm_size, rows_size = lax.axis_size("tm"), lax.axis_size("rows")
+
+    def at(steps, sign):
+        return (
+            (tm + sign * steps[0] + tm_size) % tm_size,
+            (rows + sign * steps[1] + rows_size) % rows_size,
+        )
+
+    barrier = pltpu.get_barrier_semaphore()
+    for steps in ROUTES:
+        pl.semaphore_signal(barrier, inc=1, device_id=at(steps, -way), device_id_type=MESH)
+    pl.semaphore_wait(barrier, len(ROUTES))
+    copies = []
+    for i in range(count):
+        copy = pltpu.make_async_remote_copy(
+            src_ref=sent[i],
+            dst_ref=received[i],
+            send_sem=send_sem.at[i],
+            recv_sem=recv_sem.at[i],
+            device_id=at(ROUTES[i % 4], way),
+            device_id_type=MESH,
+        )
+        copy.start()
+        copies.append(copy)
+    for copy in copies:
+        copy.wait()
+
+
+def exchanged(way, collective_id, *pieces):
+    count = len(pieces)
+    return pl.pallas_call(
+        functools.partial(exchange_kernel, way),
+        in_specs=[pl.BlockSpec(memory_space=pl.ANY)] * count,
+        out_specs=[pl.BlockSpec(memory_space=pl.ANY)] * count,
+        out_shape=[jax.ShapeDtypeStruct(p.shape, p.dtype) for p in pieces],
+        scratch_shapes=[pltpu.SemaphoreType.DMA((count,)), pltpu.SemaphoreType.DMA((count,))],
+        compiler_params=pltpu.CompilerParams(
+            collective_id=collective_id, has_side_effects=True, vmem_limit_bytes=VMEM_LIMIT
+        ),
+        name="exchange_there" if way == 1 else "exchange_back",
+    )(*pieces)
+
+
 def reduce_kernel(jobs, *refs):
-    parts, outs = refs[:jobs], refs[jobs : 2 * jobs]
-    scratch = refs[2 * jobs : 7 * jobs]
+    matrices = 2 * jobs // 3
+    parts, outs, refs = refs[:jobs], refs[jobs : jobs + matrices], refs[jobs + matrices :]
+    scratch = refs[: 5 * jobs]
     held = [scratch[5 * i : 5 * i + 2] for i in range(jobs)]
     slots = [scratch[5 * i + 2 : 5 * i + 5] for i in range(jobs)]
-    send_sem, recv_sem, local_sem = refs[7 * jobs :]
+    send_sem, recv_sem, local_sem = refs[5 * jobs :]
     here = coordinates()
     partners = [beside(here, "core", 1)] + [
         beside(here, axis, steps) for axis in "xyz" for steps in (1, 2, 3)
@@ -619,7 +677,12 @@
                 for slot in range(3):
                     total = total + slots[i][stage - 1][slot].astype(F32)
                 if stage == 3:
-                    outs[i][...] = total
+                    gqkv, gout = outs[i // 3 * 2 : i // 3 * 2 + 2]
+                    if i % 3 == 2:
+                        gqkv[:, 1280:1536] = total[:, 0:256]
+                        gout[...] = total[:, 256:768]
+                    else:
+                        gqkv[:, 640 * (i % 3) : 640 * (i % 3 + 1)] = total
                     continue
                 source = slots[i][stage - 1].at[3]
                 source[...] = total.astype(BF16)
@@ -659,8 +722,10 @@
     return pl.pallas_call(
         functools.partial(reduce_kernel, jobs),
         in_specs=[pl.BlockSpec(memory_space=pl.ANY)] * jobs,
-        out_specs=[pl.BlockSpec(memory_space=pltpu.VMEM)] * jobs,
-        out_shape=[jax.ShapeDtypeStruct((4, part.shape[-1]), F32) for part in parts],
+        out_specs=[pl.BlockSpec(memory_space=pltpu.VMEM)] * (2 * jobs // 3),
+        out_shape=[
+            jax.ShapeDtypeStruct((4, width), F32) for _ in range(jobs // 3) for width in (3 * C, C)
+        ],
         scratch_shapes=scratch
         + [
             pltpu.SemaphoreType.DMA((jobs, 10)),
@@ -672,37 +737,6 @@
         ),
         name="reduce_gradients",
     )(*parts)
-
-
-def moved(block, axes, steps):
-    sizes = [lax.axis_size(a) for a in axes]
-    total = math.prod(sizes)
-
-    def place(index):
-        out = []
-        for size in reversed(sizes):
-            out.append(index % size)
-            index //= size
-        return out[::-1]
-
-    def number(places):
-        index = 0
-        for p, size in zip(places, sizes):
-            index = index * size + p % size
-        return index
-
-    route = [
-        (number([p + s for p, s in zip(place(i), steps)]), i) for i in range(total)
-    ]
-    return lax.ppermute(block, axes if len(axes) > 1 else axes[0], route)
-
-
-def exchanged(row, tm, corner, step):
-    return (
-        moved(row, ("rows",), (step,)),
-        moved(tm, ("tm",), (step,)),
-        moved(corner, ("tm", "rows"), (step, step)),
-    )
 
 
 def per_device(
@@ -717,19 +751,15 @@
     cot = cotangent.transpose(1, 2, 0, 3)
     first = (gain_first.reshape(1, C), bias_first.reshape(1, C), qkv_first, out_first)
     second = (gain_second.reshape(1, C), bias_second.reshape(1, C), qkv_second, out_second)
-    c_pieces = (cot,) + exchanged(cot[0:3], cot[3:14, :, 0:4], cot[0:3, :, 0:4], 1)
-    *saved, own, row, tm, corner = forward_first(x, first)
-    y_pieces = (own,) + exchanged(row, tm, corner, 1)
-    own, row, tm, corner, *parts2 = second_block(scale, y_pieces, c_pieces, second)
-    d_pieces = (own,) + exchanged(row, tm, corner, -1)
-    grad, *parts1 = backward_first(scale, x, first, saved, d_pieces)
-    sums = reduced(parts1 + parts2)
-
-    def matrices(sums):
-        gqkv = jnp.concatenate([sums[0], sums[1], sums[2][:, :256]], axis=1)
-        return gqkv, sums[2][:, 256:]
-
-    return (grad.transpose(2, 0, 1, 3), *matrices(sums[:3]), *matrices(sums[3:]))
+    saved, y_pieces, c_pieces = forward_first(x, cot, first)
+    arrived = exchanged(1, 1, *y_pieces[1:], *c_pieces[1:])
+    y_pieces = [y_pieces[0], *arrived[:4]]
+    c_pieces = [c_pieces[0], *arrived[4:]]
+    *d_pieces, part0, part1, part2 = second_block(scale, y_pieces, c_pieces, second)
+    d_pieces = [d_pieces[0], *exchanged(-1, 2, *d_pieces[1:])]
+    grad, *parts = backward_first(scale, x, first, saved, d_pieces)
+    sums = reduced([*parts, part0, part1, part2])
+    return (grad.transpose(2, 0, 1, 3), *sums)
 
 
 def solution(mesh):

time: 176 us -> 166 us (0.943)
  Pallas kernels: 122 us -> 160 us
  waiting for transfers between devices: 25.1 us -> 0 us
  starting transfers between devices: 17.4 us -> 0 us
  local copies, waits for them, and re-layouts: 8.69 us -> 5.28 us
    pallas_call x1 -> x3, Pallas kernels: 18 us -> 54.3 us  [the longest x2 35.8 us: exchanged(): pl.pallas_call(functools.partial(exchange_kernel, way), in_specs=[pl.Bloc...]
    ppermute x9 -> x0, waiting for transfers between devices: 25.1 us -> none  [moved(): return lax.ppermute(block, axes if len(axes) > 1 else axes[0], route)]
    ppermute x9 -> x0, starting transfers between devices: 17.4 us -> none  [moved(): return lax.ppermute(block, axes if len(axes) > 1 else axes[0], route)]
    slice x7 -> x0, local copies, waits for them, and re-layouts: 6.99 us -> none  [the longest x2 2.59 us: matrices(): return (gqkv, sums[2][:, 256:])]
    unnamed x18 -> x4, local copies, waits for them, and re-layouts: 1.7 us -> 5.28 us
    pallas_call x1, Pallas kernels: 24 us -> 26 us  [reduced(): pl.pallas_call(functools.partial(reduce_kernel, jobs), in_specs=[pl.Block...]
  transfers between devices with their start and end apart: 9 -> 0, of which waited for: 4 -> 0; matrix products, arithmetic and copies ran while one was open for 1% -> 0% of each run, Pallas kernels for 10% -> 0%
where the time goes in v3:
time: 166 us
  Pallas kernels  160 us (96%)
  local copies, waits for them, and re-layouts  5.28 us (3%)
    pallas_call x1, Pallas kernels, second_block(): pl.pallas_call(functools.partial(second_kernel, scale), grid=(2, GROUP),...  47.4 us
    pallas_call x2, Pallas kernels, exchanged(): pl.pallas_call(functools.partial(exchange_kernel, way), in_specs=[pl.Bloc...  35.8 us
    pallas_call x1, Pallas kernels, backward_first(): pl.pallas_call(functools.partial(backward_first_kernel, scale), grid=(2,...  31.8 us
    pallas_call x1, Pallas kernels, reduced(): pl.pallas_call(functools.partial(reduce_kernel, jobs), in_specs=[pl.Block...  26 us
    pallas_call x1, Pallas kernels, forward_first(): pl.pallas_call(forward_kernel, grid=(2, GROUP), in_specs=[WINDOW, WINDOW]...  18.6 us
    unnamed x4, local copies, waits for them, and re-layouts  5.28 us

profile of v3, /device:TPU:0, one launch (start us, length us, event | category | flops | bytes accessed | tf_op | source)
XLA Modules:
  0.0 165.6 jit_solution(9395084683073330928)
XLA Ops:
  0.6 18.6 %forward_first.1 = (bf16[2,16,392,392]{3,2,1,0:T(8,128)(2,1)}, bf16[2,512,392]{2,1,0:T(8,128)(2,1)}, f32[2,4,4,392]{3,2,1,0:T(4,128)}, bf16[11,7,4,512]{3,2,1,0:...) custom-call(bf16[14,7,8,512]{3,2,1,0:T(8,128)(2,1)} %bitcast.7, ...), custom_call_target="tpu_custom_call" | custom-call | tf_op jit(solution)/shard_map/forward_first/pallas_call | solution.py:471
  19.2 21.8 %exchange_there.1 = (bf16[7,7,4,512]{3,2,1,0:T(4,128)(2,1)}, bf16[4,7,4,512]{3,2,1,0:T(4,128)(2,1)}, bf16[3,7,4,512]{3,2,1,0:T(4,128)(2,1)}, bf16[3,7,4,512]{3,2...) custom-call(bf16[7,7,4,512]{3,2,1,0:T(4,128)(2,1)} %get-tuple-elemen, ...), custom_call_target="tpu_custom_call" | custom-call | tf_op jit(solution)/shard_map/exchange_there/pallas_call | solution.py:614
  41.0 47.4 %second_block.1 = (bf16[11,7,4,512]{3,2,1,0:T(4,128)(2,1)}, bf16[7,7,4,512]{3,2,1,0:T(4,128)(2,1)}, bf16[4,7,4,512]{3,2,1,0:T(4,128)(2,1)}, bf16[3,7,4,512]{3,2,...) custom-call(bf16[11,7,4,512]{3,2,1,0:T(4,128)(2,1)} %get-tuple-eleme, ...), custom_call_target="tpu_custom_call" | custom-call | tf_op jit(solution)/shard_map/second_block/pallas_call | solution.py:520
  88.5 13.9 %exchange_back.1 = (bf16[7,7,4,512]{3,2,1,0:T(4,128)(2,1)}, bf16[4,7,4,512]{3,2,1,0:T(4,128)(2,1)}, bf16[3,7,4,512]{3,2,1,0:T(4,128)(2,1)}, bf16[3,7,4,512]{3,2,1,0:T(4,128)(2,1)}) custom-call(bf16[7,7,4,512]{3,2,1,0:T(4,128)(2,1)} %get-tuple-element.68.refs_0_, bf16[4,7,4,512]{3,2,1,0:T(4,128)(2,1)} %get-tuple-element.69.refs_1_, ...), custom_call_target="tpu_custom_call" | custom-call | tf_op jit(solution)/shard_map/exchange_back/pallas_call | solution.py:614
  102.4 31.8 %backward_first.1 = (bf16[14,7,8,512]{3,2,1,0:T(8,128)(2,1)}, bf16[2,4,4,4,4,640]{5,4,3,2,1,0:T(4,128)(2,1)}, bf16[2,4,4,4,4,640]{5,4,3,2,1,0:T(4,128)(2,1)}, bf16[2,4,4,4,4,768]{5,4,3,2,1,0:T(4,128)(2,1)}) custom-call(bf16[14,7,8,512]{3,2,1,0:T(8,128)(2,1)} %bitcast.8, f32[1,512]{1,0:T(1,128)} %bitcast.11, f32[1,512]{1,0:T(1,128)} %bitcast.13, ...), custom_call_target="tpu_custom_call" | custom-call | tf_op jit(solution)/shard_map/backward_first/pallas_call | solution.py:489
  134.3 26.0 %reduce_gradients.1 = (f32[4,1536]{1,0:T(4,128)}, f32[4,512]{1,0:T(4,128)}, f32[4,1536]{1,0:T(4,128)}, f32[4,512]{1,0:T(4,128)}) custom-call(bf16[2,4,4,4,4,640]{5,4,3,2,1,0:T(4,128)(2,1)} %get-tuple-element.77.refs_0_, bf16[2,4,4,4,4,640]{5,4,3,2,1,0:T(4,128)(2,1)} %get-tuple-element.78.refs_1_, bf16[2,4,4,4,4,768]{5,4,3,2,1,0:T(4,128)(2,1)} %get-tuple-element.79.refs_2_, ...), custom_call_target="tpu_custom_call" | custom-call | tf_op jit(solution)/shard_map/reduce_gradients/pallas_call | solution.py:722
  160.3 1.3 copy.19
  161.6 1.3 copy.20
  162.9 1.3 copy.21
  164.3 1.3 copy.22

commit v4 on v0

v4 whole, which is shorter than its diff:
```python
import functools
import math

import jax
import jax.numpy as jnp
from jax import lax
from jax.experimental import pallas as pl
from jax.experimental.pallas import tpu as pltpu
from jax.sharding import PartitionSpec as P

F32, BF16 = jnp.float32, jnp.bfloat16
C, HEADS, HD = 512, 16, 32
TOK = 392
GROUP = 4
VROWS = 48
LOG2E = math.log2(math.e)
QSCALE = HD ** (-0.5) * LOG2E
MASKED = -1000000000.0 * LOG2E
LN2 = math.log(2.0)
SPLIT = ((0, 224), (224, 392))
VIRTUAL = 16
ROWS = 400
VMEM_LIMIT = 56 * 1024 * 1024


def mm(a, b):
    return lax.dot_general(a, b, (((1,), (0,)), ((), ())), preferred_element_type=F32)


def mm_nt(a, b):
    return lax.dot_general(a, b, (((1,), (1,)), ((), ())), preferred_element_type=F32)


def mm_tn(a, b):
    return lax.dot_general(a, b, (((0,), (0,)), ((), ())), preferred_element_type=F32)


def standardized(values):
    center = values - jnp.mean(values, axis=-1, keepdims=True)
    rstd = lax.rsqrt(jnp.mean(center * center, axis=-1, keepdims=True) + 1e-05)
    return center * rstd, rstd


def tiles(block):
    return block.astype(F32).reshape(-1, C)


def own_lanes(j, block):
    lane = lax.broadcasted_iota(jnp.int32, block.shape, 1) // HD
    return jnp.where(lane == j, block, jnp.zeros_like(block))


def put_diagonal(ref, turned, pitch, column=0):
    for head in range(HEADS):
        at = pitch * (head % GROUP) + column
        ref[HD * head : HD * (head + 1), at : at + turned.shape[1]] = turned[HD * head : HD * (head + 1)]


def put_values(vt, turned, lane):
    count = turned.shape[1]
    for head in range(HEADS):
        vt[VROWS * head : VROWS * head + HD, lane : lane + count] = turned[HD * head : HD * (head + 1)]
        vt[VROWS * head + HD : VROWS * (head + 1), lane : lane + count] = jnp.ones(
            (VROWS - HD, count), BF16
        )


def channels_of(g, first=0):
    return pl.ds(pl.multiple_of(g * 128 + first, 128), 128)


def head_channels(g, j):
    return pl.ds(pl.multiple_of(g * 128 + j * HD, HD), HD)


def head_values(g, j):
    return pl.ds(pl.multiple_of(g * GROUP * VROWS + j * VROWS, 16), VROWS)


MESH = pl.DeviceIdType.MESH
ROUTES = ((-1, 0), (1, 0), (0, -1), (1, -1))


class Exchange:
    def __init__(self, way, send_sem, recv_sem):
        self.way, self.sems, self.copies = way, (send_sem, recv_sem), []

    def device(self, steps, sign):
        size = lax.axis_size("tm"), lax.axis_size("rows")
        here = lax.axis_index("tm"), lax.axis_index("rows")
        return tuple((i + sign * d + n) % n for i, d, n in zip(here, steps, size))

    def greet(self):
        for steps in ROUTES:
            pl.semaphore_signal(
                pltpu.get_barrier_semaphore(),
                inc=1,
                device_id=self.device(steps, -self.way),
                device_id_type=MESH,
            )

    def wait_for_others(self):
        pl.semaphore_wait(pltpu.get_barrier_semaphore(), len(ROUTES))

    def send(self, route, source, target):
        i = len(self.copies)
        copy = pltpu.make_async_remote_copy(
            src_ref=source,
            dst_ref=target,
            send_sem=self.sems[0].at[i],
            recv_sem=self.sems[1].at[i],
            device_id=self.device(ROUTES[route], self.way),
            device_id_type=MESH,
        )
        copy.start()
        self.copies.append(copy)

    def wait(self):
        for copy in self.copies:
            copy.wait()


def pieces_of(whole, w, pieces):
    own, ahead, behind, above, corner = pieces
    if w == 0:
        above[...] = whole[0:3, :, 0:4].astype(BF16)
        corner[...] = whole[0:3, :, 4:8].astype(BF16)
        ahead[0:4] = whole[3:7, :, 0:4].astype(BF16)
        own[0:4] = whole[3:7, :, 4:8].astype(BF16)
    else:
        ahead[4:7] = whole[0:3, :, 0:4].astype(BF16)
        own[4:7] = whole[0:3, :, 4:8].astype(BF16)
        behind[...] = whole[3:7, :, 4:8].astype(BF16)
        own[7:11] = whole[3:7, :, 0:4].astype(BF16)


def joined(low, high):
    return jnp.concatenate([low.astype(F32), high.astype(F32)], axis=2)


def forward_kernel(
    x_ref, cot_ref, gain_ref, bias_ref, wqkv_ref, wout_ref, mixt_ref, stat_ref, *refs,
):
    y_own, c_own, y_there, c_there, y_here, c_here = (
        refs[0], refs[1], refs[2:6], refs[6:10], refs[10:14], refs[14:18]
    )
    qbd, k, vt, send_sem, recv_sem = refs[18:]
    exchange = Exchange(1, send_sem, recv_sem)
    exchange.greet()
    for w in range(2):
        pieces_of(cot_ref[7 * w : 7 * w + 7].astype(F32), w, (c_own, *c_here))
    exchange.wait_for_others()
    for route in range(4):
        exchange.send(route, c_here[route], c_there[route])
    qbd[...] = jnp.zeros_like(qbd)
    for w in range(2):
        rows = slice(7 * w, 7 * w + 7)
        x = tiles(x_ref[rows])
        xhat, _ = standardized(x)
        normed = (xhat * gain_ref[...] + bias_ref[...]).astype(BF16)
        put_diagonal(qbd, (mm(normed, wqkv_ref[:, 0:C]) * QSCALE).astype(BF16).T, 512)
        k[...] = mm(normed, wqkv_ref[:, C : 2 * C]).astype(BF16)
        put_values(vt, mm(normed, wqkv_ref[:, 2 * C :]).astype(BF16).T, 0)

        def group(g, carry):
            kg = k[:, channels_of(g)]
            for j in range(GROUP):
                lanes = slice(512 * j, 512 * (j + 1))
                scores = mm(kg, qbd[channels_of(g), lanes])
                top = jnp.max(scores, axis=0, keepdims=True)
                e = jnp.exp2(scores - top).astype(BF16)
                mixed = mm(vt[head_values(g, j), :], e)
                sums = mixed[HD : HD + 1]
                stat_ref[w, g, :, lanes] = top + jnp.log2(sums)
                mixt_ref[w, head_channels(g, j), :] = (mixed[:HD] * (1.0 / sums)).astype(BF16)
            return carry

        lax.fori_loop(0, HEADS // GROUP, group, 0)
        y = x + mm_tn(mixt_ref[w, :, 0:TOK], wout_ref[...])
        pieces_of(y.reshape(7, 7, 8, C), w, (y_own, *y_here))
        if w == 0:
            exchange.send(2, y_here[2], y_there[2])
            exchange.send(3, y_here[3], y_there[3])
            exchange.send(0, y_here[0].at[0:4], y_there[0].at[0:4])
        else:
            exchange.send(0, y_here[0].at[4:7], y_there[0].at[4:7])
            exchange.send(1, y_here[1], y_there[1])
    exchange.wait()


def write_parts(gqkv, gout, parts):
    def layer(z, carry):
        for xy in range(16):
            x, y = xy // 4, xy % 4
            rows = pl.ds(pl.multiple_of((z * 16 + x // 2 * 8 + y * 2 + x % 2) * 8, 8), 8)
            blocks = (
                gqkv[rows, 0:640],
                gqkv[rows, 640:1280],
                jnp.concatenate([gqkv[rows, 1280:1536], gout[rows, :]], axis=1),
            )
            for part, block, place in zip(parts, blocks, ((x, y, z), (y, z, x), (z, x, y))):
                part[(0,) + place] = block[0:4].astype(BF16)
                part[(1,) + place] = block[4:8].astype(BF16)
        return carry

    lax.fori_loop(0, 4, layer, 0)


def norm_backward(dnormed, xhat, rstd, gain):
    d = dnormed.astype(BF16).astype(F32) * gain
    return rstd * (
        d
        - jnp.mean(d, axis=-1, keepdims=True)
        - xhat * jnp.mean(d * xhat, axis=-1, keepdims=True)
    )


def finish_gradients(scale, normed, dproj, mixt, cot_b, gqkv_s, gout_s, part_refs):
    gout_s[...] = mm(mixt[...], cot_b[...]) * scale
    gqkv_s[...] = mm_tn(normed[...], dproj[...]) * scale
    write_parts(gqkv_s, gout_s, part_refs)


def backward_first_kernel(
    scale,
    x_ref, gain_ref, bias_ref, wqkv_ref, wout_ref, mixt_ref, stat_ref,
    own, ahead, behind, above, corner,
    grad_ref, part0_ref, part1_ref, part2_ref,
    normed_s, dproj, cot_b, mixt_all, qbd, k, kt, v, qn, don, dobd, p_s, ds_s, dqt, do_rows, q_rows, gqkv_s, gout_s,
):
    for ref in (qbd, dobd, do_rows, q_rows, normed_s, dproj, cot_b):
        ref[...] = jnp.zeros_like(ref)
    for w in range(2):
        base = ROWS * w
        xhat, rstd = standardized(tiles(x_ref[7 * w : 7 * w + 7]))
        normed = (xhat * gain_ref[...] + bias_ref[...]).astype(BF16)
        normed_s[base : base + TOK] = normed
        queries = (mm(normed, wqkv_ref[:, 0:C]) * QSCALE).astype(BF16)
        qn[...] = queries
        put_diagonal(qbd, queries.T, 512)
        keys = mm(normed, wqkv_ref[:, C : 2 * C]).astype(BF16)
        k[...] = keys
        kt[...] = keys.T
        v[...] = mm(normed, wqkv_ref[:, 2 * C :]).astype(BF16)
        if w == 0:
            parts = [joined(above[...], corner[...]), joined(ahead[0:4], own[0:4])]
        else:
            parts = [joined(ahead[4:7], own[4:7]), joined(own[7:11], behind[...])]
        cot = jnp.concatenate([part.reshape(-1, C) for part in parts], axis=0)
        cot_h = cot.astype(BF16)
        cot_b[512 * w : 512 * w + TOK] = cot_h
        dmixed = mm_nt(cot_h, wout_ref[...]).astype(BF16)
        don[...] = dmixed
        put_diagonal(dobd, dmixed.T, 512)
        mixt_all[:, 512 * w : 512 * (w + 1)] = mixt_ref[w]

        def group(g, carry):
            kg = k[:, channels_of(g)]
            vg = v[:, channels_of(g)]
            qg = qn[:, channels_of(g)]
            dog = don[:, channels_of(g)]
            for j in range(GROUP):
                lanes = slice(512 * j, 512 * (j + 1))
                do_rows[512 * j : 512 * j + TOK] = own_lanes(j, dog)
                q_rows[512 * j : 512 * j + TOK] = own_lanes(j, qg)
                scores = mm(kg, qbd[channels_of(g), lanes])
                p = jnp.exp2(scores - stat_ref[w, g, :, lanes]).astype(BF16)
                p_s[:, lanes] = p
                dsum = jnp.sum(
                    mixt_ref[w, head_channels(g, j), :].astype(F32)
                    * dobd[head_channels(g, j), lanes].astype(F32),
                    axis=0, keepdims=True,
                )
                dp = mm(vg, dobd[channels_of(g), lanes]) - dsum
                ds = (p.astype(F32) * dp).astype(BF16)
                ds_s[:, lanes] = ds
                dq = mm(kt[head_channels(g, j), :], ds)
                dqt[HD * j : HD * (j + 1), :] = (dq[:, 0:TOK] * HD ** (-0.5)).astype(BF16)
            dk = mm(ds_s[...], q_rows[...]) * LN2
            dv = mm(p_s[...], do_rows[...])
            rows = slice(base, base + TOK)
            dproj[rows, channels_of(g)] = dqt[...].T
            dproj[rows, channels_of(g, C)] = dk.astype(BF16)
            dproj[rows, channels_of(g, 2 * C)] = dv.astype(BF16)
            return carry

        lax.fori_loop(0, HEADS // GROUP, group, 0)
        dnormed = mm_nt(dproj[base : base + TOK], wqkv_ref[...])
        total = cot + norm_backward(dnormed, xhat, rstd, gain_ref[...])
        grad_ref[7 * w : 7 * w + 7] = total.reshape(7, 7, 8, C).astype(BF16)
    finish_gradients(
        scale, normed_s, dproj, mixt_all, cot_b, gqkv_s, gout_s, (part0_ref, part1_ref, part2_ref)
    )


def second_kernel(
    scale,
    y_own, y_ahead, y_behind, y_above, y_corner, c_own, c_ahead, c_behind, c_above, c_corner,
    gain_ref, bias_ref, wqkv_ref, wout_ref,
    own, ahead_there, behind_there, above_there, corner_there, part0_ref, part1_ref, part2_ref,
    normed_s, dproj, cot_b, mixt, qbd, k, kt, v, vt, qn, dot_s, dobd, dopt, dqt,
    e_a, e_b, ds_a, ds_b, do_rows, q_rows, pen, cot_s, xhat_s, gqkv_s, gout_s,
    ahead, behind, above, corner, send_sem, recv_sem,
):
    exchange = Exchange(-1, send_sem, recv_sem)
    exchange.greet()
    e_s, ds_s = (e_a, e_b), (ds_a, ds_b)
    for ref in (qbd, dobd, do_rows, q_rows, normed_s, dproj, cot_b, mixt):
        ref[...] = jnp.zeros_like(ref)
    for w in range(2):
        base = ROWS * w
        last_frames = lax.axis_index("tm") == (lax.axis_size("tm") - 1 if w == 0 else 0)
        last_rows = (lax.axis_index("rows") == lax.axis_size("rows") - 1) if w == 1 else False

        def region_of(token, segment):
            columns = 4 if segment == 0 else 3
            late = jnp.where(last_frames & (token % 8 < 4), 1, 0)
            below = jnp.where(last_rows & (token // 8 // columns >= 4), 2, 0)
            return late + below

        def gather(into, own, ahead, behind, above, corner):
            def put(rho, count, whole):
                into[32 * rho : 32 * (rho + count)] = whole[:, 3:7].reshape(-1, C)
                into[224 + 24 * rho : 224 + 24 * (rho + count)] = whole[:, 0:3].reshape(-1, C)

            if w == 0:
                put(0, 7, joined(ahead[...], own[0:7]))
            else:
                put(0, 4, joined(own[7:11], behind[...]))
                put(4, 3, joined(above[...], corner[...]))

        gather(xhat_s, y_own, y_ahead, y_behind, y_above, y_corner)
        gather(cot_s, c_own, c_ahead, c_behind, c_above, c_corner)
        xhat, rstd = standardized(xhat_s[...])
        xhat_s[...] = xhat
        normed = (xhat * gain_ref[...] + bias_ref[...]).astype(BF16)
        normed_s[base : base + TOK] = normed
        queries = (mm(normed, wqkv_ref[:, 0:C]) * QSCALE).astype(BF16)
        qn[...] = queries
        keys = mm(normed, wqkv_ref[:, C : 2 * C]).astype(BF16)
        k[...] = keys
        values_f = mm(normed, wqkv_ref[:, 2 * C :])
        values = values_f.astype(BF16)
        v[...] = values
        cot_h = cot_s[...].astype(BF16)
        dmixed = mm_nt(cot_h, wout_ref[...]).astype(BF16)
        for s, (start, stop) in enumerate(SPLIT):
            count = stop - start
            cot_b[512 * w + 256 * s : 512 * w + 256 * s + count] = cot_h[start:stop]
            put_diagonal(qbd, queries[start:stop].T, 256, 1024 * s)
            kt[:, 256 * s : 256 * s + count] = keys[start:stop].T
            dot_s[:, 256 * s : 256 * s + count] = dmixed[start:stop].T
            turned = values[start:stop].T
            put_values(vt, turned, 256 * s)
            total = jnp.sum(turned.astype(F32), axis=1, keepdims=True)
            other = 1 - s
            lane = 256 * other + SPLIT[other][1] - SPLIT[other][0]
            first = lax.broadcasted_iota(jnp.int32, (C, VIRTUAL), 1) == 0
            total = jnp.where(first, total, 0.0).astype(BF16)
            number = jnp.where(first[0 : VROWS - HD], float(count), 0.0).astype(BF16)
            for head in range(HEADS):
                at = VROWS * head
                vt[at : at + HD, lane : lane + VIRTUAL] = total[HD * head : HD * (head + 1)]
                vt[at + HD : at + VROWS, lane : lane + VIRTUAL] = number
            shape = (count, 256)
            key = region_of(lax.broadcasted_iota(jnp.int32, shape, 0), s)
            query = region_of(lax.broadcasted_iota(jnp.int32, shape, 1), s)
            pen[start:stop] = jnp.where(key == query, 0.0, 1.0)

        def group(g, carry):
            virtual_dv = []
            grads = []
            for s, (start, stop) in enumerate(SPLIT):
                count = stop - start
                kg = k[start:stop, channels_of(g)]
                apart = pen[start:stop] > 0.5
                sums_of = []
                for j in range(GROUP):
                    lanes = slice(256 * j, 256 * (j + 1))
                    scores = mm(kg, qbd[channels_of(g), 1024 * s + 256 * j : 1024 * s + 256 * (j + 1)])
                    scores = jnp.where(apart, MASKED, scores)
                    top = jnp.maximum(jnp.max(scores, axis=0, keepdims=True), MASKED)
                    e_s[s][0:count, lanes] = jnp.exp2(scores - top).astype(BF16)
                    first = lax.broadcasted_iota(jnp.int32, (VIRTUAL, 256), 0) == 0
                    e_s[s][count : count + VIRTUAL, lanes] = jnp.where(
                        first, jnp.exp2(MASKED - top), 0.0
                    ).astype(BF16)
                for j in range(GROUP):
                    lanes = slice(256 * j, 256 * (j + 1))
                    tokens = slice(256 * s, 256 * (s + 1))
                    mixed = mm(
                        vt[head_values(g, j), 256 * s : 256 * s + count + VIRTUAL], e_s[s][:, lanes]
                    )
                    inv = 1.0 / mixed[HD : HD + 1]
                    mixed = mixed[:HD] * inv
                    mixt[head_channels(g, j), 512 * w + 256 * s : 512 * w + 256 * s + count] = mixed[
                        :, 0:count
                    ].astype(BF16)
                    do = dot_s[head_channels(g, j), tokens].astype(F32) * inv
                    inside = lax.broadcasted_iota(jnp.int32, do.shape, 1) < count
                    do = jnp.where(inside, do, 0.0).astype(BF16)
                    sums_of.append(jnp.sum(mixed * do.astype(F32), axis=0, keepdims=True))
                    dopt[HD * j : HD * (j + 1), tokens] = do
                    dobd[HD * j : HD * (j + 1), 1024 * s + 256 * j : 1024 * s + 256 * (j + 1)] = do
                turned = dopt[:, 256 * s : 256 * (s + 1)].T
                qg = qn[start:stop, channels_of(g)]
                for j in range(GROUP):
                    lanes = slice(256 * j, 256 * (j + 1))
                    at = 1024 * s + 256 * j
                    do_rows[at : at + 256] = own_lanes(j, turned)
                    q_rows[at : at + count] = own_lanes(j, qg)
                    dp = mm(v[start:stop, channels_of(g)], dobd[:, at : at + 256]) - sums_of[j]
                    ds = e_s[s][0:count, lanes].astype(F32) * jnp.where(apart, 0.0, dp)
                    ds = ds.astype(BF16)
                    ds_s[s][:, lanes] = ds
                    dq = mm(kt[head_channels(g, j), 256 * s : 256 * s + count], ds)
                    dqt[HD * j : HD * (j + 1), 256 * s : 256 * (s + 1)] = (dq * HD ** (-0.5)).astype(BF16)
                block = slice(1024 * s, 1024 * (s + 1))
                dv = mm(e_s[s][...], do_rows[block])
                dk = mm(ds_s[s][...], q_rows[block]) * LN2
                virtual_dv.append(dv[count : count + 1])
                grads.append((dk, dv[0:count]))
            for s, (start, stop) in enumerate(SPLIT):
                rows = slice(base + start, base + stop)
                dk, dv = grads[s]
                dproj[rows, channels_of(g)] = dqt[:, 256 * s : 256 * s + stop - start].T
                dproj[rows, channels_of(g, C)] = dk.astype(BF16)
                dproj[rows, channels_of(g, 2 * C)] = (dv + virtual_dv[1 - s]).astype(BF16)
            return carry

        lax.fori_loop(0, HEADS // GROUP, group, 0)
        dnormed = mm_nt(dproj[base : base + TOK], wqkv_ref[...])
        total = cot_s[...] + norm_backward(dnormed, xhat_s[...], rstd, gain_ref[...])
        whole = jnp.concatenate(
            [total[224:392].reshape(7, 3, 8, C), total[0:224].reshape(7, 4, 8, C)], axis=1
        )
        low, high = whole[:, :, 0:4].astype(BF16), whole[:, :, 4:8].astype(BF16)
        if w == 0:
            ahead[...] = low
            own[0:7] = high
            exchange.wait_for_others()
            exchange.send(0, ahead, ahead_there)
        else:
            own[7:11] = low[0:4]
            behind[...] = high[0:4]
            above[...] = low[4:7]
            corner[...] = high[4:7]
            exchange.send(1, behind, behind_there)
            exchange.send(2, above, above_there)
            exchange.send(3, corner, corner_there)
    finish_gradients(
        scale, normed_s, dproj, mixt, cot_b, gqkv_s, gout_s, (part0_ref, part1_ref, part2_ref)
    )
    exchange.wait()


def piece_shapes():
    return [(rows, 7, 4, C) for rows in (11, 7, 4, 3, 3)]


WIDTHS = (640, 640, 768)
PARTS = [(2, 4, 4, 4, 4, width) for width in WIDTHS]
SAVED = [
    jax.ShapeDtypeStruct((2, C, 512), BF16),
    jax.ShapeDtypeStruct((2, HEADS // GROUP, 1, 2048), F32),
]
TOKENS = (14, 7, 8, C)
IN_VMEM = pl.BlockSpec(memory_space=pltpu.VMEM)


ANYWHERE = pl.BlockSpec(memory_space=pl.ANY)


def call(kernel, name, args, out_shape, scratch, there=(), copies=0, collective_id=None):
    semaphores = [pltpu.SemaphoreType.DMA((copies,))] * 2 if copies else []
    return pl.pallas_call(
        kernel,
        in_specs=[IN_VMEM] * len(args),
        out_specs=[ANYWHERE if i in there else IN_VMEM for i in range(len(out_shape))],
        out_shape=out_shape,
        scratch_shapes=[pltpu.VMEM(shape, dtype) for shape, dtype in scratch] + semaphores,
        compiler_params=pltpu.CompilerParams(
            vmem_limit_bytes=VMEM_LIMIT,
            has_side_effects=bool(copies),
            collective_id=collective_id,
        ),
        name=name,
    )(*args)


def halves(shapes):
    return [jax.ShapeDtypeStruct(shape, BF16) for shape in shapes]


def forward_first(x, cot, weights):
    pieces = piece_shapes()
    outs = call(
        forward_kernel,
        "forward_first",
        (x, cot, *weights),
        SAVED + halves(pieces[:1] * 2 + pieces[1:] * 2),
        [(shape, BF16) for shape in pieces[1:] * 2]
        + [((C, 2048), BF16), ((TOK, C), BF16), ((HEADS * VROWS, TOK), BF16)],
        there=range(4, 12),
        copies=9,
        collective_id=1,
    )
    return outs[:2], [outs[2], *outs[4:8]], [outs[3], *outs[8:12]]


GRADIENT_SCRATCH = [((2 * ROWS, C), BF16), ((2 * ROWS, 3 * C), BF16), ((1024, C), BF16), ((C, 1024), BF16)]
MATRICES = [((C, 3 * C), F32), ((C, C), F32)]


def backward_first(scale, x, weights, saved, pieces):
    return call(
        functools.partial(backward_first_kernel, scale),
        "backward_first",
        (x, *weights, *saved, *pieces),
        halves([TOKENS] + PARTS),
        GRADIENT_SCRATCH
        + [
            ((C, 2048), BF16), ((TOK, C), BF16), ((C, TOK), BF16), ((TOK, C), BF16),
            ((TOK, C), BF16), ((TOK, C), BF16), ((C, 2048), BF16),
            ((TOK, 2048), BF16), ((TOK, 2048), BF16), ((128, TOK), BF16),
            ((2048, 128), BF16), ((2048, 128), BF16),
        ]
        + MATRICES,
    )


def second_block(scale, y_pieces, c_pieces, weights):
    return call(
        functools.partial(second_kernel, scale),
        "second_block",
        (*y_pieces, *c_pieces, *weights),
        halves(piece_shapes() + PARTS),
        GRADIENT_SCRATCH
        + [
            ((C, 2048), BF16), ((TOK, C), BF16), ((C, 512), BF16), ((TOK, C), BF16),
            ((HEADS * VROWS, 512), BF16), ((TOK, C), BF16), ((C, 512), BF16),
            ((128, 2048), BF16), ((128, 512), BF16), ((128, 512), BF16),
            ((224 + VIRTUAL, 1024), BF16), ((168 + VIRTUAL, 1024), BF16),
            ((224, 1024), BF16), ((168, 1024), BF16),
            ((2048, 128), BF16), ((2048, 128), BF16),
            ((TOK, 256), F32), ((TOK, C), F32), ((TOK, C), F32),
        ]
        + MATRICES
        + [(shape, BF16) for shape in piece_shapes()[1:]],
        there=range(1, 5),
        copies=4,
        collective_id=2,
    )


def coordinates():
    tm, rows = lax.axis_index("tm"), lax.axis_index("rows")
    return {
        "x": tm // 4 % 2 * 2 + rows // 2,
        "y": tm % 4,
        "z": tm // 8,
        "core": rows % 2,
    }


def device_at(place):
    tm = place["z"] * 8 + place["x"] // 2 * 4 + place["y"]
    return (tm, place["x"] % 2 * 2 + place["core"])


def beside(here, axis, steps):
    return device_at({**here, axis: (here[axis] + steps) % (2 if axis == "core" else 4)})


ORDERS = ("xyz", "yzx", "zxy")


def reduce_kernel(jobs, *refs):
    matrices = 2 * jobs // 3
    parts, outs, refs = refs[:jobs], refs[jobs : jobs + matrices], refs[jobs + matrices :]
    scratch = refs[: 5 * jobs]
    held = [scratch[5 * i : 5 * i + 2] for i in range(jobs)]
    slots = [scratch[5 * i + 2 : 5 * i + 5] for i in range(jobs)]
    send_sem, recv_sem, local_sem = refs[5 * jobs :]
    here = coordinates()
    partners = [beside(here, "core", 1)] + [
        beside(here, axis, steps) for axis in "xyz" for steps in (1, 2, 3)
    ]
    barrier = pltpu.get_barrier_semaphore()
    for partner in partners:
        pl.semaphore_signal(barrier, inc=1, device_id=partner, device_id_type=MESH)

    local = []
    for i in range(jobs):
        copy = pltpu.make_async_copy(parts[i].at[here["core"]], held[i][0], local_sem.at[i])
        copy.start()
        local.append(copy)
    pl.semaphore_wait(barrier, len(partners))

    flying = []
    for i in range(jobs):
        copy = pltpu.make_async_remote_copy(
            src_ref=parts[i].at[1 - here["core"]],
            dst_ref=held[i][1],
            send_sem=send_sem.at[i, 0],
            recv_sem=recv_sem.at[i, 0],
            device_id=partners[0],
            device_id_type=MESH,
        )
        copy.start()
        flying.append([copy])

    sent = list(flying)
    sums = [None] * jobs
    for stage in range(4):
        for i in range(jobs):
            order = ORDERS[i % 3]
            for copy in flying[i]:
                copy.wait_recv()
            if stage == 0:
                local[i].wait()
                for a in range(4):
                    total = held[i][0][a].astype(F32) + held[i][1][a].astype(F32)
                    held[i][0][a] = total.astype(BF16)
                source = held[i][0]
            else:
                total = sums[i]
                for slot in range(3):
                    total = total + slots[i][stage - 1][slot].astype(F32)
                if stage == 3:
                    gqkv, gout = outs[i // 3 * 2 : i // 3 * 2 + 2]
                    if i % 3 == 2:
                        gqkv[:, 1280:1536] = total[:, 0:256]
                        gout[...] = total[:, 256:768]
                    else:
                        gqkv[:, 640 * (i % 3) : 640 * (i % 3 + 1)] = total
                    continue
                source = slots[i][stage - 1].at[3]
                source[...] = total.astype(BF16)
            axis = order[stage]
            copies = []
            for steps in (1, 2, 3):
                copy = pltpu.make_async_remote_copy(
                    src_ref=source.at[(here[axis] + steps) % 4],
                    dst_ref=slots[i][stage].at[steps - 1],
                    send_sem=send_sem.at[i, 3 * stage + steps],
                    recv_sem=recv_sem.at[i, 3 * stage + steps],
                    device_id=beside(here, axis, steps),
                    device_id_type=MESH,
                )
                copy.start()
                copies.append(copy)
            sums[i] = source[here[axis]].astype(F32)
            flying[i] = copies
            sent.append(copies)
    for copies in sent:
        for copy in copies:
            copy.wait_send()


def reduced(parts):
    jobs = len(parts)
    scratch = []
    for part in parts:
        width = part.shape[-1]
        scratch += [
            pltpu.VMEM((4, 4, 4, 4, width), BF16),
            pltpu.VMEM((4, 4, 4, 4, width), BF16),
            pltpu.VMEM((4, 4, 4, 4, width), BF16),
            pltpu.VMEM((4, 4, 4, width), BF16),
            pltpu.VMEM((4, 4, width), BF16),
        ]
    return pl.pallas_call(
        functools.partial(reduce_kernel, jobs),
        in_specs=[pl.BlockSpec(memory_space=pl.ANY)] * jobs,
        out_specs=[pl.BlockSpec(memory_space=pltpu.VMEM)] * (2 * jobs // 3),
        out_shape=[
            jax.ShapeDtypeStruct((4, width), F32) for _ in range(jobs // 3) for width in (3 * C, C)
        ],
        scratch_shapes=scratch
        + [
            pltpu.SemaphoreType.DMA((jobs, 10)),
            pltpu.SemaphoreType.DMA((jobs, 10)),
            pltpu.SemaphoreType.DMA((jobs,)),
        ],
        compiler_params=pltpu.CompilerParams(
            collective_id=0, has_side_effects=True, vmem_limit_bytes=VMEM_LIMIT
        ),
        name="reduce_gradients",
    )(*parts)


def per_device(
    video_clip, cotangent,
    gain_first, bias_first, qkv_first, out_first,
    gain_second, bias_second, qkv_second, out_second,
):
    frames, rows_here, columns, channels = video_clip.shape
    devices = lax.axis_size("tm") * lax.axis_size("rows")
    scale = 1.0 / math.sqrt(frames * rows_here * columns * devices)
    x = video_clip.transpose(1, 2, 0, 3)
    cot = cotangent.transpose(1, 2, 0, 3)
    first = (gain_first.reshape(1, C), bias_first.reshape(1, C), qkv_first, out_first)
    second = (gain_second.reshape(1, C), bias_second.reshape(1, C), qkv_second, out_second)
    saved, y_pieces, c_pieces = forward_first(x, cot, first)
    *d_pieces, part0, part1, part2 = second_block(scale, y_pieces, c_pieces, second)
    grad, *parts = backward_first(scale, x, first, saved, d_pieces)
    sums = reduced([*parts, part0, part1, part2])
    return (grad.transpose(2, 0, 1, 3), *sums)


def solution(mesh):
    clip = P("tm", "rows", None, None)
    scattered = P(("tm", "rows"), None)
    return jax.shard_map(
        per_device,
        mesh=mesh,
        in_specs=(clip, clip) + (P(),) * 8,
        out_specs=(clip,) + (scattered,) * 4,
        check_vma=False,
    )
```

time: 524 us -> 138 us (0.26); the launches traced: 514 us -> 138 us
  matrix products: 172 us -> 0 us
  waiting for transfers between devices: 147 us -> 0 us
  Pallas kernels: 0 us -> 132 us
  other arithmetic: 82.8 us -> 0 us
  local copies, waits for them, and re-layouts: 85.2 us -> 5.28 us
  between operations: 15.4 us -> 0.66 us
  starting transfers between devices: 11 us -> 0 us
    dot_general x21 -> x0, matrix products: 143 us -> none  [the longest x4 66.9 us: attend(): jnp.einsum('nqhd,nkhd->nhqk', query_rows, key_rows) * head_size ** (-0.5)]
    pallas_call x0 -> x4, Pallas kernels: none -> 132 us  [the longest x3 103 us: call(): pl.pallas_call(kernel, in_specs=[IN_VMEM] * len(args), out_specs=[ANYWHER...]
    unnamed x2 -> x0, waiting for transfers between devices: 130 us -> none
    convert_element_type x8 -> x0, other arithmetic: 44.7 us -> none  [the longest x2 32.4 us: attend(): jax.nn.softmax(scores, axis=-1).astype(jnp.bfloat16)]
    convert_element_type x15 -> x0, local copies, waits for them, and re-layouts: 32.4 us -> none  [the longest x6 17.6 us: forward_block(): input_float = windows_in.astype(jnp.float32)]
    sub x2 -> x0, matrix products: 29.4 us -> none  [attend(): jax.nn.softmax(scores, axis=-1).astype(jnp.bfloat16)]
    reduce_sum x9 -> x0, other arithmetic: 28.2 us -> none  [the longest x1 14.2 us: attend(): jax.nn.softmax(scores, axis=-1).astype(jnp.bfloat16)]
    optimization_barrier x4 -> x0, local copies, waits for them, and re-layouts: 18.5 us -> none  [attend(): packed = lax.optimization_barrier(projected.astype(jnp.bfloat16))]
  transfers between devices with their start and end apart: 7 -> 0, of which waited for: 3 -> 0; matrix products, arithmetic and copies ran while one was open for 17% -> 0% of each run, Pallas kernels for 0% -> 0%
where the time goes in v4:
time: 138 us
  Pallas kernels  132 us (96%)
  local copies, waits for them, and re-layouts  5.28 us (4%)
    pallas_call x3, Pallas kernels, call(): pl.pallas_call(kernel, in_specs=[IN_VMEM] * len(args), out_specs=[ANYWHER...  103 us
    pallas_call x1, Pallas kernels, reduced(): pl.pallas_call(functools.partial(reduce_kernel, jobs), in_specs=[pl.Block...  28.7 us
    unnamed x4, local copies, waits for them, and re-layouts  5.28 us

profile of v4, /device:TPU:0, one launch (start us, length us, event | category | flops | bytes accessed | tf_op | source)
XLA Modules:
  0.0 138.1 jit_solution(3520076422340664162)
XLA Ops:
  0.6 32.9 %forward_first.1 = (bf16[2,512,512]{2,1,0:T(8,128)(2,1)}, f32[2,4,1,2048]{3,2,1,0:T(1,128)}, bf16[11,7,4,512]{3,2,1,0:T(4,128)(2,1)}, bf16[11,7,4,512]{3,2,1,0:T...) custom-call(bf16[14,7,8,512]{3,2,1,0:T(8,128)(2,1)} %bitcast.7, ...), custom_call_target="tpu_custom_call" | custom-call | tf_op jit(solution)/shard_map/forward_first/pallas_call | solution.py:476
  33.5 37.6 %second_block.1 = (bf16[11,7,4,512]{3,2,1,0:T(4,128)(2,1)}, bf16[7,7,4,512]{3,2,1,0:T(4,128)(2,1)}, bf16[4,7,4,512]{3,2,1,0:T(4,128)(2,1)}, bf16[3,7,4,512]{3,2,...) custom-call(bf16[11,7,4,512]{3,2,1,0:T(4,128)(2,1)} %get-tuple-eleme, ...), custom_call_target="tpu_custom_call" | custom-call | tf_op jit(solution)/shard_map/second_block/pallas_call | solution.py:476
  71.1 33.0 %backward_first.1 = (bf16[14,7,8,512]{3,2,1,0:T(8,128)(2,1)}, bf16[2,4,4,4,4,640]{5,4,3,2,1,0:T(4,128)(2,1)}, bf16[2,4,4,4,4,640]{5,4,3,2,1,0:T(4,128)(2,1)}, bf16[2,4,4,4,4,768]{5,4,3,2,1,0:T(4,128)(2,1)}) custom-call(bf16[14,7,8,512]{3,2,1,0:T(8,128)(2,1)} %bitcast.8, f32[1,512]{1,0:T(1,128)} %bitcast.11, f32[1,512]{1,0:T(1,128)} %bitcast.13, ...), custom_call_target="tpu_custom_call" | custom-call | tf_op jit(solution)/shard_map/backward_first/pallas_call | solution.py:476
  104.1 28.7 %reduce_gradients.1 = (f32[4,1536]{1,0:T(4,128)}, f32[4,512]{1,0:T(4,128)}, f32[4,1536]{1,0:T(4,128)}, f32[4,512]{1,0:T(4,128)}) custom-call(bf16[2,4,4,4,4,640]{5,4,3,2,1,0:T(4,128)(2,1)} %get-tuple-element.51.refs_0_, bf16[2,4,4,4,4,640]{5,4,3,2,1,0:T(4,128)(2,1)} %get-tuple-element.52.refs_1_, bf16[2,4,4,4,4,768]{5,4,3,2,1,0:T(4,128)(2,1)} %get-tuple-element.53.refs_2_, ...), custom_call_target="tpu_custom_call" | custom-call | tf_op jit(solution)/shard_map/reduce_gradients/pallas_call | solution.py:673
  132.8 1.3 copy.19
  134.2 1.3 copy.20
  135.5 1.3 copy.21
  136.8 1.3 copy.22

commit v5 on v4

--- a/solution.py
+++ b/solution.py
@@ -188,22 +188,40 @@
     exchange.wait()
 
 
-def write_parts(gqkv, gout, parts):
+def write_part(g, block, part):
+    turn = g % 3
+
     def layer(z, carry):
         for xy in range(16):
             x, y = xy // 4, xy % 4
             rows = pl.ds(pl.multiple_of((z * 16 + x // 2 * 8 + y * 2 + x % 2) * 8, 8), 8)
-            blocks = (
-                gqkv[rows, 0:640],
-                gqkv[rows, 640:1280],
-                jnp.concatenate([gqkv[rows, 1280:1536], gout[rows, :]], axis=1),
-            )
-            for part, block, place in zip(parts, blocks, ((x, y, z), (y, z, x), (z, x, y))):
-                part[(0,) + place] = block[0:4].astype(BF16)
-                part[(1,) + place] = block[4:8].astype(BF16)
+            values = block[rows, :]
+            first = jnp.where(turn == 0, x, jnp.where(turn == 1, y, z))
+            second = jnp.where(turn == 0, y, jnp.where(turn == 1, z, x))
+            third = jnp.where(turn == 0, z, jnp.where(turn == 1, x, y))
+            part[0, first, second, third] = values[0:4].astype(BF16)
+            part[1, first, second, third] = values[4:8].astype(BF16)
         return carry
 
     lax.fori_loop(0, 4, layer, 0)
+
+
+def group_gradients(scale, g, normed_t, dproj, mixt, cot_b, block, part):
+    block[:, 0:384] = mm(normed_t[...], dproj[:, columns_of(g)]) * scale
+    block[:, 384:512] = mm(mixt[...], cot_b[:, channels_of(g)]) * scale
+    write_part(g, block, part)
+
+
+def columns_of(g):
+    return pl.ds(pl.multiple_of(g * 384, 128), 384)
+
+
+def sort_columns(sorted_ref, wqkv_ref):
+    for g in range(HEADS // GROUP):
+        for i in range(3):
+            sorted_ref[:, 384 * g + 128 * i : 384 * g + 128 * (i + 1)] = wqkv_ref[
+                :, C * i + 128 * g : C * i + 128 * (g + 1)
+            ]
 
 
 def norm_backward(dnormed, xhat, rstd, gain):
@@ -215,100 +233,251 @@
     )
 
 
-def finish_gradients(scale, normed, dproj, mixt, cot_b, gqkv_s, gout_s, part_refs):
-    gout_s[...] = mm(mixt[...], cot_b[...]) * scale
-    gqkv_s[...] = mm_tn(normed[...], dproj[...]) * scale
-    write_parts(gqkv_s, gout_s, part_refs)
+def coordinates():
+    tm, rows = lax.axis_index("tm"), lax.axis_index("rows")
+    return {
+        "x": tm // 4 % 2 * 2 + rows // 2,
+        "y": tm % 4,
+        "z": tm // 8,
+        "core": rows % 2,
+    }
+
+
+def device_at(place):
+    tm = place["z"] * 8 + place["x"] // 2 * 4 + place["y"]
+    return (tm, place["x"] % 2 * 2 + place["core"])
+
+
+def beside(here, axis, steps):
+    return device_at({**here, axis: (here[axis] + steps) % (2 if axis == "core" else 4)})
+
+
+ORDERS = ("xyz", "yzx", "zxy")
+
+
+class Reduction:
+    def __init__(self, order, here, partners, part, local_sem, buffers, sems):
+        self.order, self.here, self.partners, self.part = order, here, partners, part
+        self.held, self.other, *self.slots = buffers
+        self.local_sem, self.sems = local_sem, sems
+
+    def remote(self, number, source, target, partner):
+        return pltpu.make_async_remote_copy(
+            src_ref=source,
+            dst_ref=target,
+            send_sem=self.sems[0].at[number],
+            recv_sem=self.sems[1].at[number],
+            device_id=partner,
+            device_id_type=MESH,
+        )
+
+    def local_copy(self):
+        return pltpu.make_async_copy(self.part.at[self.here["core"]], self.held, self.local_sem)
+
+    def core_copy(self):
+        return self.remote(0, self.part.at[1 - self.here["core"]], self.other, self.partners["core", 1])
+
+    def source(self, step):
+        return self.held if step == 0 else self.slots[step - 1].at[3]
+
+    def axis_copies(self, step):
+        axis = self.order[step]
+        return [
+            self.remote(
+                3 * step + away,
+                self.source(step).at[(self.here[axis] + away) % 4],
+                self.slots[step].at[away - 1],
+                self.partners[axis, away],
+            )
+            for away in (1, 2, 3)
+        ]
+
+    def start(self):
+        self.core_copy().start()
+
+    def advance(self, stage, out=None):
+        if stage == 0:
+            self.core_copy().wait_recv()
+            if self.local_sem is not None:
+                self.local_copy().wait()
+                own = self.held
+            else:
+                own = self.part.at[self.here["core"]]
+            for i in range(4):
+                self.held[i] = (own[i].astype(F32) + self.other[i].astype(F32)).astype(BF16)
+        else:
+            for copy in self.axis_copies(stage - 1):
+                copy.wait_recv()
+            total = self.source(stage - 1)[self.here[self.order[stage - 1]]].astype(F32)
+            for slot in range(3):
+                total = total + self.slots[stage - 1][slot].astype(F32)
+            if stage == 3:
+                out(total)
+                return
+            self.slots[stage - 1][3] = total.astype(BF16)
+        for copy in self.axis_copies(stage):
+            copy.start()
+
+    def finish(self):
+        self.core_copy().wait_send()
+        for step in range(3):
+            for copy in self.axis_copies(step):
+                copy.wait_send()
+
+
+JOBS = HEADS // GROUP
 
 
 def backward_first_kernel(
     scale,
     x_ref, gain_ref, bias_ref, wqkv_ref, wout_ref, mixt_ref, stat_ref,
-    own, ahead, behind, above, corner,
-    grad_ref, part0_ref, part1_ref, part2_ref,
-    normed_s, dproj, cot_b, mixt_all, qbd, k, kt, v, qn, don, dobd, p_s, ds_s, dqt, do_rows, q_rows, gqkv_s, gout_s,
+    own, ahead, behind, above, corner, parts_second,
+    grad_ref, gqkv1, gout1, gqkv2, gout2,
+    normed_t, dproj, cot_b, mixt_all, wsorted, block, parts_first,
+    qbd, k, kt, v, qn, don, dobd, p_s, ds_s, dqt, do_rows, q_rows, cot_s, xhat_s, rstd_s,
+    held, other, slots_a, slots_b, slots_c, local_sem, send_sem, recv_sem,
 ):
-    for ref in (qbd, dobd, do_rows, q_rows, normed_s, dproj, cot_b):
+    here = coordinates()
+    partners = {("core", 1): beside(here, "core", 1)}
+    for axis in "xyz":
+        for away in (1, 2, 3):
+            partners[axis, away] = beside(here, axis, away)
+    barrier = pltpu.get_barrier_semaphore()
+    for partner in partners.values():
+        pl.semaphore_signal(barrier, inc=1, device_id=partner, device_id_type=MESH)
+
+    def job(i):
+        of_first = i < JOBS
+        g = i % JOBS
+        return Reduction(
+            ORDERS[g % 3],
+            here,
+            partners,
+            parts_first.at[g] if of_first else parts_second.at[g],
+            None if of_first else local_sem.at[g],
+            [ref.at[i] for ref in (held, other, slots_a, slots_b, slots_c)],
+            (send_sem.at[i], recv_sem.at[i]),
+        )
+
+    def result(i):
+        gqkv, gout = (gqkv1, gout1) if i < JOBS else (gqkv2, gout2)
+        g = i % JOBS
+
+        def out(total):
+            for part in range(3):
+                at = C * part + 128 * g
+                gqkv[:, at : at + 128] = total[:, 128 * part : 128 * (part + 1)]
+            gout[:, 128 * g : 128 * (g + 1)] = total[:, 384:512]
+
+        return out
+
+    first, second = [job(i) for i in range(JOBS)], [job(JOBS + i) for i in range(JOBS)]
+    for reduction in second:
+        reduction.local_copy().start()
+    for ref in (qbd, dobd, do_rows, q_rows, normed_t, dproj, cot_b):
         ref[...] = jnp.zeros_like(ref)
+    sort_columns(wsorted, wqkv_ref)
     for w in range(2):
-        base = ROWS * w
         xhat, rstd = standardized(tiles(x_ref[7 * w : 7 * w + 7]))
+        xhat_s[w] = xhat
+        rstd_s[w] = rstd
         normed = (xhat * gain_ref[...] + bias_ref[...]).astype(BF16)
-        normed_s[base : base + TOK] = normed
+        normed_t[:, 512 * w : 512 * w + TOK] = normed.T
         queries = (mm(normed, wqkv_ref[:, 0:C]) * QSCALE).astype(BF16)
-        qn[...] = queries
-        put_diagonal(qbd, queries.T, 512)
+        qn[w] = queries
+        put_diagonal(qbd.at[w], queries.T, 512)
         keys = mm(normed, wqkv_ref[:, C : 2 * C]).astype(BF16)
-        k[...] = keys
-        kt[...] = keys.T
-        v[...] = mm(normed, wqkv_ref[:, 2 * C :]).astype(BF16)
+        k[w] = keys
+        kt[w] = keys.T
+        v[w] = mm(normed, wqkv_ref[:, 2 * C :]).astype(BF16)
         if w == 0:
-            parts = [joined(above[...], corner[...]), joined(ahead[0:4], own[0:4])]
+            pieces = [joined(above[...], corner[...]), joined(ahead[0:4], own[0:4])]
         else:
-            parts = [joined(ahead[4:7], own[4:7]), joined(own[7:11], behind[...])]
-        cot = jnp.concatenate([part.reshape(-1, C) for part in parts], axis=0)
+            pieces = [joined(ahead[4:7], own[4:7]), joined(own[7:11], behind[...])]
+        cot = jnp.concatenate([piece.reshape(-1, C) for piece in pieces], axis=0)
+        cot_s[w] = cot
         cot_h = cot.astype(BF16)
         cot_b[512 * w : 512 * w + TOK] = cot_h
         dmixed = mm_nt(cot_h, wout_ref[...]).astype(BF16)
-        don[...] = dmixed
-        put_diagonal(dobd, dmixed.T, 512)
+        don[w] = dmixed
+        put_diagonal(dobd.at[w], dmixed.T, 512)
         mixt_all[:, 512 * w : 512 * (w + 1)] = mixt_ref[w]
-
-        def group(g, carry):
-            kg = k[:, channels_of(g)]
-            vg = v[:, channels_of(g)]
-            qg = qn[:, channels_of(g)]
-            dog = don[:, channels_of(g)]
+        if w == 0:
+            pl.semaphore_wait(barrier, len(partners))
+            for reduction in second:
+                reduction.start()
+
+    def group(g, carry):
+        for w in range(2):
+            kg = k[w, :, channels_of(g)]
+            vg = v[w, :, channels_of(g)]
+            qg = qn[w, :, channels_of(g)]
+            dog = don[w, :, channels_of(g)]
             for j in range(GROUP):
                 lanes = slice(512 * j, 512 * (j + 1))
                 do_rows[512 * j : 512 * j + TOK] = own_lanes(j, dog)
                 q_rows[512 * j : 512 * j + TOK] = own_lanes(j, qg)
-                scores = mm(kg, qbd[channels_of(g), lanes])
+                scores = mm(kg, qbd[w, channels_of(g), lanes])
                 p = jnp.exp2(scores - stat_ref[w, g, :, lanes]).astype(BF16)
                 p_s[:, lanes] = p
                 dsum = jnp.sum(
                     mixt_ref[w, head_channels(g, j), :].astype(F32)
-                    * dobd[head_channels(g, j), lanes].astype(F32),
+                    * dobd[w, head_channels(g, j), lanes].astype(F32),
                     axis=0, keepdims=True,
                 )
-                dp = mm(vg, dobd[channels_of(g), lanes]) - dsum
+                dp = mm(vg, dobd[w, channels_of(g), lanes]) - dsum
                 ds = (p.astype(F32) * dp).astype(BF16)
                 ds_s[:, lanes] = ds
-                dq = mm(kt[head_channels(g, j), :], ds)
+                dq = mm(kt[w, head_channels(g, j), :], ds)
                 dqt[HD * j : HD * (j + 1), :] = (dq[:, 0:TOK] * HD ** (-0.5)).astype(BF16)
             dk = mm(ds_s[...], q_rows[...]) * LN2
             dv = mm(p_s[...], do_rows[...])
-            rows = slice(base, base + TOK)
-            dproj[rows, channels_of(g)] = dqt[...].T
-            dproj[rows, channels_of(g, C)] = dk.astype(BF16)
-            dproj[rows, channels_of(g, 2 * C)] = dv.astype(BF16)
-            return carry
-
-        lax.fori_loop(0, HEADS // GROUP, group, 0)
-        dnormed = mm_nt(dproj[base : base + TOK], wqkv_ref[...])
-        total = cot + norm_backward(dnormed, xhat, rstd, gain_ref[...])
+            dproj[512 * w : 512 * w + TOK, columns_of(g)] = jnp.concatenate(
+                [dqt[...].T, dk.astype(BF16), dv.astype(BF16)], axis=1
+            )
+        group_gradients(scale, g, normed_t, dproj, mixt_all, cot_b, block, parts_first.at[g])
+        for now in range(JOBS):
+
+            @pl.when(g == now)
+            def _():
+                first[now].start()
+                for i in range(JOBS):
+                    second[i].advance(now, result(JOBS + i))
+                for i in range(now):
+                    first[i].advance(now - 1 - i)
+
+        return carry
+
+    lax.fori_loop(0, JOBS, group, 0)
+    for w in range(2):
+        dnormed = mm_nt(dproj[512 * w : 512 * w + TOK], wsorted[...])
+        total = cot_s[w] + norm_backward(dnormed, xhat_s[w], rstd_s[w], gain_ref[...])
         grad_ref[7 * w : 7 * w + 7] = total.reshape(7, 7, 8, C).astype(BF16)
-    finish_gradients(
-        scale, normed_s, dproj, mixt_all, cot_b, gqkv_s, gout_s, (part0_ref, part1_ref, part2_ref)
-    )
+    for now in range(JOBS, 2 * JOBS):
+        for i in range(JOBS):
+            if 0 <= now - 1 - i <= 3:
+                first[i].advance(now - 1 - i, result(i))
+    for reduction in first + second:
+        reduction.finish()
 
 
 def second_kernel(
     scale,
     y_own, y_ahead, y_behind, y_above, y_corner, c_own, c_ahead, c_behind, c_above, c_corner,
     gain_ref, bias_ref, wqkv_ref, wout_ref,
-    own, ahead_there, behind_there, above_there, corner_there, part0_ref, part1_ref, part2_ref,
-    normed_s, dproj, cot_b, mixt, qbd, k, kt, v, vt, qn, dot_s, dobd, dopt, dqt,
-    e_a, e_b, ds_a, ds_b, do_rows, q_rows, pen, cot_s, xhat_s, gqkv_s, gout_s,
+    own, ahead_there, behind_there, above_there, corner_there, parts,
+    normed_t, dproj, cot_b, mixt, wsorted, block, qbd, k, kt, v, vt, qn, dot_s, dobd, dopt, dqt,
+    e_a, e_b, ds_a, ds_b, do_rows, q_rows, pen, cot_s, xhat_s,
     ahead, behind, above, corner, send_sem, recv_sem,
 ):
     exchange = Exchange(-1, send_sem, recv_sem)
     exchange.greet()
     e_s, ds_s = (e_a, e_b), (ds_a, ds_b)
-    for ref in (qbd, dobd, do_rows, q_rows, normed_s, dproj, cot_b, mixt):
+    for ref in (qbd, dobd, do_rows, q_rows, normed_t, dproj, cot_b, mixt):
         ref[...] = jnp.zeros_like(ref)
+    sort_columns(wsorted, wqkv_ref)
     for w in range(2):
-        base = ROWS * w
+        base = 512 * w
         last_frames = lax.axis_index("tm") == (lax.axis_size("tm") - 1 if w == 0 else 0)
         last_rows = (lax.axis_index("rows") == lax.axis_size("rows") - 1) if w == 1 else False
 
@@ -334,7 +503,7 @@
         xhat, rstd = standardized(xhat_s[...])
         xhat_s[...] = xhat
         normed = (xhat * gain_ref[...] + bias_ref[...]).astype(BF16)
-        normed_s[base : base + TOK] = normed
+        normed_t[:, base : base + TOK] = normed.T
         queries = (mm(normed, wqkv_ref[:, 0:C]) * QSCALE).astype(BF16)
         qn[...] = queries
         keys = mm(normed, wqkv_ref[:, C : 2 * C]).astype(BF16)
@@ -423,13 +592,18 @@
             for s, (start, stop) in enumerate(SPLIT):
                 rows = slice(base + start, base + stop)
                 dk, dv = grads[s]
-                dproj[rows, channels_of(g)] = dqt[:, 256 * s : 256 * s + stop - start].T
-                dproj[rows, channels_of(g, C)] = dk.astype(BF16)
-                dproj[rows, channels_of(g, 2 * C)] = (dv + virtual_dv[1 - s]).astype(BF16)
+                dproj[rows, columns_of(g)] = jnp.concatenate(
+                    [
+                        dqt[:, 256 * s : 256 * s + stop - start].T,
+                        dk.astype(BF16),
+                        (dv + virtual_dv[1 - s]).astype(BF16),
+                    ],
+                    axis=1,
+                )
             return carry
 
         lax.fori_loop(0, HEADS // GROUP, group, 0)
-        dnormed = mm_nt(dproj[base : base + TOK], wqkv_ref[...])
+        dnormed = mm_nt(dproj[base : base + TOK], wsorted[...])
         total = cot_s[...] + norm_backward(dnormed, xhat_s[...], rstd, gain_ref[...])
         whole = jnp.concatenate(
             [total[224:392].reshape(7, 3, 8, C), total[0:224].reshape(7, 4, 8, C)], axis=1
@@ -448,9 +622,12 @@
             exchange.send(1, behind, behind_there)
             exchange.send(2, above, above_there)
             exchange.send(3, corner, corner_there)
-    finish_gradients(
-        scale, normed_s, dproj, mixt, cot_b, gqkv_s, gout_s, (part0_ref, part1_ref, part2_ref)
-    )
+
+    def gradients(g, carry):
+        group_gradients(scale, g, normed_t, dproj, mixt, cot_b, block, parts.at[g])
+        return carry
+
+    lax.fori_loop(0, JOBS, gradients, 0)
     exchange.wait()
 
 
@@ -458,8 +635,7 @@
     return [(rows, 7, 4, C) for rows in (11, 7, 4, 3, 3)]
 
 
-WIDTHS = (640, 640, 768)
-PARTS = [(2, 4, 4, 4, 4, width) for width in WIDTHS]
+PARTS = [(JOBS, 2, 4, 4, 4, 4, 512)]
 SAVED = [
     jax.ShapeDtypeStruct((2, C, 512), BF16),
     jax.ShapeDtypeStruct((2, HEADS // GROUP, 1, 2048), F32),
@@ -471,17 +647,19 @@
 ANYWHERE = pl.BlockSpec(memory_space=pl.ANY)
 
 
-def call(kernel, name, args, out_shape, scratch, there=(), copies=0, collective_id=None):
-    semaphores = [pltpu.SemaphoreType.DMA((copies,))] * 2 if copies else []
+def call(
+    kernel, name, args, out_shape, scratch, there=(), far=(), semaphores=(), collective_id=None
+):
     return pl.pallas_call(
         kernel,
-        in_specs=[IN_VMEM] * len(args),
+        in_specs=[ANYWHERE if i in far else IN_VMEM for i in range(len(args))],
         out_specs=[ANYWHERE if i in there else IN_VMEM for i in range(len(out_shape))],
         out_shape=out_shape,
-        scratch_shapes=[pltpu.VMEM(shape, dtype) for shape, dtype in scratch] + semaphores,
+        scratch_shapes=[pltpu.VMEM(shape, dtype) for shape, dtype in scratch]
+        + [pltpu.SemaphoreType.DMA(shape) for shape in semaphores],
         compiler_params=pltpu.CompilerParams(
             vmem_limit_bytes=VMEM_LIMIT,
-            has_side_effects=bool(copies),
+            has_side_effects=collective_id is not None,
             collective_id=collective_id,
         ),
         name=name,
@@ -502,31 +680,62 @@
         [(shape, BF16) for shape in pieces[1:] * 2]
         + [((C, 2048), BF16), ((TOK, C), BF16), ((HEADS * VROWS, TOK), BF16)],
         there=range(4, 12),
-        copies=9,
+        semaphores=[(9,)] * 2,
         collective_id=1,
     )
     return outs[:2], [outs[2], *outs[4:8]], [outs[3], *outs[8:12]]
 
 
-GRADIENT_SCRATCH = [((2 * ROWS, C), BF16), ((2 * ROWS, 3 * C), BF16), ((1024, C), BF16), ((C, 1024), BF16)]
-MATRICES = [((C, 3 * C), F32), ((C, C), F32)]
-
-
-def backward_first(scale, x, weights, saved, pieces):
+GRADIENT_SCRATCH = [
+    ((C, 1024), BF16), ((1024, 3 * C), BF16), ((1024, C), BF16), ((C, 1024), BF16), ((C, 3 * C), BF16), ((C, C), F32),
+]
+
+
+def backward_first(scale, x, weights, saved, pieces, parts):
+    both = 2 * JOBS
+    args = (x, *weights, *saved, *pieces, parts)
     return call(
         functools.partial(backward_first_kernel, scale),
         "backward_first",
-        (x, *weights, *saved, *pieces),
-        halves([TOKENS] + PARTS),
+        args,
+        halves([TOKENS]) + [jax.ShapeDtypeStruct((4, width), F32) for width in (3 * C, C)] * 2,
         GRADIENT_SCRATCH
+        + [(PARTS[0], BF16)]
         + [
-            ((C, 2048), BF16), ((TOK, C), BF16), ((C, TOK), BF16), ((TOK, C), BF16),
-            ((TOK, C), BF16), ((TOK, C), BF16), ((C, 2048), BF16),
+            ((2, C, 2048), BF16), ((2, TOK, C), BF16), ((2, C, TOK), BF16), ((2, TOK, C), BF16),
+            ((2, TOK, C), BF16), ((2, TOK, C), BF16), ((2, C, 2048), BF16),
             ((TOK, 2048), BF16), ((TOK, 2048), BF16), ((128, TOK), BF16),
             ((2048, 128), BF16), ((2048, 128), BF16),
+            ((2, TOK, C), F32), ((2, TOK, C), F32), ((2, TOK, 1), F32),
         ]
-        + MATRICES,
+        + [((both, 4, 4, 4, 4, 512), BF16)] * 3
+        + [((both, 4, 4, 4, 512), BF16), ((both, 4, 4, 512), BF16)],
+        far=(len(args) - 1,),
+        semaphores=[(JOBS,), (both, 10), (both, 10)],
+        collective_id=3,
     )
+
+
+def hand_on_kernel(*refs):
+    grad, *sums = refs[:5]
+    grad_out, *sums_out = refs[5:10]
+    copy = pltpu.make_async_copy(grad, grad_out, refs[10])
+    copy.start()
+    for source, target in zip(sums, sums_out):
+        target[...] = source[...]
+    copy.wait()
+
+
+def handed_on(outs):
+    return pl.pallas_call(
+        hand_on_kernel,
+        in_specs=[ANYWHERE] + [IN_VMEM] * 4,
+        out_specs=[ANYWHERE] + [IN_VMEM] * 4,
+        out_shape=[jax.ShapeDtypeStruct(out.shape, out.dtype) for out in outs],
+        scratch_shapes=[pltpu.SemaphoreType.DMA],
+        compiler_params=pltpu.CompilerParams(vmem_limit_bytes=VMEM_LIMIT),
+        name="hand_on",
+    )(*outs)
 
 
 def second_block(scale, y_pieces, c_pieces, weights):
@@ -545,149 +754,11 @@
             ((2048, 128), BF16), ((2048, 128), BF16),
             ((TOK, 256), F32), ((TOK, C), F32), ((TOK, C), F32),
         ]
-        + MATRICES
         + [(shape, BF16) for shape in piece_shapes()[1:]],
         there=range(1, 5),
-        copies=4,
+        semaphores=[(4,)] * 2,
         collective_id=2,
     )
-
-
-def coordinates():
-    tm, rows = lax.axis_index("tm"), lax.axis_index("rows")
-    return {
-        "x": tm // 4 % 2 * 2 + rows // 2,
-        "y": tm % 4,
-        "z": tm // 8,
-        "core": rows % 2,
-    }
-
-
-def device_at(place):
-    tm = place["z"] * 8 + place["x"] // 2 * 4 + place["y"]
-    return (tm, place["x"] % 2 * 2 + place["core"])
-
-
-def beside(here, axis, steps):
-    return device_at({**here, axis: (here[axis] + steps) % (2 if axis == "core" else 4)})
-
-
-ORDERS = ("xyz", "yzx", "zxy")
-
-
-def reduce_kernel(jobs, *refs):
-    matrices = 2 * jobs // 3
-    parts, outs, refs = refs[:jobs], refs[jobs : jobs + matrices], refs[jobs + matrices :]
-    scratch = refs[: 5 * jobs]
-    held = [scratch[5 * i : 5 * i + 2] for i in range(jobs)]
-    slots = [scratch[5 * i + 2 : 5 * i + 5] for i in range(jobs)]
-    send_sem, recv_sem, local_sem = refs[5 * jobs :]
-    here = coordinates()
-    partners = [beside(here, "core", 1)] + [
-        beside(here, axis, steps) for axis in "xyz" for steps in (1, 2, 3)
-    ]
-    barrier = pltpu.get_barrier_semaphore()
-    for partner in partners:
-        pl.semaphore_signal(barrier, inc=1, device_id=partner, device_id_type=MESH)
-
-    local = []
-    for i in range(jobs):
-        copy = pltpu.make_async_copy(parts[i].at[here["core"]], held[i][0], local_sem.at[i])
-        copy.start()
-        local.append(copy)
-    pl.semaphore_wait(barrier, len(partners))
-
-    flying = []
-    for i in range(jobs):
-        copy = pltpu.make_async_remote_copy(
-            src_ref=parts[i].at[1 - here["core"]],
-            dst_ref=held[i][1],
-            send_sem=send_sem.at[i, 0],
-            recv_sem=recv_sem.at[i, 0],
-            device_id=partners[0],
-            device_id_type=MESH,
-        )
-        copy.start()
-        flying.append([copy])
-
-    sent = list(flying)
-    sums = [None] * jobs
-    for stage in range(4):
-        for i in range(jobs):
-            order = ORDERS[i % 3]
-            for copy in flying[i]:
-                copy.wait_recv()
-            if stage == 0:
-                local[i].wait()
-                for a in range(4):
-                    total = held[i][0][a].astype(F32) + held[i][1][a].astype(F32)
-                    held[i][0][a] = total.astype(BF16)
-                source = held[i][0]
-            else:
-                total = sums[i]
-                for slot in range(3):
-                    total = total + slots[i][stage - 1][slot].astype(F32)
-                if stage == 3:
-                    gqkv, gout = outs[i // 3 * 2 : i // 3 * 2 + 2]
-                    if i % 3 == 2:
-                        gqkv[:, 1280:1536] = total[:, 0:256]
-                        gout[...] = total[:, 256:768]
-                    else:
-                        gqkv[:, 640 * (i % 3) : 640 * (i % 3 + 1)] = total
-                    continue
-                source = slots[i][stage - 1].at[3]
-                source[...] = total.astype(BF16)
-            axis = order[stage]
-            copies = []
-            for steps in (1, 2, 3):
-                copy = pltpu.make_async_remote_copy(
-                    src_ref=source.at[(here[axis] + steps) % 4],
-                    dst_ref=slots[i][stage].at[steps - 1],
-                    send_sem=send_sem.at[i, 3 * stage + steps],
-                    recv_sem=recv_sem.at[i, 3 * stage + steps],
-                    device_id=beside(here, axis, steps),
-                    device_id_type=MESH,
-                )
-                copy.start()
-                copies.append(copy)
-            sums[i] = source[here[axis]].astype(F32)
-            flying[i] = copies
-            sent.append(copies)
-    for copies in sent:
-        for copy in copies:
-            copy.wait_send()
-
-
-def reduced(parts):
-    jobs = len(parts)
-    scratch = []
-    for part in parts:
-        width = part.shape[-1]
-        scratch += [
-            pltpu.VMEM((4, 4, 4, 4, width), BF16),
-            pltpu.VMEM((4, 4, 4, 4, width), BF16),
-            pltpu.VMEM((4, 4, 4, 4, width), BF16),
-            pltpu.VMEM((4, 4, 4, width), BF16),
-            pltpu.VMEM((4, 4, width), BF16),
-        ]
-    return pl.pallas_call(
-        functools.partial(reduce_kernel, jobs),
-        in_specs=[pl.BlockSpec(memory_space=pl.ANY)] * jobs,
-        out_specs=[pl.BlockSpec(memory_space=pltpu.VMEM)] * (2 * jobs // 3),
-        out_shape=[
-            jax.ShapeDtypeStruct((4, width), F32) for _ in range(jobs // 3) for width in (3 * C, C)
-        ],
-        scratch_shapes=scratch
-        + [
-            pltpu.SemaphoreType.DMA((jobs, 10)),
-            pltpu.SemaphoreType.DMA((jobs, 10)),
-            pltpu.SemaphoreType.DMA((jobs,)),
-        ],
-        compiler_params=pltpu.CompilerParams(
-            collective_id=0, has_side_effects=True, vmem_limit_bytes=VMEM_LIMIT
-        ),
-        name="reduce_gradients",
-    )(*parts)
 
 
 def per_device(
@@ -703,9 +774,8 @@
     first = (gain_first.reshape(1, C), bias_first.reshape(1, C), qkv_first, out_first)
     second = (gain_second.reshape(1, C), bias_second.reshape(1, C), qkv_second, out_second)
     saved, y_pieces, c_pieces = forward_first(x, cot, first)
-    *d_pieces, part0, part1, part2 = second_block(scale, y_pieces, c_pieces, second)
-    grad, *parts = backward_first(scale, x, first, saved, d_pieces)
-    sums = reduced([*parts, part0, part1, part2])
+    *d_pieces, parts = second_block(scale, y_pieces, c_pieces, second)
+    grad, *sums = handed_on(backward_first(scale, x, first, saved, d_pieces, parts))
     return (grad.transpose(2, 0, 1, 3), *sums)
 
 

time: 138 us -> 157 us (1.14)
  Pallas kernels: 132 us -> 156 us
  local copies, waits for them, and re-layouts: 5.28 us -> 0 us
    pallas_call x4, Pallas kernels: 132 us -> 156 us  [the longest x3 130 us: call(): pl.pallas_call(kernel, in_specs=[ANYWHERE if i in far else IN_VMEM for i...]
    unnamed x4 -> x0, local copies, waits for them, and re-layouts: 5.28 us -> none
where the time goes in v5:
time: 157 us
  Pallas kernels  156 us (99%)
    pallas_call x3, Pallas kernels, call(): pl.pallas_call(kernel, in_specs=[ANYWHERE if i in far else IN_VMEM for i...  130 us
    pallas_call x1, Pallas kernels, handed_on(): pl.pallas_call(hand_on_kernel, in_specs=[ANYWHERE] + [IN_VMEM] * 4, out_s...  26.8 us

profile of v5, /device:TPU:0, one launch (start us, length us, event | category | flops | bytes accessed | tf_op | source)
XLA Modules:
  0.0 157.2 jit_solution(1728617278769583960)
XLA Ops:
  0.6 32.9 %forward_first.1 = (bf16[2,512,512]{2,1,0:T(8,128)(2,1)}, f32[2,4,1,2048]{3,2,1,0:T(1,128)}, bf16[11,7,4,512]{3,2,1,0:T(4,128)(2,1)}, bf16[11,7,4,512]{3,2,1,0:T...) custom-call(bf16[14,7,8,512]{3,2,1,0:T(8,128)(2,1)} %bitcast.7, ...), custom_call_target="tpu_custom_call" | custom-call | tf_op jit(solution)/shard_map/forward_first/pallas_call | solution.py:653
  33.5 38.9 %second_block.1 = (bf16[11,7,4,512]{3,2,1,0:T(4,128)(2,1)}, bf16[7,7,4,512]{3,2,1,0:T(4,128)(2,1)}, bf16[4,7,4,512]{3,2,1,0:T(4,128)(2,1)}, bf16[3,7,4,512]{3,2,...) custom-call(bf16[11,7,4,512]{3,2,1,0:T(4,128)(2,1)} %get-tuple-element.35.y_own, ...), custom_call_target="tpu_custom_call" | custom-call | tf_op jit(solution)/shard_map/second_block/pallas_call | solution.py:653
  72.4 57.7 %backward_first.1 = (bf16[14,7,8,512]{3,2,1,0:T(8,128)(2,1)}, f32[4,1536]{1,0:T(4,128)}, f32[4,512]{1,0:T(4,128)}, f32[4,1536]{1,0:T(4,128)}, f32[4,512]{1,0:T(4,128)}) custom-call(bf16[14,7,8,512]{3,2,1,0:T(8,128)(2,1)} %bitcast.8, f32[1,512]{1,0:T(1,128)} %bitcast.11, f32[1,512]{1,0:T(1,128)} %bitcast.13, bf16[512,1536]{1,0:T(8,128)(2,1)} %wqkv_ref.5, ...), custom_call_target="tpu_custom_call" | custom-call | tf_op jit(solution)/shard_map/backward_first/pallas_call | solution.py:653
  130.2 26.8 %hand_on.1 = (bf16[14,7,8,512]{3,2,1,0:T(8,128)(2,1)}, f32[4,1536]{1,0:T(4,128)}, f32[4,512]{1,0:T(4,128)}, f32[4,1536]{1,0:T(4,128)}, f32[4,512]{1,0:T(4,128)}) custom-call(bf16[14,7,8,512]{3,2,1,0:T(8,128)(2,1)} %get-tuple-element.51.refs_0_, f32[4,1536]{1,0:T(4,128)} %get-tuple-element.52.refs_1_, f32[4,512]{1,0:T(4,128)} %get-tuple-element.53.refs_2_, ...), custom_call_target="tpu_custom_call" | custom-call | tf_op jit(solution)/shard_map/hand_on/pallas_call | solution.py:730

commit v6 on v5

--- a/solution.py
+++ b/solution.py
@@ -90,34 +90,42 @@
         here = lax.axis_index("tm"), lax.axis_index("rows")
         return tuple((i + sign * d + n) % n for i, d, n in zip(here, steps, size))
 
-    def greet(self):
-        for steps in ROUTES:
-            pl.semaphore_signal(
-                pltpu.get_barrier_semaphore(),
-                inc=1,
-                device_id=self.device(steps, -self.way),
-                device_id_type=MESH,
-            )
+    def greet(self, ways):
+        self.ways = ways
+        for way in ways:
+            for steps in ROUTES:
+                pl.semaphore_signal(
+                    pltpu.get_barrier_semaphore(),
+                    inc=1,
+                    device_id=self.device(steps, -way),
+                    device_id_type=MESH,
+                )
 
     def wait_for_others(self):
-        pl.semaphore_wait(pltpu.get_barrier_semaphore(), len(ROUTES))
-
-    def send(self, route, source, target):
+        pl.semaphore_wait(pltpu.get_barrier_semaphore(), len(self.ways) * len(ROUTES))
+
+    def send(self, route, source, target, way=None):
         i = len(self.copies)
         copy = pltpu.make_async_remote_copy(
             src_ref=source,
             dst_ref=target,
             send_sem=self.sems[0].at[i],
             recv_sem=self.sems[1].at[i],
-            device_id=self.device(ROUTES[route], self.way),
+            device_id=self.device(ROUTES[route], way or self.way),
             device_id_type=MESH,
         )
         copy.start()
         self.copies.append(copy)
 
-    def wait(self):
-        for copy in self.copies:
-            copy.wait()
+    def wait_for(self, numbers):
+        for i in numbers:
+            self.copies[i].wait_recv()
+
+    def wait(self, arrived=()):
+        for i, copy in enumerate(self.copies):
+            copy.wait_send()
+            if i not in arrived:
+                copy.wait_recv()
 
 
 def pieces_of(whole, w, pieces):
@@ -141,17 +149,16 @@
 def forward_kernel(
     x_ref, cot_ref, gain_ref, bias_ref, wqkv_ref, wout_ref, mixt_ref, stat_ref, *refs,
 ):
-    y_own, c_own, y_there, c_there, y_here, c_here = (
-        refs[0], refs[1], refs[2:6], refs[6:10], refs[10:14], refs[14:18]
+    y_own, y_there, c_own, c_ahead_there, c_later, y_here = (
+        refs[0], refs[1:5], refs[5], refs[6], refs[7:10], refs[10:14]
     )
-    qbd, k, vt, send_sem, recv_sem = refs[18:]
+    c_ahead, qbd, k, vt, send_sem, recv_sem = refs[14:]
     exchange = Exchange(1, send_sem, recv_sem)
-    exchange.greet()
+    exchange.greet((1,))
     for w in range(2):
-        pieces_of(cot_ref[7 * w : 7 * w + 7].astype(F32), w, (c_own, *c_here))
+        pieces_of(cot_ref[7 * w : 7 * w + 7].astype(F32), w, (c_own, c_ahead, *c_later))
     exchange.wait_for_others()
-    for route in range(4):
-        exchange.send(route, c_here[route], c_there[route])
+    exchange.send(0, c_ahead, c_ahead_there)
     qbd[...] = jnp.zeros_like(qbd)
     for w in range(2):
         rows = slice(7 * w, 7 * w + 7)
@@ -449,11 +456,12 @@
         return carry
 
     lax.fori_loop(0, JOBS, group, 0)
-    for w in range(2):
-        dnormed = mm_nt(dproj[512 * w : 512 * w + TOK], wsorted[...])
-        total = cot_s[w] + norm_backward(dnormed, xhat_s[w], rstd_s[w], gain_ref[...])
-        grad_ref[7 * w : 7 * w + 7] = total.reshape(7, 7, 8, C).astype(BF16)
     for now in range(JOBS, 2 * JOBS):
+        w = now - JOBS
+        if w < 2:
+            dnormed = mm_nt(dproj[512 * w : 512 * w + TOK], wsorted[...])
+            total = cot_s[w] + norm_backward(dnormed, xhat_s[w], rstd_s[w], gain_ref[...])
+            grad_ref[7 * w : 7 * w + 7] = total.reshape(7, 7, 8, C).astype(BF16)
         for i in range(JOBS):
             if 0 <= now - 1 - i <= 3:
                 first[i].advance(now - 1 - i, result(i))
@@ -463,15 +471,15 @@
 
 def second_kernel(
     scale,
-    y_own, y_ahead, y_behind, y_above, y_corner, c_own, c_ahead, c_behind, c_above, c_corner,
+    y_own, y_ahead, y_behind, y_above, y_corner, c_own, c_ahead, c_behind_here, c_above_here, c_corner_here,
     gain_ref, bias_ref, wqkv_ref, wout_ref,
     own, ahead_there, behind_there, above_there, corner_there, parts,
     normed_t, dproj, cot_b, mixt, wsorted, block, qbd, k, kt, v, vt, qn, dot_s, dobd, dopt, dqt,
     e_a, e_b, ds_a, ds_b, do_rows, q_rows, pen, cot_s, xhat_s,
-    ahead, behind, above, corner, send_sem, recv_sem,
+    ahead, behind, above, corner, c_behind, c_above, c_corner, send_sem, recv_sem,
 ):
     exchange = Exchange(-1, send_sem, recv_sem)
-    exchange.greet()
+    exchange.greet((1, -1))
     e_s, ds_s = (e_a, e_b), (ds_a, ds_b)
     for ref in (qbd, dobd, do_rows, q_rows, normed_t, dproj, cot_b, mixt):
         ref[...] = jnp.zeros_like(ref)
@@ -499,6 +507,8 @@
                 put(4, 3, joined(above[...], corner[...]))
 
         gather(xhat_s, y_own, y_ahead, y_behind, y_above, y_corner)
+        if w == 1:
+            exchange.wait_for((0, 1, 2))
         gather(cot_s, c_own, c_ahead, c_behind, c_above, c_corner)
         xhat, rstd = standardized(xhat_s[...])
         xhat_s[...] = xhat
@@ -535,6 +545,12 @@
             key = region_of(lax.broadcasted_iota(jnp.int32, shape, 0), s)
             query = region_of(lax.broadcasted_iota(jnp.int32, shape, 1), s)
             pen[start:stop] = jnp.where(key == query, 0.0, 1.0)
+
+        if w == 0:
+            exchange.wait_for_others()
+            exchange.send(1, c_behind_here, c_behind, 1)
+            exchange.send(2, c_above_here, c_above, 1)
+            exchange.send(3, c_corner_here, c_corner, 1)
 
         def group(g, carry):
             virtual_dv = []
@@ -612,7 +628,6 @@
         if w == 0:
             ahead[...] = low
             own[0:7] = high
-            exchange.wait_for_others()
             exchange.send(0, ahead, ahead_there)
         else:
             own[7:11] = low[0:4]
@@ -628,7 +643,7 @@
         return carry
 
     lax.fori_loop(0, JOBS, gradients, 0)
-    exchange.wait()
+    exchange.wait((0, 1, 2))
 
 
 def piece_shapes():
@@ -676,14 +691,14 @@
         forward_kernel,
         "forward_first",
         (x, cot, *weights),
-        SAVED + halves(pieces[:1] * 2 + pieces[1:] * 2),
-        [(shape, BF16) for shape in pieces[1:] * 2]
+        SAVED + halves(pieces * 2),
+        [(shape, BF16) for shape in pieces[1:] + pieces[1:2]]
         + [((C, 2048), BF16), ((TOK, C), BF16), ((HEADS * VROWS, TOK), BF16)],
-        there=range(4, 12),
-        semaphores=[(9,)] * 2,
+        there=(3, 4, 5, 6, 8),
+        semaphores=[(6,)] * 2,
         collective_id=1,
     )
-    return outs[:2], [outs[2], *outs[4:8]], [outs[3], *outs[8:12]]
+    return outs[:2], outs[2:7], outs[7:]
 
 
 GRADIENT_SCRATCH = [
@@ -717,25 +732,18 @@
 
 
 def hand_on_kernel(*refs):
-    grad, *sums = refs[:5]
-    grad_out, *sums_out = refs[5:10]
-    copy = pltpu.make_async_copy(grad, grad_out, refs[10])
-    copy.start()
-    for source, target in zip(sums, sums_out):
+    for source, target in zip(refs[:5], refs[5:]):
         target[...] = source[...]
-    copy.wait()
 
 
 def handed_on(outs):
-    return pl.pallas_call(
+    return call(
         hand_on_kernel,
-        in_specs=[ANYWHERE] + [IN_VMEM] * 4,
-        out_specs=[ANYWHERE] + [IN_VMEM] * 4,
-        out_shape=[jax.ShapeDtypeStruct(out.shape, out.dtype) for out in outs],
-        scratch_shapes=[pltpu.SemaphoreType.DMA],
-        compiler_params=pltpu.CompilerParams(vmem_limit_bytes=VMEM_LIMIT),
-        name="hand_on",
-    )(*outs)
+        "hand_on",
+        outs,
+        [jax.ShapeDtypeStruct(out.shape, out.dtype) for out in outs],
+        [],
+    )
 
 
 def second_block(scale, y_pieces, c_pieces, weights):
@@ -754,9 +762,9 @@
             ((2048, 128), BF16), ((2048, 128), BF16),
             ((TOK, 256), F32), ((TOK, C), F32), ((TOK, C), F32),
         ]
-        + [(shape, BF16) for shape in piece_shapes()[1:]],
+        + [(shape, BF16) for shape in piece_shapes()[1:] + piece_shapes()[2:]],
         there=range(1, 5),
-        semaphores=[(4,)] * 2,
+        semaphores=[(7,)] * 2,
         collective_id=2,
     )
 

time: 157 us -> 137 us (0.87)
  Pallas kernels: 156 us -> 136 us
    pallas_call x1 -> x0, Pallas kernels: 26.8 us -> none  [handed_on(): pl.pallas_call(hand_on_kernel, in_specs=[ANYWHERE] + [IN_VMEM] * 4, out_s...]
    pallas_call x3 -> x4, Pallas kernels: 130 us -> 136 us  [call(): pl.pallas_call(kernel, in_specs=[ANYWHERE if i in far else IN_VMEM for i...]
where the time goes in v6:
time: 137 us
  Pallas kernels  136 us (99%)
    pallas_call x4, Pallas kernels, call(): pl.pallas_call(kernel, in_specs=[ANYWHERE if i in far else IN_VMEM for i...  136 us

profile of v6, /device:TPU:0, one launch (start us, length us, event | category | flops | bytes accessed | tf_op | source)
XLA Modules:
  0.0 136.9 jit_solution(16391982274335344692)
XLA Ops:
  0.6 32.9 %forward_first.1 = (bf16[2,512,512]{2,1,0:T(8,128)(2,1)}, f32[2,4,1,2048]{3,2,1,0:T(1,128)}, bf16[11,7,4,512]{3,2,1,0:T(4,128)(2,1)}, bf16[7,7,4,512]{3,2,1,0:T(...) custom-call(bf16[14,7,8,512]{3,2,1,0:T(8,128)(2,1)} %bitcast.7, ...), custom_call_target="tpu_custom_call" | custom-call | tf_op jit(solution)/shard_map/forward_first/pallas_call | solution.py:668
  33.5 42.9 %second_block.1 = (bf16[11,7,4,512]{3,2,1,0:T(4,128)(2,1)}, bf16[7,7,4,512]{3,2,1,0:T(4,128)(2,1)}, bf16[4,7,4,512]{3,2,1,0:T(4,128)(2,1)}, bf16[3,7,4,512]{3,2,...) custom-call(bf16[11,7,4,512]{3,2,1,0:T(4,128)(2,1)} %get-tuple-element.35.y_own, ...), custom_call_target="tpu_custom_call" | custom-call | tf_op jit(solution)/shard_map/second_block/pallas_call | solution.py:668
  76.4 58.4 %backward_first.1 = (bf16[14,7,8,512]{3,2,1,0:T(8,128)(2,1)}, f32[4,1536]{1,0:T(4,128)}, f32[4,512]{1,0:T(4,128)}, f32[4,1536]{1,0:T(4,128)}, f32[4,512]{1,0:T(4,128)}) custom-call(bf16[14,7,8,512]{3,2,1,0:T(8,128)(2,1)} %bitcast.8, f32[1,512]{1,0:T(1,128)} %bitcast.11, f32[1,512]{1,0:T(1,128)} %bitcast.13, bf16[512,1536]{1,0:T(8,128)(2,1)} %wqkv_ref.5, ...), custom_call_target="tpu_custom_call" | custom-call | tf_op jit(solution)/shard_map/backward_first/pallas_call | solution.py:668
  134.8 2.1 %hand_on.1 = (bf16[14,7,8,512]{3,2,1,0:T(8,128)(2,1)}, f32[4,1536]{1,0:T(4,128)}, f32[4,512]{1,0:T(4,128)}, f32[4,1536]{1,0:T(4,128)}, f32[4,512]{1,0:T(4,128)}) custom-call(bf16[14,7,8,512]{3,2,1,0:T(8,128)(2,1)} %get-tuple-element.51.refs_0_, f32[4,1536]{1,0:T(4,128)} %get-tuple-element.52.refs_1_, f32[4,512]{1,0:T(4,128)} %get-tuple-element.53.refs_2_, ...), custom_call_target="tpu_custom_call" | custom-call | tf_op jit(solution)/shard_map/hand_on/pallas_call | solution.py:668

commit v7 on v6

--- a/solution.py
+++ b/solution.py
@@ -12,7 +12,6 @@
 C, HEADS, HD = 512, 16, 32
 TOK = 392
 GROUP = 4
-VROWS = 48
 LOG2E = math.log2(math.e)
 QSCALE = HD ** (-0.5) * LOG2E
 MASKED = -1000000000.0 * LOG2E
@@ -20,7 +19,7 @@
 SPLIT = ((0, 224), (224, 392))
 VIRTUAL = 16
 ROWS = 400
-VMEM_LIMIT = 56 * 1024 * 1024
+MIB = 1024 * 1024
 
 
 def mm(a, b):
@@ -56,25 +55,12 @@
         ref[HD * head : HD * (head + 1), at : at + turned.shape[1]] = turned[HD * head : HD * (head + 1)]
 
 
-def put_values(vt, turned, lane):
-    count = turned.shape[1]
-    for head in range(HEADS):
-        vt[VROWS * head : VROWS * head + HD, lane : lane + count] = turned[HD * head : HD * (head + 1)]
-        vt[VROWS * head + HD : VROWS * (head + 1), lane : lane + count] = jnp.ones(
-            (VROWS - HD, count), BF16
-        )
-
-
 def channels_of(g, first=0):
     return pl.ds(pl.multiple_of(g * 128 + first, 128), 128)
 
 
 def head_channels(g, j):
     return pl.ds(pl.multiple_of(g * 128 + j * HD, HD), HD)
-
-
-def head_values(g, j):
-    return pl.ds(pl.multiple_of(g * GROUP * VROWS + j * VROWS, 16), VROWS)
 
 
 MESH = pl.DeviceIdType.MESH
@@ -149,10 +135,9 @@
 def forward_kernel(
     x_ref, cot_ref, gain_ref, bias_ref, wqkv_ref, wout_ref, mixt_ref, stat_ref, *refs,
 ):
-    y_own, y_there, c_own, c_ahead_there, c_later, y_here = (
-        refs[0], refs[1:5], refs[5], refs[6], refs[7:10], refs[10:14]
-    )
-    c_ahead, qbd, k, vt, send_sem, recv_sem = refs[14:]
+    y_own, y_ahead_there, y_behind, y_above_there, y_corner_there = refs[0:5]
+    c_own, c_ahead_there, *c_later = refs[5:10]
+    y_ahead, y_above, y_corner, c_ahead, qbd, k, vt, send_sem, recv_sem = refs[10:]
     exchange = Exchange(1, send_sem, recv_sem)
     exchange.greet((1,))
     for w in range(2):
@@ -167,7 +152,7 @@
         normed = (xhat * gain_ref[...] + bias_ref[...]).astype(BF16)
         put_diagonal(qbd, (mm(normed, wqkv_ref[:, 0:C]) * QSCALE).astype(BF16).T, 512)
         k[...] = mm(normed, wqkv_ref[:, C : 2 * C]).astype(BF16)
-        put_values(vt, mm(normed, wqkv_ref[:, 2 * C :]).astype(BF16).T, 0)
+        vt[...] = mm(normed, wqkv_ref[:, 2 * C :]).astype(BF16).T
 
         def group(g, carry):
             kg = k[:, channels_of(g)]
@@ -175,23 +160,22 @@
                 lanes = slice(512 * j, 512 * (j + 1))
                 scores = mm(kg, qbd[channels_of(g), lanes])
                 top = jnp.max(scores, axis=0, keepdims=True)
-                e = jnp.exp2(scores - top).astype(BF16)
-                mixed = mm(vt[head_values(g, j), :], e)
-                sums = mixed[HD : HD + 1]
+                e = jnp.exp2(scores - top)
+                sums = jnp.sum(e, axis=0, keepdims=True)
+                mixed = mm(vt[head_channels(g, j), :], e.astype(BF16))
                 stat_ref[w, g, :, lanes] = top + jnp.log2(sums)
-                mixt_ref[w, head_channels(g, j), :] = (mixed[:HD] * (1.0 / sums)).astype(BF16)
+                mixt_ref[w, head_channels(g, j), :] = (mixed * (1.0 / sums)).astype(BF16)
             return carry
 
         lax.fori_loop(0, HEADS // GROUP, group, 0)
         y = x + mm_tn(mixt_ref[w, :, 0:TOK], wout_ref[...])
-        pieces_of(y.reshape(7, 7, 8, C), w, (y_own, *y_here))
+        pieces_of(y.reshape(7, 7, 8, C), w, (y_own, y_ahead, y_behind, y_above, y_corner))
         if w == 0:
-            exchange.send(2, y_here[2], y_there[2])
-            exchange.send(3, y_here[3], y_there[3])
-            exchange.send(0, y_here[0].at[0:4], y_there[0].at[0:4])
+            exchange.send(2, y_above, y_above_there)
+            exchange.send(3, y_corner, y_corner_there)
+            exchange.send(0, y_ahead.at[0:4], y_ahead_there.at[0:4])
         else:
-            exchange.send(0, y_here[0].at[4:7], y_there[0].at[4:7])
-            exchange.send(1, y_here[1], y_there[1])
+            exchange.send(0, y_ahead.at[4:7], y_ahead_there.at[4:7])
     exchange.wait()
 
 
@@ -422,11 +406,11 @@
             dog = don[w, :, channels_of(g)]
             for j in range(GROUP):
                 lanes = slice(512 * j, 512 * (j + 1))
-                do_rows[512 * j : 512 * j + TOK] = own_lanes(j, dog)
-                q_rows[512 * j : 512 * j + TOK] = own_lanes(j, qg)
+                do_rows[w, 512 * j : 512 * j + TOK] = own_lanes(j, dog)
+                q_rows[w, 512 * j : 512 * j + TOK] = own_lanes(j, qg)
                 scores = mm(kg, qbd[w, channels_of(g), lanes])
                 p = jnp.exp2(scores - stat_ref[w, g, :, lanes]).astype(BF16)
-                p_s[:, lanes] = p
+                p_s[w, :, lanes] = p
                 dsum = jnp.sum(
                     mixt_ref[w, head_channels(g, j), :].astype(F32)
                     * dobd[w, head_channels(g, j), lanes].astype(F32),
@@ -434,13 +418,13 @@
                 )
                 dp = mm(vg, dobd[w, channels_of(g), lanes]) - dsum
                 ds = (p.astype(F32) * dp).astype(BF16)
-                ds_s[:, lanes] = ds
+                ds_s[w, :, lanes] = ds
                 dq = mm(kt[w, head_channels(g, j), :], ds)
-                dqt[HD * j : HD * (j + 1), :] = (dq[:, 0:TOK] * HD ** (-0.5)).astype(BF16)
-            dk = mm(ds_s[...], q_rows[...]) * LN2
-            dv = mm(p_s[...], do_rows[...])
+                dqt[w, HD * j : HD * (j + 1), :] = (dq[:, 0:TOK] * HD ** (-0.5)).astype(BF16)
+            dk = mm(ds_s[w], q_rows[w]) * LN2
+            dv = mm(p_s[w], do_rows[w])
             dproj[512 * w : 512 * w + TOK, columns_of(g)] = jnp.concatenate(
-                [dqt[...].T, dk.astype(BF16), dv.astype(BF16)], axis=1
+                [dqt[w].T, dk.astype(BF16), dv.astype(BF16)], axis=1
             )
         group_gradients(scale, g, normed_t, dproj, mixt_all, cot_b, block, parts_first.at[g])
         for now in range(JOBS):
@@ -471,12 +455,12 @@
 
 def second_kernel(
     scale,
-    y_own, y_ahead, y_behind, y_above, y_corner, c_own, c_ahead, c_behind_here, c_above_here, c_corner_here,
+    y_own, y_ahead, y_behind_here, y_above, y_corner, c_own, c_ahead, c_behind_here, c_above_here, c_corner_here,
     gain_ref, bias_ref, wqkv_ref, wout_ref,
     own, ahead_there, behind_there, above_there, corner_there, parts,
     normed_t, dproj, cot_b, mixt, wsorted, block, qbd, k, kt, v, vt, qn, dot_s, dobd, dopt, dqt,
     e_a, e_b, ds_a, ds_b, do_rows, q_rows, pen, cot_s, xhat_s,
-    ahead, behind, above, corner, c_behind, c_above, c_corner, send_sem, recv_sem,
+    ahead, behind, above, corner, c_behind, c_above, c_corner, y_behind, send_sem, recv_sem,
 ):
     exchange = Exchange(-1, send_sem, recv_sem)
     exchange.greet((1, -1))
@@ -506,9 +490,9 @@
                 put(0, 4, joined(own[7:11], behind[...]))
                 put(4, 3, joined(above[...], corner[...]))
 
+        if w == 1:
+            exchange.wait_for((0, 1, 2, 3))
         gather(xhat_s, y_own, y_ahead, y_behind, y_above, y_corner)
-        if w == 1:
-            exchange.wait_for((0, 1, 2))
         gather(cot_s, c_own, c_ahead, c_behind, c_above, c_corner)
         xhat, rstd = standardized(xhat_s[...])
         xhat_s[...] = xhat
@@ -530,17 +514,12 @@
             kt[:, 256 * s : 256 * s + count] = keys[start:stop].T
             dot_s[:, 256 * s : 256 * s + count] = dmixed[start:stop].T
             turned = values[start:stop].T
-            put_values(vt, turned, 256 * s)
+            vt[:, 256 * s : 256 * s + count] = turned
             total = jnp.sum(turned.astype(F32), axis=1, keepdims=True)
             other = 1 - s
             lane = 256 * other + SPLIT[other][1] - SPLIT[other][0]
             first = lax.broadcasted_iota(jnp.int32, (C, VIRTUAL), 1) == 0
-            total = jnp.where(first, total, 0.0).astype(BF16)
-            number = jnp.where(first[0 : VROWS - HD], float(count), 0.0).astype(BF16)
-            for head in range(HEADS):
-                at = VROWS * head
-                vt[at : at + HD, lane : lane + VIRTUAL] = total[HD * head : HD * (head + 1)]
-                vt[at + HD : at + VROWS, lane : lane + VIRTUAL] = number
+            vt[:, lane : lane + VIRTUAL] = jnp.where(first, total, 0.0).astype(BF16)
             shape = (count, 256)
             key = region_of(lax.broadcasted_iota(jnp.int32, shape, 0), s)
             query = region_of(lax.broadcasted_iota(jnp.int32, shape, 1), s)
@@ -548,6 +527,7 @@
 
         if w == 0:
             exchange.wait_for_others()
+            exchange.send(1, y_behind_here, y_behind, 1)
             exchange.send(1, c_behind_here, c_behind, 1)
             exchange.send(2, c_above_here, c_above, 1)
             exchange.send(3, c_corner_here, c_corner, 1)
@@ -559,25 +539,25 @@
                 count = stop - start
                 kg = k[start:stop, channels_of(g)]
                 apart = pen[start:stop] > 0.5
-                sums_of = []
+                sums_of, invs = [], []
                 for j in range(GROUP):
                     lanes = slice(256 * j, 256 * (j + 1))
                     scores = mm(kg, qbd[channels_of(g), 1024 * s + 256 * j : 1024 * s + 256 * (j + 1)])
                     scores = jnp.where(apart, MASKED, scores)
                     top = jnp.maximum(jnp.max(scores, axis=0, keepdims=True), MASKED)
-                    e_s[s][0:count, lanes] = jnp.exp2(scores - top).astype(BF16)
+                    e = jnp.exp2(scores - top)
+                    e_s[s][0:count, lanes] = e.astype(BF16)
+                    rest = jnp.exp2(MASKED - top)
                     first = lax.broadcasted_iota(jnp.int32, (VIRTUAL, 256), 0) == 0
-                    e_s[s][count : count + VIRTUAL, lanes] = jnp.where(
-                        first, jnp.exp2(MASKED - top), 0.0
-                    ).astype(BF16)
+                    e_s[s][count : count + VIRTUAL, lanes] = jnp.where(first, rest, 0.0).astype(BF16)
+                    invs.append(1.0 / (jnp.sum(e, axis=0, keepdims=True) + (TOK - count) * rest))
                 for j in range(GROUP):
                     lanes = slice(256 * j, 256 * (j + 1))
                     tokens = slice(256 * s, 256 * (s + 1))
-                    mixed = mm(
-                        vt[head_values(g, j), 256 * s : 256 * s + count + VIRTUAL], e_s[s][:, lanes]
+                    inv = invs[j]
+                    mixed = inv * mm(
+                        vt[head_channels(g, j), 256 * s : 256 * s + count + VIRTUAL], e_s[s][:, lanes]
                     )
-                    inv = 1.0 / mixed[HD : HD + 1]
-                    mixed = mixed[:HD] * inv
                     mixt[head_channels(g, j), 512 * w + 256 * s : 512 * w + 256 * s + count] = mixed[
                         :, 0:count
                     ].astype(BF16)
@@ -643,7 +623,7 @@
         return carry
 
     lax.fori_loop(0, JOBS, gradients, 0)
-    exchange.wait((0, 1, 2))
+    exchange.wait((0, 1, 2, 3))
 
 
 def piece_shapes():
@@ -663,7 +643,7 @@
 
 
 def call(
-    kernel, name, args, out_shape, scratch, there=(), far=(), semaphores=(), collective_id=None
+    kernel, name, args, out_shape, scratch, vmem, there=(), far=(), semaphores=(), collective_id=None
 ):
     return pl.pallas_call(
         kernel,
@@ -673,7 +653,7 @@
         scratch_shapes=[pltpu.VMEM(shape, dtype) for shape, dtype in scratch]
         + [pltpu.SemaphoreType.DMA(shape) for shape in semaphores],
         compiler_params=pltpu.CompilerParams(
-            vmem_limit_bytes=VMEM_LIMIT,
+            vmem_limit_bytes=vmem * MIB,
             has_side_effects=collective_id is not None,
             collective_id=collective_id,
         ),
@@ -692,10 +672,11 @@
         "forward_first",
         (x, cot, *weights),
         SAVED + halves(pieces * 2),
-        [(shape, BF16) for shape in pieces[1:] + pieces[1:2]]
-        + [((C, 2048), BF16), ((TOK, C), BF16), ((HEADS * VROWS, TOK), BF16)],
-        there=(3, 4, 5, 6, 8),
-        semaphores=[(6,)] * 2,
+        [(shape, BF16) for shape in (pieces[1], *pieces[3:], pieces[1])]
+        + [((C, 2048), BF16), ((TOK, C), BF16), ((C, TOK), BF16)],
+        vmem=20,
+        there=(3, 5, 6, 8),
+        semaphores=[(5,)] * 2,
         collective_id=1,
     )
     return outs[:2], outs[2:7], outs[7:]
@@ -719,12 +700,13 @@
         + [
             ((2, C, 2048), BF16), ((2, TOK, C), BF16), ((2, C, TOK), BF16), ((2, TOK, C), BF16),
             ((2, TOK, C), BF16), ((2, TOK, C), BF16), ((2, C, 2048), BF16),
-            ((TOK, 2048), BF16), ((TOK, 2048), BF16), ((128, TOK), BF16),
-            ((2048, 128), BF16), ((2048, 128), BF16),
+            ((2, TOK, 2048), BF16), ((2, TOK, 2048), BF16), ((2, 128, TOK), BF16),
+            ((2, 2048, 128), BF16), ((2, 2048, 128), BF16),
             ((2, TOK, C), F32), ((2, TOK, C), F32), ((2, TOK, 1), F32),
         ]
         + [((both, 4, 4, 4, 4, 512), BF16)] * 3
         + [((both, 4, 4, 4, 512), BF16), ((both, 4, 4, 512), BF16)],
+        vmem=46,
         far=(len(args) - 1,),
         semaphores=[(JOBS,), (both, 10), (both, 10)],
         collective_id=3,
@@ -743,6 +725,7 @@
         outs,
         [jax.ShapeDtypeStruct(out.shape, out.dtype) for out in outs],
         [],
+        vmem=8,
     )
 
 
@@ -755,16 +738,17 @@
         GRADIENT_SCRATCH
         + [
             ((C, 2048), BF16), ((TOK, C), BF16), ((C, 512), BF16), ((TOK, C), BF16),
-            ((HEADS * VROWS, 512), BF16), ((TOK, C), BF16), ((C, 512), BF16),
+            ((C, 512), BF16), ((TOK, C), BF16), ((C, 512), BF16),
             ((128, 2048), BF16), ((128, 512), BF16), ((128, 512), BF16),
             ((224 + VIRTUAL, 1024), BF16), ((168 + VIRTUAL, 1024), BF16),
             ((224, 1024), BF16), ((168, 1024), BF16),
             ((2048, 128), BF16), ((2048, 128), BF16),
             ((TOK, 256), F32), ((TOK, C), F32), ((TOK, C), F32),
         ]
-        + [(shape, BF16) for shape in piece_shapes()[1:] + piece_shapes()[2:]],
+        + [(shape, BF16) for shape in piece_shapes()[1:] + piece_shapes()[2:] + piece_shapes()[2:3]],
+        vmem=28,
         there=range(1, 5),
-        semaphores=[(7,)] * 2,
+        semaphores=[(8,)] * 2,
         collective_id=2,
     )
 

time: 137 us -> 132 us (0.964)
  Pallas kernels: 136 us -> 125 us
  local copies, waits for them, and re-layouts: 0 us -> 6.13 us
    pallas_call x4, Pallas kernels: 136 us -> 125 us  [call(): pl.pallas_call(kernel, in_specs=[ANYWHERE if i in far else IN_VMEM for i...]
    unnamed x0 -> x30, local copies, waits for them, and re-layouts: none -> 6.13 us
where the time goes in v7:
time: 132 us
  Pallas kernels  125 us (95%)
  local copies, waits for them, and re-layouts  6.13 us (5%)
    pallas_call x4, Pallas kernels, call(): pl.pallas_call(kernel, in_specs=[ANYWHERE if i in far else IN_VMEM for i...  125 us
    unnamed x30, local copies, waits for them, and re-layouts  6.13 us

profile of v7, /device:TPU:0, one launch (start us, length us, event | category | flops | bytes accessed | tf_op | source)
XLA Modules:
  0.0 131.5 jit_solution(10691235221773285809)
XLA Ops:
  0.6 0.0 copy-start
  0.6 1.4 %copy-done = bf16[512,1536]{1,0:T(8,128)(2,1)S(1)} copy-done((bf16[512,1536]{1,0:T(8,128)(2,1)S(1)}, bf16[512,1536]{1,0:T(8,128)(2,1)}, u32[]{:S(2)}) %copy-start) | copy-done | bytes 1572888
  2.0 1.1 copy-done.2
  3.2 1.0 copy-done.4
  4.2 1.1 copy-done.7
  5.4 0.7 copy-done.9
  6.0 0.7 copy-done.11
  6.7 27.5 %forward_first.1 = (bf16[2,512,512]{2,1,0:T(8,128)(2,1)S(1)}, f32[2,4,1,2048]{3,2,1,0:T(1,128)S(1)}, bf16[11,7,4,512]{3,2,1,0:T(4,128)(2,1)S(1)}, bf16[7,7,4,512...) custom-call(bf16[14,7,8,512]{3,2,1,0:T(8,128)(2,1)S(1)} %bitcast.7, ...), custom_call_target="tpu_custom_call" | custom-call | tf_op jit(solution)/shard_map/forward_first/pallas_call | solution.py:648
  34.3 0.0 copy-done.6
  34.3 0.0 copy-done.8
  34.3 0.0 copy-done.13
  34.3 0.0 copy-start.1
  34.3 0.0 copy-start.3
  34.3 0.0 copy-start.5
  34.3 0.0 copy-start.10
  34.3 0.0 copy-start.12
  34.4 40.6 %second_block.1 = (bf16[11,7,4,512]{3,2,1,0:T(4,128)(2,1)S(1)}, bf16[7,7,4,512]{3,2,1,0:T(4,128)(2,1)S(1)}, bf16[4,7,4,512]{3,2,1,0:T(4,128)(2,1)S(1)}, bf16[3,7...) custom-call(bf16[11,7,4,512]{3,2,1,0:T(4,128)(2,1)S(1)} %get-tuple-ele, ...), custom_call_target="tpu_custom_call" | custom-call | tf_op jit(solution)/shard_map/second_block/pallas_call | solution.py:648
  75.0 0.0 copy-done.1
  75.0 0.0 copy-done.3
  75.0 0.0 copy-done.5
  75.0 0.0 copy-done.10
  75.0 0.0 copy-done.12
  75.1 55.5 %backward_first.1 = (bf16[14,7,8,512]{3,2,1,0:T(8,128)(2,1)S(1)}, f32[4,1536]{1,0:T(4,128)S(1)}, f32[4,512]{1,0:T(4,128)S(1)}, f32[4,1536]{1,0:T(4,128)S(1)}, f32[4,512]{1,0:T(4,128)S(1)}) custom-call(bf16[14,7,8,512]{3,2,1,0:T(8,128)(2,1)S(1)} %bitcast.8, f32[1,512]{1,0:T(1,128)S(1)} %bitcast.11, f32[1,512]{1,0:T(1,128)S(1)} %bitcast.13, ...), custom_call_target="tpu_custom_call" | custom-call | tf_op jit(solution)/shard_map/backward_first/pallas_call | solution.py:648
  130.6 1.0 hand_on.1
  (10 shorter events, 0.0 us)
Async XLA Ops:
  0.6 1.4 %copy-start = (bf16[512,1536]{1,0:T(8,128)(2,1)S(1)}, bf16[512,1536]{1,0:T(8,128)(2,1)}, u32[]{:S(2)}) copy-start(bf16[512,1536]{1,0:T(8,128)(2,1)} %wqkv_ref.5) | copy-start | bytes 4718596
  2.0 1.1 copy-start.2
  3.2 1.0 copy-start.4
  4.2 1.1 copy-start.7
  5.4 0.7 copy-start.9
  6.0 0.7 copy-start.11
  6.7 27.5 %copy-start.6 = (bf16[512,1536]{1,0:T(8,128)(2,1)S(1)}, bf16[512,1536]{1,0:T(8,128)(2,1)}, u32[]{:S(2)}) copy-start(bf16[512,1536]{1,0:T(8,128)(2,1)} %wqkv_ref.4) | copy-start | bytes 4718596
  6.7 27.5 %copy-start.8 = (bf16[512,512]{1,0:T(8,128)(2,1)S(1)}, bf16[512,512]{1,0:T(8,128)(2,1)}, u32[]{:S(2)}) copy-start(bf16[512,512]{1,0:T(8,128)(2,1)} %wout_ref.4) | copy-start | bytes 1572868
  6.7 27.5 %copy-start.13 = (f32[512]{0:T(512)S(1)}, f32[512]{0:T(512)}, u32[]{:S(2)}) copy-start(f32[512]{0:T(512)} %param.16) | copy-start | bytes 6148
  6.7 27.6 %copy-start.14 = (f32[512]{0:T(512)S(1)}, f32[512]{0:T(512)}, u32[]{:S(2)}) copy-start(f32[512]{0:T(512)} %param.17) | copy-start | bytes 6148
  34.3 40.7 %copy-start.1 = (bf16[512,1536]{1,0:T(8,128)(2,1)S(1)}, bf16[512,1536]{1,0:T(8,128)(2,1)}, u32[]{:S(2)}) copy-start(bf16[512,1536]{1,0:T(8,128)(2,1)} %wqkv_ref.5) | copy-start | bytes 4718596
  34.3 40.7 %copy-start.3 = (bf16[8,14,7,512]{3,0,2,1:T(8,128)(2,1)S(1)}, bf16[8,14,7,512]{3,0,2,1:T(8,128)(2,1)}, u32[]{:S(2)}) copy-start(bf16[8,14,7,512]{3,0,2,1:T(8,128)(2,1)} %param.10) | copy-start | bytes 2408452
  34.3 40.7 %copy-start.5 = (bf16[512,512]{1,0:T(8,128)(2,1)S(1)}, bf16[512,512]{1,0:T(8,128)(2,1)}, u32[]{:S(2)}) copy-start(bf16[512,512]{1,0:T(8,128)(2,1)} %wout_ref.5) | copy-start | bytes 1572868
  34.3 40.7 %copy-start.10 = (f32[512]{0:T(512)S(1)}, f32[512]{0:T(512)}, u32[]{:S(2)}) copy-start(f32[512]{0:T(512)} %param.12) | copy-start | bytes 6148
  34.3 40.7 %copy-start.12 = (f32[512]{0:T(512)S(1)}, f32[512]{0:T(512)}, u32[]{:S(2)}) copy-start(f32[512]{0:T(512)} %param.13) | copy-start | bytes 6148

commit v8 on v7

--- a/solution.py
+++ b/solution.py
@@ -17,6 +17,8 @@
 MASKED = -1000000000.0 * LOG2E
 LN2 = math.log(2.0)
 SPLIT = ((0, 224), (224, 392))
+MAIN = 384
+LEFT = TOK - MAIN
 VIRTUAL = 16
 ROWS = 400
 MIB = 1024 * 1024
@@ -53,6 +55,24 @@
     for head in range(HEADS):
         at = pitch * (head % GROUP) + column
         ref[HD * head : HD * (head + 1), at : at + turned.shape[1]] = turned[HD * head : HD * (head + 1)]
+
+
+def left_rows(block):
+    rows = jnp.concatenate([block.astype(F32)] * HEADS, axis=0)
+    row = lax.broadcasted_iota(jnp.int32, rows.shape, 0) // LEFT
+    lane = lax.broadcasted_iota(jnp.int32, rows.shape, 1) // HD
+    return jnp.where(row == lane, rows, 0.0)
+
+
+def from_left(product):
+    turned = product.T
+    row = lax.broadcasted_iota(jnp.int32, turned.shape, 0) // LEFT
+    lane = lax.broadcasted_iota(jnp.int32, turned.shape, 1) // HD
+    return jnp.sum(jnp.where(row == lane, turned, 0.0).reshape(HEADS, LEFT, C), axis=0)
+
+
+def pair_channels(g, pair):
+    return pl.ds(pl.multiple_of(g * 128 + pair * 64, 64), 64)
 
 
 def channels_of(g, first=0):
@@ -133,7 +153,7 @@
 
 
 def forward_kernel(
-    x_ref, cot_ref, gain_ref, bias_ref, wqkv_ref, wout_ref, mixt_ref, stat_ref, *refs,
+    x_ref, cot_ref, gain_ref, bias_ref, wqkv_ref, wout_ref, mixt_ref, stat_ref, stat_left, *refs,
 ):
     y_own, y_ahead_there, y_behind, y_above_there, y_corner_there = refs[0:5]
     c_own, c_ahead_there, *c_later = refs[5:10]
@@ -150,24 +170,37 @@
         x = tiles(x_ref[rows])
         xhat, _ = standardized(x)
         normed = (xhat * gain_ref[...] + bias_ref[...]).astype(BF16)
-        put_diagonal(qbd, (mm(normed, wqkv_ref[:, 0:C]) * QSCALE).astype(BF16).T, 512)
+        queries = mm(normed, wqkv_ref[:, 0:C]) * QSCALE
+        put_diagonal(qbd, queries[0:MAIN].astype(BF16).T, MAIN)
         k[...] = mm(normed, wqkv_ref[:, C : 2 * C]).astype(BF16)
         vt[...] = mm(normed, wqkv_ref[:, 2 * C :]).astype(BF16).T
 
         def group(g, carry):
             kg = k[:, channels_of(g)]
-            for j in range(GROUP):
-                lanes = slice(512 * j, 512 * (j + 1))
+            for pair in range(2):
+                lanes = slice(768 * pair, 768 * (pair + 1))
                 scores = mm(kg, qbd[channels_of(g), lanes])
                 top = jnp.max(scores, axis=0, keepdims=True)
                 e = jnp.exp2(scores - top)
                 sums = jnp.sum(e, axis=0, keepdims=True)
-                mixed = mm(vt[head_channels(g, j), :], e.astype(BF16))
+                mixed = mm(vt[pair_channels(g, pair), :], e.astype(BF16)) * (1.0 / sums)
                 stat_ref[w, g, :, lanes] = top + jnp.log2(sums)
-                mixt_ref[w, head_channels(g, j), :] = (mixed * (1.0 / sums)).astype(BF16)
+                for i in range(2):
+                    mixt_ref[w, head_channels(g, 2 * pair + i), 0:MAIN] = mixed[
+                        HD * i : HD * (i + 1), MAIN * i : MAIN * (i + 1)
+                    ].astype(BF16)
             return carry
 
         lax.fori_loop(0, HEADS // GROUP, group, 0)
+        scores = mm(k[...], left_rows(queries[MAIN:TOK]).astype(BF16).T)
+        top = jnp.max(scores, axis=0, keepdims=True)
+        e = jnp.exp2(scores - top)
+        sums = jnp.sum(e, axis=0, keepdims=True)
+        stat_left[w] = top + jnp.log2(sums)
+        mixed = from_left(mm(vt[...], e.astype(BF16)) * (1.0 / sums))
+        mixt_ref[w, :, MAIN:512] = jnp.concatenate(
+            [mixed, jnp.zeros((128 - LEFT, C), F32)], axis=0
+        ).T.astype(BF16)
         y = x + mm_tn(mixt_ref[w, :, 0:TOK], wout_ref[...])
         pieces_of(y.reshape(7, 7, 8, C), w, (y_own, y_ahead, y_behind, y_above, y_corner))
         if w == 0:
@@ -179,9 +212,7 @@
     exchange.wait()
 
 
-def write_part(g, block, part):
-    turn = g % 3
-
+def write_part(turn, block, part):
     def layer(z, carry):
         for xy in range(16):
             x, y = xy // 4, xy % 4
@@ -197,10 +228,10 @@
     lax.fori_loop(0, 4, layer, 0)
 
 
-def group_gradients(scale, g, normed_t, dproj, mixt, cot_b, block, part):
+def group_gradients(scale, g, turn, normed_t, dproj, mixt, cot_b, block, part):
     block[:, 0:384] = mm(normed_t[...], dproj[:, columns_of(g)]) * scale
     block[:, 384:512] = mm(mixt[...], cot_b[:, channels_of(g)]) * scale
-    write_part(g, block, part)
+    write_part(turn, block, part)
 
 
 def columns_of(g):
@@ -247,7 +278,8 @@
 
 
 class Reduction:
-    def __init__(self, order, here, partners, part, local_sem, buffers, sems):
+    def __init__(self, order, plane, here, partners, part, local_sem, buffers, sems):
+        self.plane = plane
         self.order, self.here, self.partners, self.part = order, here, partners, part
         self.held, self.other, *self.slots = buffers
         self.local_sem, self.sems = local_sem, sems
@@ -283,6 +315,19 @@
             for away in (1, 2, 3)
         ]
 
+    def plane_copies(self):
+        a, b = self.order[1:]
+        copies = []
+        for i in range(1, 16):
+            da, db = i // 4, i % 4
+            partner = (b, db) if da == 0 else (a, da) if db == 0 else (a, b, da, db)
+            block = self.source(1).at[(self.here[a] + da) % 4, (self.here[b] + db) % 4]
+            copies.append(self.remote(3 + i, block, self.slots[1].at[da, db], self.partners[partner]))
+        return copies
+
+    def copies(self, step):
+        return self.plane_copies() if self.plane and step == 1 else self.axis_copies(step)
+
     def start(self):
         self.core_copy().start()
 
@@ -297,22 +342,29 @@
             for i in range(4):
                 self.held[i] = (own[i].astype(F32) + self.other[i].astype(F32)).astype(BF16)
         else:
-            for copy in self.axis_copies(stage - 1):
+            for copy in self.copies(stage - 1):
                 copy.wait_recv()
             total = self.source(stage - 1)[self.here[self.order[stage - 1]]].astype(F32)
+            if self.plane and stage == 2:
+                a, b = self.order[1:]
+                total = self.source(1)[self.here[a], self.here[b]].astype(F32)
+                for i in range(1, 16):
+                    total = total + self.slots[1][i // 4, i % 4].astype(F32)
+                out(total)
+                return
             for slot in range(3):
                 total = total + self.slots[stage - 1][slot].astype(F32)
             if stage == 3:
                 out(total)
                 return
             self.slots[stage - 1][3] = total.astype(BF16)
-        for copy in self.axis_copies(stage):
+        for copy in self.copies(stage):
             copy.start()
 
     def finish(self):
         self.core_copy().wait_send()
-        for step in range(3):
-            for copy in self.axis_copies(step):
+        for step in range(2 if self.plane else 3):
+            for copy in self.copies(step):
                 copy.wait_send()
 
 
@@ -321,18 +373,23 @@
 
 def backward_first_kernel(
     scale,
-    x_ref, gain_ref, bias_ref, wqkv_ref, wout_ref, mixt_ref, stat_ref,
+    x_ref, gain_ref, bias_ref, wqkv_ref, wout_ref, mixt_ref, stat_ref, stat_left,
     own, ahead, behind, above, corner, parts_second,
     grad_ref, gqkv1, gout1, gqkv2, gout2,
     normed_t, dproj, cot_b, mixt_all, wsorted, block, parts_first,
     qbd, k, kt, v, qn, don, dobd, p_s, ds_s, dqt, do_rows, q_rows, cot_s, xhat_s, rstd_s,
-    held, other, slots_a, slots_b, slots_c, local_sem, send_sem, recv_sem,
+    dk_left, dv_left, dq_left, held, other, slots_a, slots_b, slots_c, local_sem, send_sem, recv_sem,
 ):
     here = coordinates()
     partners = {("core", 1): beside(here, "core", 1)}
     for axis in "xyz":
         for away in (1, 2, 3):
             partners[axis, away] = beside(here, axis, away)
+    for dy in (1, 2, 3):
+        for dz in (1, 2, 3):
+            partners["y", "z", dy, dz] = device_at(
+                {**here, "y": (here["y"] + dy) % 4, "z": (here["z"] + dz) % 4}
+            )
     barrier = pltpu.get_barrier_semaphore()
     for partner in partners.values():
         pl.semaphore_signal(barrier, inc=1, device_id=partner, device_id_type=MESH)
@@ -341,7 +398,8 @@
         of_first = i < JOBS
         g = i % JOBS
         return Reduction(
-            ORDERS[g % 3],
+            ORDERS[0] if of_first else ORDERS[g % 3],
+            of_first,
             here,
             partners,
             parts_first.at[g] if of_first else parts_second.at[g],
@@ -376,7 +434,7 @@
         normed_t[:, 512 * w : 512 * w + TOK] = normed.T
         queries = (mm(normed, wqkv_ref[:, 0:C]) * QSCALE).astype(BF16)
         qn[w] = queries
-        put_diagonal(qbd.at[w], queries.T, 512)
+        put_diagonal(qbd.at[w], queries[0:MAIN].T, MAIN)
         keys = mm(normed, wqkv_ref[:, C : 2 * C]).astype(BF16)
         k[w] = keys
         kt[w] = keys.T
@@ -391,8 +449,18 @@
         cot_b[512 * w : 512 * w + TOK] = cot_h
         dmixed = mm_nt(cot_h, wout_ref[...]).astype(BF16)
         don[w] = dmixed
-        put_diagonal(dobd.at[w], dmixed.T, 512)
+        put_diagonal(dobd.at[w], dmixed[0:MAIN].T, MAIN)
         mixt_all[:, 512 * w : 512 * (w + 1)] = mixt_ref[w]
+        q_left = left_rows(queries[MAIN:TOK]).astype(BF16)
+        do_left = left_rows(dmixed[MAIN:TOK])
+        mixed = mixt_ref[w, :, MAIN:512].astype(F32).T[0:LEFT]
+        dsum = jnp.sum((do_left * jnp.concatenate([mixed] * HEADS, axis=0)).T, axis=0, keepdims=True)
+        do_left = do_left.astype(BF16)
+        p = jnp.exp2(mm(k[w], q_left.T) - stat_left[w])
+        ds = (p * (mm(v[w], do_left.T) - dsum)).astype(BF16)
+        dv_left[w] = mm(p.astype(BF16), do_left)
+        dk_left[w] = mm(ds, q_left)
+        dq_left[w] = from_left(mm(kt[w], ds))
         if w == 0:
             pl.semaphore_wait(barrier, len(partners))
             for reduction in second:
@@ -405,28 +473,36 @@
             qg = qn[w, :, channels_of(g)]
             dog = don[w, :, channels_of(g)]
             for j in range(GROUP):
-                lanes = slice(512 * j, 512 * (j + 1))
-                do_rows[w, 512 * j : 512 * j + TOK] = own_lanes(j, dog)
-                q_rows[w, 512 * j : 512 * j + TOK] = own_lanes(j, qg)
+                do_rows[w, MAIN * j : MAIN * (j + 1)] = own_lanes(j, dog[0:MAIN])
+                q_rows[w, MAIN * j : MAIN * (j + 1)] = own_lanes(j, qg[0:MAIN])
+            for pair in range(2):
+                lanes = slice(768 * pair, 768 * (pair + 1))
                 scores = mm(kg, qbd[w, channels_of(g), lanes])
                 p = jnp.exp2(scores - stat_ref[w, g, :, lanes]).astype(BF16)
                 p_s[w, :, lanes] = p
-                dsum = jnp.sum(
-                    mixt_ref[w, head_channels(g, j), :].astype(F32)
-                    * dobd[w, head_channels(g, j), lanes].astype(F32),
-                    axis=0, keepdims=True,
-                )
-                dp = mm(vg, dobd[w, channels_of(g), lanes]) - dsum
+                dsums = []
+                for j in (2 * pair, 2 * pair + 1):
+                    dsums.append(
+                        jnp.sum(
+                            mixt_ref[w, head_channels(g, j), 0:MAIN].astype(F32)
+                            * dobd[w, head_channels(g, j), MAIN * j : MAIN * (j + 1)].astype(F32),
+                            axis=0, keepdims=True,
+                        )
+                    )
+                dp = mm(vg, dobd[w, channels_of(g), lanes]) - jnp.concatenate(dsums, axis=1)
                 ds = (p.astype(F32) * dp).astype(BF16)
                 ds_s[w, :, lanes] = ds
-                dq = mm(kt[w, head_channels(g, j), :], ds)
-                dqt[w, HD * j : HD * (j + 1), :] = (dq[:, 0:TOK] * HD ** (-0.5)).astype(BF16)
-            dk = mm(ds_s[w], q_rows[w]) * LN2
-            dv = mm(p_s[w], do_rows[w])
+                dq = mm(kt[w, pair_channels(g, pair), :], ds)
+                for i in range(2):
+                    j = 2 * pair + i
+                    dqt[w, HD * j : HD * (j + 1), :] = dq[HD * i : HD * (i + 1), MAIN * i : MAIN * (i + 1)]
+            dk = (mm(ds_s[w], q_rows[w]) + dk_left[w, :, channels_of(g)]) * LN2
+            dv = mm(p_s[w], do_rows[w]) + dv_left[w, :, channels_of(g)]
+            dq = jnp.concatenate([dqt[w].T, dq_left[w, :, channels_of(g)]], axis=0) * HD ** (-0.5)
             dproj[512 * w : 512 * w + TOK, columns_of(g)] = jnp.concatenate(
-                [dqt[w].T, dk.astype(BF16), dv.astype(BF16)], axis=1
+                [dq.astype(BF16), dk.astype(BF16), dv.astype(BF16)], axis=1
             )
-        group_gradients(scale, g, normed_t, dproj, mixt_all, cot_b, block, parts_first.at[g])
+        group_gradients(scale, g, 0, normed_t, dproj, mixt_all, cot_b, block, parts_first.at[g])
         for now in range(JOBS):
 
             @pl.when(g == now)
@@ -435,19 +511,19 @@
                 for i in range(JOBS):
                     second[i].advance(now, result(JOBS + i))
                 for i in range(now):
-                    first[i].advance(now - 1 - i)
+                    first[i].advance(now - 1 - i, result(i))
 
         return carry
 
     lax.fori_loop(0, JOBS, group, 0)
-    for now in range(JOBS, 2 * JOBS):
+    for now in range(JOBS, 2 * JOBS - 1):
         w = now - JOBS
         if w < 2:
             dnormed = mm_nt(dproj[512 * w : 512 * w + TOK], wsorted[...])
             total = cot_s[w] + norm_backward(dnormed, xhat_s[w], rstd_s[w], gain_ref[...])
             grad_ref[7 * w : 7 * w + 7] = total.reshape(7, 7, 8, C).astype(BF16)
         for i in range(JOBS):
-            if 0 <= now - 1 - i <= 3:
+            if 0 <= now - 1 - i <= 2:
                 first[i].advance(now - 1 - i, result(i))
     for reduction in first + second:
         reduction.finish()
@@ -619,7 +695,7 @@
             exchange.send(3, corner, corner_there)
 
     def gradients(g, carry):
-        group_gradients(scale, g, normed_t, dproj, mixt, cot_b, block, parts.at[g])
+        group_gradients(scale, g, g % 3, normed_t, dproj, mixt, cot_b, block, parts.at[g])
         return carry
 
     lax.fori_loop(0, JOBS, gradients, 0)
@@ -633,7 +709,8 @@
 PARTS = [(JOBS, 2, 4, 4, 4, 4, 512)]
 SAVED = [
     jax.ShapeDtypeStruct((2, C, 512), BF16),
-    jax.ShapeDtypeStruct((2, HEADS // GROUP, 1, 2048), F32),
+    jax.ShapeDtypeStruct((2, HEADS // GROUP, 1, 4 * MAIN), F32),
+    jax.ShapeDtypeStruct((2, 1, 128), F32),
 ]
 TOKENS = (14, 7, 8, C)
 IN_VMEM = pl.BlockSpec(memory_space=pltpu.VMEM)
@@ -673,13 +750,13 @@
         (x, cot, *weights),
         SAVED + halves(pieces * 2),
         [(shape, BF16) for shape in (pieces[1], *pieces[3:], pieces[1])]
-        + [((C, 2048), BF16), ((TOK, C), BF16), ((C, TOK), BF16)],
+        + [((C, 4 * MAIN), BF16), ((TOK, C), BF16), ((C, TOK), BF16)],
         vmem=20,
-        there=(3, 5, 6, 8),
+        there=(4, 6, 7, 9),
         semaphores=[(5,)] * 2,
         collective_id=1,
     )
-    return outs[:2], outs[2:7], outs[7:]
+    return outs[:3], outs[3:8], outs[8:]
 
 
 GRADIENT_SCRATCH = [
@@ -698,17 +775,18 @@
         GRADIENT_SCRATCH
         + [(PARTS[0], BF16)]
         + [
-            ((2, C, 2048), BF16), ((2, TOK, C), BF16), ((2, C, TOK), BF16), ((2, TOK, C), BF16),
-            ((2, TOK, C), BF16), ((2, TOK, C), BF16), ((2, C, 2048), BF16),
-            ((2, TOK, 2048), BF16), ((2, TOK, 2048), BF16), ((2, 128, TOK), BF16),
-            ((2, 2048, 128), BF16), ((2, 2048, 128), BF16),
+            ((2, C, 4 * MAIN), BF16), ((2, TOK, C), BF16), ((2, C, TOK), BF16), ((2, TOK, C), BF16),
+            ((2, TOK, C), BF16), ((2, TOK, C), BF16), ((2, C, 4 * MAIN), BF16),
+            ((2, TOK, 4 * MAIN), BF16), ((2, TOK, 4 * MAIN), BF16), ((2, 128, MAIN), F32),
+            ((2, 4 * MAIN, 128), BF16), ((2, 4 * MAIN, 128), BF16),
             ((2, TOK, C), F32), ((2, TOK, C), F32), ((2, TOK, 1), F32),
+            ((2, TOK, C), F32), ((2, TOK, C), F32), ((2, LEFT, C), F32),
         ]
         + [((both, 4, 4, 4, 4, 512), BF16)] * 3
         + [((both, 4, 4, 4, 512), BF16), ((both, 4, 4, 512), BF16)],
         vmem=46,
         far=(len(args) - 1,),
-        semaphores=[(JOBS,), (both, 10), (both, 10)],
+        semaphores=[(JOBS,), (both, 19), (both, 19)],
         collective_id=3,
     )
 

time: 132 us -> 124 us (0.939)
  Pallas kernels: 125 us -> 117 us
    pallas_call x4, Pallas kernels: 125 us -> 117 us  [call(): pl.pallas_call(kernel, in_specs=[ANYWHERE if i in far else IN_VMEM for i...]
where the time goes in v8:
time: 124 us
  Pallas kernels  117 us (94%)
  local copies, waits for them, and re-layouts  6.13 us (5%)
    pallas_call x4, Pallas kernels, call(): pl.pallas_call(kernel, in_specs=[ANYWHERE if i in far else IN_VMEM for i...  117 us
    unnamed x30, local copies, waits for them, and re-layouts  6.13 us

profile of v8, /device:TPU:0, one launch (start us, length us, event | category | flops | bytes accessed | tf_op | source)
XLA Modules:
  0.0 123.6 jit_solution(5720336745776621542)
XLA Ops:
  0.6 0.0 copy-start
  0.6 1.4 %copy-done = bf16[512,1536]{1,0:T(8,128)(2,1)S(1)} copy-done((bf16[512,1536]{1,0:T(8,128)(2,1)S(1)}, bf16[512,1536]{1,0:T(8,128)(2,1)}, u32[]{:S(2)}) %copy-start) | copy-done | bytes 1572888
  2.0 1.1 copy-done.2
  3.2 1.0 copy-done.4
  4.2 1.1 copy-done.7
  5.4 0.7 copy-done.9
  6.0 0.7 copy-done.11
  6.7 24.7 %forward_first.1 = (bf16[2,512,512]{2,1,0:T(8,128)(2,1)S(1)}, f32[2,4,1,1536]{3,2,1,0:T(1,128)S(1)}, f32[2,1,128]{2,1,0:T(1,128)S(1)}, bf16[11,7,4,512]{3,2,1,0:...) custom-call(bf16[14,7,8,512]{3,2,1,0:T(8,128)(2,1)S(1)} %bitcast.7, ...), custom_call_target="tpu_custom_call" | custom-call | tf_op jit(solution)/shard_map/forward_first/pallas_call | solution.py:725
  31.4 0.0 copy-done.6
  31.4 0.0 copy-done.8
  31.5 0.0 copy-done.13
  31.5 0.0 copy-done.14
  31.5 0.0 copy-start.1
  31.5 0.0 copy-start.3
  31.5 0.0 copy-start.5
  31.5 0.0 copy-start.10
  31.5 0.0 copy-start.12
  31.5 40.6 %second_block.1 = (bf16[11,7,4,512]{3,2,1,0:T(4,128)(2,1)S(1)}, bf16[7,7,4,512]{3,2,1,0:T(4,128)(2,1)S(1)}, bf16[4,7,4,512]{3,2,1,0:T(4,128)(2,1)S(1)}, bf16[3,7...) custom-call(bf16[11,7,4,512]{3,2,1,0:T(4,128)(2,1)S(1)} %get-tuple-ele, ...), custom_call_target="tpu_custom_call" | custom-call | tf_op jit(solution)/shard_map/second_block/pallas_call | solution.py:725
  72.2 0.0 copy-done.1
  72.2 0.0 copy-done.3
  72.2 0.0 copy-done.5
  72.2 0.0 copy-done.10
  72.2 50.4 %backward_first.1 = (bf16[14,7,8,512]{3,2,1,0:T(8,128)(2,1)S(1)}, f32[4,1536]{1,0:T(4,128)S(1)}, f32[4,512]{1,0:T(4,128)S(1)}, f32[4,1536]{1,0:T(4,128)S(1)}, f32[4,512]{1,0:T(4,128)S(1)}) custom-call(bf16[14,7,8,512]{3,2,1,0:T(8,128)(2,1)S(1)} %bitcast.8, f32[1,512]{1,0:T(1,128)S(1)} %bitcast.11, f32[1,512]{1,0:T(1,128)S(1)} %bitcast.13, ...), custom_call_target="tpu_custom_call" | custom-call | tf_op jit(solution)/shard_map/backward_first/pallas_call | solution.py:725
  122.6 1.0 hand_on.1
  (10 shorter events, 0.0 us)
Async XLA Ops:
  0.6 1.4 %copy-start = (bf16[512,1536]{1,0:T(8,128)(2,1)S(1)}, bf16[512,1536]{1,0:T(8,128)(2,1)}, u32[]{:S(2)}) copy-start(bf16[512,1536]{1,0:T(8,128)(2,1)} %wqkv_ref.5) | copy-start | bytes 4718596
  2.0 1.1 copy-start.2
  3.2 1.0 copy-start.4
  4.2 1.1 copy-start.7
  5.4 0.7 copy-start.9
  6.0 0.7 copy-start.11
  6.7 24.7 %copy-start.6 = (bf16[512,1536]{1,0:T(8,128)(2,1)S(1)}, bf16[512,1536]{1,0:T(8,128)(2,1)}, u32[]{:S(2)}) copy-start(bf16[512,1536]{1,0:T(8,128)(2,1)} %wqkv_ref.4) | copy-start | bytes 4718596
  6.7 24.7 %copy-start.8 = (bf16[512,512]{1,0:T(8,128)(2,1)S(1)}, bf16[512,512]{1,0:T(8,128)(2,1)}, u32[]{:S(2)}) copy-start(bf16[512,512]{1,0:T(8,128)(2,1)} %wout_ref.4) | copy-start | bytes 1572868
  6.7 24.7 %copy-start.13 = (f32[512]{0:T(512)S(1)}, f32[512]{0:T(512)}, u32[]{:S(2)}) copy-start(f32[512]{0:T(512)} %param.16) | copy-start | bytes 6148
  6.7 24.7 %copy-start.14 = (f32[512]{0:T(512)S(1)}, f32[512]{0:T(512)}, u32[]{:S(2)}) copy-start(f32[512]{0:T(512)} %param.17) | copy-start | bytes 6148
  31.5 40.7 %copy-start.1 = (bf16[512,1536]{1,0:T(8,128)(2,1)S(1)}, bf16[512,1536]{1,0:T(8,128)(2,1)}, u32[]{:S(2)}) copy-start(bf16[512,1536]{1,0:T(8,128)(2,1)} %wqkv_ref.5) | copy-start | bytes 4718596
  31.5 40.7 %copy-start.3 = (bf16[8,14,7,512]{3,0,2,1:T(8,128)(2,1)S(1)}, bf16[8,14,7,512]{3,0,2,1:T(8,128)(2,1)}, u32[]{:S(2)}) copy-start(bf16[8,14,7,512]{3,0,2,1:T(8,128)(2,1)} %param.10) | copy-start | bytes 2408452
  31.5 40.7 %copy-start.5 = (bf16[512,512]{1,0:T(8,128)(2,1)S(1)}, bf16[512,512]{1,0:T(8,128)(2,1)}, u32[]{:S(2)}) copy-start(bf16[512,512]{1,0:T(8,128)(2,1)} %wout_ref.5) | copy-start | bytes 1572868
  31.5 40.7 %copy-start.10 = (f32[512]{0:T(512)S(1)}, f32[512]{0:T(512)}, u32[]{:S(2)}) copy-start(f32[512]{0:T(512)} %param.12) | copy-start | bytes 6148
  31.5 40.7 %copy-start.12 = (f32[512]{0:T(512)S(1)}, f32[512]{0:T(512)}, u32[]{:S(2)}) copy-start(f32[512]{0:T(512)} %param.13) | copy-start | bytes 6148

commit v9 on v8

--- a/solution.py
+++ b/solution.py
@@ -153,23 +153,37 @@
 
 
 def forward_kernel(
-    x_ref, cot_ref, gain_ref, bias_ref, wqkv_ref, wout_ref, mixt_ref, stat_ref, stat_left, *refs,
+    x_far, cot_far, gain_far, bias_far, wqkv_far, wout_far, mixt_ref, stat_ref, stat_left, *refs,
 ):
     y_own, y_ahead_there, y_behind, y_above_there, y_corner_there = refs[0:5]
     c_own, c_ahead_there, *c_later = refs[5:10]
-    y_ahead, y_above, y_corner, c_ahead, qbd, k, vt, send_sem, recv_sem = refs[10:]
+    y_ahead, y_above, y_corner, c_ahead, qbd, k, vt = refs[10:17]
+    x_ref, cot_ref, gain_ref, bias_ref, wqkv_ref, wout_ref, send_sem, recv_sem, load_sem = refs[17:]
+    loads = []
+    for far, near in (
+        (cot_far, cot_ref), (x_far, x_ref), (gain_far, gain_ref), (bias_far, bias_ref),
+        (wqkv_far, wqkv_ref), (wout_far, wout_ref),
+    ):
+        loads.append(pltpu.make_async_copy(far, near, load_sem.at[len(loads)]))
+        loads[-1].start()
     exchange = Exchange(1, send_sem, recv_sem)
     exchange.greet((1,))
+    qbd[...] = jnp.zeros_like(qbd)
+    loads[0].wait()
     for w in range(2):
         pieces_of(cot_ref[7 * w : 7 * w + 7].astype(F32), w, (c_own, c_ahead, *c_later))
     exchange.wait_for_others()
     exchange.send(0, c_ahead, c_ahead_there)
-    qbd[...] = jnp.zeros_like(qbd)
+    for load in loads[1:4]:
+        load.wait()
     for w in range(2):
         rows = slice(7 * w, 7 * w + 7)
         x = tiles(x_ref[rows])
         xhat, _ = standardized(x)
         normed = (xhat * gain_ref[...] + bias_ref[...]).astype(BF16)
+        if w == 0:
+            for load in loads[4:]:
+                load.wait()
         queries = mm(normed, wqkv_ref[:, 0:C]) * QSCALE
         put_diagonal(qbd, queries[0:MAIN].astype(BF16).T, MAIN)
         k[...] = mm(normed, wqkv_ref[:, C : 2 * C]).astype(BF16)
@@ -369,6 +383,7 @@
 
 
 JOBS = HEADS // GROUP
+SECOND_STAGES = {0: 0, 2: 1, 3: 2}
 
 
 def backward_first_kernel(
@@ -509,7 +524,8 @@
             def _():
                 first[now].start()
                 for i in range(JOBS):
-                    second[i].advance(now, result(JOBS + i))
+                    if now in SECOND_STAGES:
+                        second[i].advance(SECOND_STAGES[now])
                 for i in range(now):
                     first[i].advance(now - 1 - i, result(i))
 
@@ -522,9 +538,12 @@
             dnormed = mm_nt(dproj[512 * w : 512 * w + TOK], wsorted[...])
             total = cot_s[w] + norm_backward(dnormed, xhat_s[w], rstd_s[w], gain_ref[...])
             grad_ref[7 * w : 7 * w + 7] = total.reshape(7, 7, 8, C).astype(BF16)
-        for i in range(JOBS):
+        for i in reversed(range(JOBS)):
             if 0 <= now - 1 - i <= 2:
                 first[i].advance(now - 1 - i, result(i))
+        if now == JOBS:
+            for i in range(JOBS):
+                second[i].advance(3, result(JOBS + i))
     for reduction in first + second:
         reduction.finish()
 
@@ -717,6 +736,7 @@
 
 
 ANYWHERE = pl.BlockSpec(memory_space=pl.ANY)
+IN_HBM = pl.BlockSpec(memory_space=pltpu.HBM)
 
 
 def call(
@@ -724,7 +744,7 @@
 ):
     return pl.pallas_call(
         kernel,
-        in_specs=[ANYWHERE if i in far else IN_VMEM for i in range(len(args))],
+        in_specs=[IN_HBM if i in far else IN_VMEM for i in range(len(args))],
         out_specs=[ANYWHERE if i in there else IN_VMEM for i in range(len(out_shape))],
         out_shape=out_shape,
         scratch_shapes=[pltpu.VMEM(shape, dtype) for shape, dtype in scratch]
@@ -750,10 +770,13 @@
         (x, cot, *weights),
         SAVED + halves(pieces * 2),
         [(shape, BF16) for shape in (pieces[1], *pieces[3:], pieces[1])]
-        + [((C, 4 * MAIN), BF16), ((TOK, C), BF16), ((C, TOK), BF16)],
-        vmem=20,
+        + [((C, 4 * MAIN), BF16), ((TOK, C), BF16), ((C, TOK), BF16)]
+        + [(x.shape, BF16), (cot.shape, BF16)]
+        + [(weight.shape, weight.dtype) for weight in weights],
+        vmem=52,
+        far=range(6),
         there=(4, 6, 7, 9),
-        semaphores=[(5,)] * 2,
+        semaphores=[(5,), (5,), (6,)],
         collective_id=1,
     )
     return outs[:3], outs[3:8], outs[8:]

time: 124 us -> 117 us (0.944)
  Pallas kernels: 117 us -> 113 us
  local copies, waits for them, and re-layouts: 6.13 us -> 2.62 us
    unnamed x30 -> x24, local copies, waits for them, and re-layouts: 6.13 us -> 2.62 us
    pallas_call x4, Pallas kernels: 117 us -> 113 us  [call(): pl.pallas_call(kernel, in_specs=[IN_HBM if i in far else IN_VMEM for i in...]
where the time goes in v9:
time: 117 us
  Pallas kernels  113 us (97%)
  local copies, waits for them, and re-layouts  2.62 us (2%)
    pallas_call x4, Pallas kernels, call(): pl.pallas_call(kernel, in_specs=[IN_HBM if i in far else IN_VMEM for i in...  113 us
    unnamed x24, local copies, waits for them, and re-layouts  2.62 us

profile of v9, /device:TPU:0, one launch (start us, length us, event | category | flops | bytes accessed | tf_op | source)
XLA Modules:
  0.0 116.7 jit_solution(17241694455546606034)
XLA Ops:
  0.6 0.0 copy-start.6
  0.6 0.7 copy-done.6
  1.3 0.0 copy-start.8
  1.3 0.7 copy-done.8
  2.0 25.7 %forward_first.1 = (bf16[2,512,512]{2,1,0:T(8,128)(2,1)}, f32[2,4,1,1536]{3,2,1,0:T(1,128)S(1)}, f32[2,1,128]{2,1,0:T(1,128)S(1)}, bf16[11,7,4,512]{3,2,1,0:T(4,...) custom-call(bf16[14,7,8,512]{3,2,1,0:T(8,128)(2,1)} %bitcast.7, ...), custom_call_target="tpu_custom_call" | custom-call | tf_op jit(solution)/shard_map/forward_first/pallas_call | solution.py:745
  27.8 0.0 copy-done.3
  27.8 0.0 copy-done.5
  27.8 0.0 copy-done.10
  27.8 0.0 copy-done.11
  27.8 0.0 copy-start
  27.8 0.0 copy-start.1
  27.8 0.0 copy-start.2
  27.8 0.0 copy-start.7
  27.8 0.0 copy-start.9
  27.9 40.7 %second_block.1 = (bf16[11,7,4,512]{3,2,1,0:T(4,128)(2,1)S(1)}, bf16[7,7,4,512]{3,2,1,0:T(4,128)(2,1)S(1)}, bf16[4,7,4,512]{3,2,1,0:T(4,128)(2,1)S(1)}, bf16[3,7...) custom-call(bf16[11,7,4,512]{3,2,1,0:T(4,128)(2,1)S(1)} %get-tuple-ele, ...), custom_call_target="tpu_custom_call" | custom-call | tf_op jit(solution)/shard_map/second_block/pallas_call | solution.py:745
  68.6 0.0 copy-done
  68.6 0.0 copy-done.1
  68.6 0.0 copy-done.2
  68.6 0.0 copy-done.7
  68.6 0.0 copy-done.9
  68.6 0.0 copy-start.4
  68.6 1.2 %copy-done.4 = bf16[2,512,512]{2,1,0:T(8,128)(2,1)S(1)} copy-done((bf16[2,512,512]{2,1,0:T(8,128)(2,1)S(1)}, bf16[2,512,512]{2,1,0:T(8,128)(2,1)}, u32[]{:S(2)}) %copy-start.4) | copy-done | bytes 1048600
  69.8 45.9 %backward_first.1 = (bf16[14,7,8,512]{3,2,1,0:T(8,128)(2,1)S(1)}, f32[4,1536]{1,0:T(4,128)S(1)}, f32[4,512]{1,0:T(4,128)S(1)}, f32[4,1536]{1,0:T(4,128)S(1)}, f32[4,512]{1,0:T(4,128)S(1)}) custom-call(bf16[14,7,8,512]{3,2,1,0:T(8,128)(2,1)S(1)} %bitcast.8, f32[1,512]{1,0:T(1,128)S(1)} %bitcast.10, f32[1,512]{1,0:T(1,128)S(1)} %bitcast.12, ...), custom_call_target="tpu_custom_call" | custom-call | tf_op jit(solution)/shard_map/backward_first/pallas_call | solution.py:745
  115.7 1.0 hand_on.1
  (4 shorter events, 0.0 us)
Async XLA Ops:
  0.6 0.7 copy-start.6
  1.3 0.7 copy-start.8
  2.0 25.8 %copy-start.3 = (bf16[512,1536]{1,0:T(8,128)(2,1)S(1)}, bf16[512,1536]{1,0:T(8,128)(2,1)}, u32[]{:S(2)}) copy-start(bf16[512,1536]{1,0:T(8,128)(2,1)} %wqkv_ref.2) | copy-start | bytes 4718596
  2.0 25.8 %copy-start.5 = (bf16[512,512]{1,0:T(8,128)(2,1)S(1)}, bf16[512,512]{1,0:T(8,128)(2,1)}, u32[]{:S(2)}) copy-start(bf16[512,512]{1,0:T(8,128)(2,1)} %wout_ref.2) | copy-start | bytes 1572868
  2.0 25.8 %copy-start.10 = (f32[512]{0:T(512)S(1)}, f32[512]{0:T(512)}, u32[]{:S(2)}) copy-start(f32[512]{0:T(512)} %param.16) | copy-start | bytes 6148
  2.0 25.8 %copy-start.11 = (f32[512]{0:T(512)S(1)}, f32[512]{0:T(512)}, u32[]{:S(2)}) copy-start(f32[512]{0:T(512)} %param.17) | copy-start | bytes 6148
  27.8 40.8 %copy-start = (bf16[512,1536]{1,0:T(8,128)(2,1)S(1)}, bf16[512,1536]{1,0:T(8,128)(2,1)}, u32[]{:S(2)}) copy-start(bf16[512,1536]{1,0:T(8,128)(2,1)} %wqkv_ref.3) | copy-start | bytes 4718596
  27.8 40.8 %copy-start.1 = (bf16[8,14,7,512]{3,0,2,1:T(8,128)(2,1)S(1)}, bf16[8,14,7,512]{3,0,2,1:T(8,128)(2,1)}, u32[]{:S(2)}) copy-start(bf16[8,14,7,512]{3,0,2,1:T(8,128)(2,1)} %param.10) | copy-start | bytes 2408452
  27.8 40.8 %copy-start.2 = (bf16[512,512]{1,0:T(8,128)(2,1)S(1)}, bf16[512,512]{1,0:T(8,128)(2,1)}, u32[]{:S(2)}) copy-start(bf16[512,512]{1,0:T(8,128)(2,1)} %wout_ref.3) | copy-start | bytes 1572868
  27.8 40.8 %copy-start.7 = (f32[512]{0:T(512)S(1)}, f32[512]{0:T(512)}, u32[]{:S(2)}) copy-start(f32[512]{0:T(512)} %param.12) | copy-start | bytes 6148
  27.8 40.8 %copy-start.9 = (f32[512]{0:T(512)S(1)}, f32[512]{0:T(512)}, u32[]{:S(2)}) copy-start(f32[512]{0:T(512)} %param.13) | copy-start | bytes 6148
  68.6 1.2 %copy-start.4 = (bf16[2,512,512]{2,1,0:T(8,128)(2,1)S(1)}, bf16[2,512,512]{2,1,0:T(8,128)(2,1)}, u32[]{:S(2)}) copy-start(bf16[2,512,512]{2,1,0:T(8,128)(2,1)} %get-tuple-element.34.mixt_ref) | copy-start | bytes 3145732

commit v10 on v9

--- a/solution.py
+++ b/solution.py
@@ -252,6 +252,14 @@
     return pl.ds(pl.multiple_of(g * 384, 128), 384)
 
 
+def clear_padding(by_rows, by_lanes):
+    for w in range(2):
+        padding = slice(512 * w + MAIN, 512 * (w + 1))
+        for ref in by_rows:
+            ref[padding] = jnp.zeros((128, ref.shape[1]), BF16)
+        by_lanes[:, padding] = jnp.zeros((C, 128), BF16)
+
+
 def sort_columns(sorted_ref, wqkv_ref):
     for g in range(HEADS // GROUP):
         for i in range(3):
@@ -400,11 +408,12 @@
     for axis in "xyz":
         for away in (1, 2, 3):
             partners[axis, away] = beside(here, axis, away)
-    for dy in (1, 2, 3):
-        for dz in (1, 2, 3):
-            partners["y", "z", dy, dz] = device_at(
-                {**here, "y": (here["y"] + dy) % 4, "z": (here["z"] + dz) % 4}
-            )
+    for a, b in ("yz", "xy"):
+        for da in (1, 2, 3):
+            for db in (1, 2, 3):
+                partners[a, b, da, db] = device_at(
+                    {**here, a: (here[a] + da) % 4, b: (here[b] + db) % 4}
+                )
     barrier = pltpu.get_barrier_semaphore()
     for partner in partners.values():
         pl.semaphore_signal(barrier, inc=1, device_id=partner, device_id_type=MESH)
@@ -413,7 +422,7 @@
         of_first = i < JOBS
         g = i % JOBS
         return Reduction(
-            ORDERS[0] if of_first else ORDERS[g % 3],
+            ORDERS[g % 2 * 2] if of_first else ORDERS[g % 3],
             of_first,
             here,
             partners,
@@ -438,8 +447,9 @@
     first, second = [job(i) for i in range(JOBS)], [job(JOBS + i) for i in range(JOBS)]
     for reduction in second:
         reduction.local_copy().start()
-    for ref in (qbd, dobd, do_rows, q_rows, normed_t, dproj, cot_b):
+    for ref in (qbd, dobd):
         ref[...] = jnp.zeros_like(ref)
+    clear_padding((dproj, cot_b), normed_t)
     sort_columns(wsorted, wqkv_ref)
     for w in range(2):
         xhat, rstd = standardized(tiles(x_ref[7 * w : 7 * w + 7]))
@@ -517,7 +527,7 @@
             dproj[512 * w : 512 * w + TOK, columns_of(g)] = jnp.concatenate(
                 [dq.astype(BF16), dk.astype(BF16), dv.astype(BF16)], axis=1
             )
-        group_gradients(scale, g, 0, normed_t, dproj, mixt_all, cot_b, block, parts_first.at[g])
+        group_gradients(scale, g, g % 2 * 2, normed_t, dproj, mixt_all, cot_b, block, parts_first.at[g])
         for now in range(JOBS):
 
             @pl.when(g == now)
@@ -560,8 +570,9 @@
     exchange = Exchange(-1, send_sem, recv_sem)
     exchange.greet((1, -1))
     e_s, ds_s = (e_a, e_b), (ds_a, ds_b)
-    for ref in (qbd, dobd, do_rows, q_rows, normed_t, dproj, cot_b, mixt):
+    for ref in (qbd, dobd, q_rows, cot_b, mixt):
         ref[...] = jnp.zeros_like(ref)
+    clear_padding((dproj,), normed_t)
     sort_columns(wsorted, wqkv_ref)
     for w in range(2):
         base = 512 * w

time: 117 us -> 116 us (level)
  no operation moved by 1% of the time
where the time goes in v10:
time: 116 us
  Pallas kernels  113 us (97%)
  local copies, waits for them, and re-layouts  2.62 us (2%)
    pallas_call x4, Pallas kernels, call(): pl.pallas_call(kernel, in_specs=[IN_HBM if i in far else IN_VMEM for i in...  113 us
    unnamed x24, local copies, waits for them, and re-layouts  2.62 us

profile of v10, /device:TPU:0, one launch (start us, length us, event | category | flops | bytes accessed | tf_op | source)
XLA Modules:
  0.0 116.2 jit_solution(8820185477413002171)
XLA Ops:
  0.6 0.0 copy-start.6
  0.6 0.7 copy-done.6
  1.3 0.0 copy-start.8
  1.3 0.7 copy-done.8
  2.0 25.7 %forward_first.1 = (bf16[2,512,512]{2,1,0:T(8,128)(2,1)}, f32[2,4,1,1536]{3,2,1,0:T(1,128)S(1)}, f32[2,1,128]{2,1,0:T(1,128)S(1)}, bf16[11,7,4,512]{3,2,1,0:T(4,...) custom-call(bf16[14,7,8,512]{3,2,1,0:T(8,128)(2,1)} %bitcast.7, ...), custom_call_target="tpu_custom_call" | custom-call | tf_op jit(solution)/shard_map/forward_first/pallas_call | solution.py:756
  27.8 0.0 copy-done.3
  27.8 0.0 copy-done.5
  27.8 0.0 copy-done.10
  27.8 0.0 copy-done.11
  27.8 0.0 copy-start
  27.8 0.0 copy-start.1
  27.8 0.0 copy-start.2
  27.8 0.0 copy-start.7
  27.8 0.0 copy-start.9
  27.9 40.7 %second_block.1 = (bf16[11,7,4,512]{3,2,1,0:T(4,128)(2,1)S(1)}, bf16[7,7,4,512]{3,2,1,0:T(4,128)(2,1)S(1)}, bf16[4,7,4,512]{3,2,1,0:T(4,128)(2,1)S(1)}, bf16[3,7...) custom-call(bf16[11,7,4,512]{3,2,1,0:T(4,128)(2,1)S(1)} %get-tuple-ele, ...), custom_call_target="tpu_custom_call" | custom-call | tf_op jit(solution)/shard_map/second_block/pallas_call | solution.py:756
  68.6 0.0 copy-done
  68.6 0.0 copy-done.1
  68.6 0.0 copy-done.2
  68.6 0.0 copy-done.7
  68.6 0.0 copy-done.9
  68.6 0.0 copy-start.4
  68.6 1.2 %copy-done.4 = bf16[2,512,512]{2,1,0:T(8,128)(2,1)S(1)} copy-done((bf16[2,512,512]{2,1,0:T(8,128)(2,1)S(1)}, bf16[2,512,512]{2,1,0:T(8,128)(2,1)}, u32[]{:S(2)}) %copy-start.4) | copy-done | bytes 1048600
  69.8 45.4 %backward_first.1 = (bf16[14,7,8,512]{3,2,1,0:T(8,128)(2,1)S(1)}, f32[4,1536]{1,0:T(4,128)S(1)}, f32[4,512]{1,0:T(4,128)S(1)}, f32[4,1536]{1,0:T(4,128)S(1)}, f32[4,512]{1,0:T(4,128)S(1)}) custom-call(bf16[14,7,8,512]{3,2,1,0:T(8,128)(2,1)S(1)} %bitcast.8, f32[1,512]{1,0:T(1,128)S(1)} %bitcast.10, f32[1,512]{1,0:T(1,128)S(1)} %bitcast.12, ...), custom_call_target="tpu_custom_call" | custom-call | tf_op jit(solution)/shard_map/backward_first/pallas_call | solution.py:756
  115.3 1.0 hand_on.1
  (4 shorter events, 0.0 us)
Async XLA Ops:
  0.6 0.7 copy-start.6
  1.3 0.7 copy-start.8
  2.0 25.8 %copy-start.3 = (bf16[512,1536]{1,0:T(8,128)(2,1)S(1)}, bf16[512,1536]{1,0:T(8,128)(2,1)}, u32[]{:S(2)}) copy-start(bf16[512,1536]{1,0:T(8,128)(2,1)} %wqkv_ref.2) | copy-start | bytes 4718596
  2.0 25.8 %copy-start.5 = (bf16[512,512]{1,0:T(8,128)(2,1)S(1)}, bf16[512,512]{1,0:T(8,128)(2,1)}, u32[]{:S(2)}) copy-start(bf16[512,512]{1,0:T(8,128)(2,1)} %wout_ref.2) | copy-start | bytes 1572868
  2.0 25.8 %copy-start.10 = (f32[512]{0:T(512)S(1)}, f32[512]{0:T(512)}, u32[]{:S(2)}) copy-start(f32[512]{0:T(512)} %param.16) | copy-start | bytes 6148
  2.0 25.8 %copy-start.11 = (f32[512]{0:T(512)S(1)}, f32[512]{0:T(512)}, u32[]{:S(2)}) copy-start(f32[512]{0:T(512)} %param.17) | copy-start | bytes 6148
  27.8 40.8 %copy-start = (bf16[512,1536]{1,0:T(8,128)(2,1)S(1)}, bf16[512,1536]{1,0:T(8,128)(2,1)}, u32[]{:S(2)}) copy-start(bf16[512,1536]{1,0:T(8,128)(2,1)} %wqkv_ref.3) | copy-start | bytes 4718596
  27.8 40.8 %copy-start.1 = (bf16[8,14,7,512]{3,0,2,1:T(8,128)(2,1)S(1)}, bf16[8,14,7,512]{3,0,2,1:T(8,128)(2,1)}, u32[]{:S(2)}) copy-start(bf16[8,14,7,512]{3,0,2,1:T(8,128)(2,1)} %param.10) | copy-start | bytes 2408452
  27.8 40.8 %copy-start.2 = (bf16[512,512]{1,0:T(8,128)(2,1)S(1)}, bf16[512,512]{1,0:T(8,128)(2,1)}, u32[]{:S(2)}) copy-start(bf16[512,512]{1,0:T(8,128)(2,1)} %wout_ref.3) | copy-start | bytes 1572868
  27.8 40.8 %copy-start.7 = (f32[512]{0:T(512)S(1)}, f32[512]{0:T(512)}, u32[]{:S(2)}) copy-start(f32[512]{0:T(512)} %param.12) | copy-start | bytes 6148
  27.8 40.8 %copy-start.9 = (f32[512]{0:T(512)S(1)}, f32[512]{0:T(512)}, u32[]{:S(2)}) copy-start(f32[512]{0:T(512)} %param.13) | copy-start | bytes 6148
  68.6 1.2 %copy-start.4 = (bf16[2,512,512]{2,1,0:T(8,128)(2,1)S(1)}, bf16[2,512,512]{2,1,0:T(8,128)(2,1)}, u32[]{:S(2)}) copy-start(bf16[2,512,512]{2,1,0:T(8,128)(2,1)} %get-tuple-element.34.mixt_ref) | copy-start | bytes 3145732

commit v11 on v10

--- a/solution.py
+++ b/solution.py
@@ -396,13 +396,21 @@
 
 def backward_first_kernel(
     scale,
-    x_ref, gain_ref, bias_ref, wqkv_ref, wout_ref, mixt_ref, stat_ref, stat_left,
+    x_ref, gain_ref, bias_ref, wqkv_ref, wout_ref, mixt_far, stat_ref, stat_left,
     own, ahead, behind, above, corner, parts_second,
     grad_ref, gqkv1, gout1, gqkv2, gout2,
     normed_t, dproj, cot_b, mixt_all, wsorted, block, parts_first,
     qbd, k, kt, v, qn, don, dobd, p_s, ds_s, dqt, do_rows, q_rows, cot_s, xhat_s, rstd_s,
-    dk_left, dv_left, dq_left, held, other, slots_a, slots_b, slots_c, local_sem, send_sem, recv_sem,
+    dk_left, dv_left, dq_left, held, other, slots_a, slots_b, slots_c, local_sem, send_sem, recv_sem, load_sem,
 ):
+    loads = [
+        pltpu.make_async_copy(
+            mixt_far.at[w], mixt_all.at[:, 512 * w : 512 * (w + 1)], load_sem.at[w]
+        )
+        for w in range(2)
+    ]
+    for load in loads:
+        load.start()
     here = coordinates()
     partners = {("core", 1): beside(here, "core", 1)}
     for axis in "xyz":
@@ -475,10 +483,10 @@
         dmixed = mm_nt(cot_h, wout_ref[...]).astype(BF16)
         don[w] = dmixed
         put_diagonal(dobd.at[w], dmixed[0:MAIN].T, MAIN)
-        mixt_all[:, 512 * w : 512 * (w + 1)] = mixt_ref[w]
+        loads[w].wait()
         q_left = left_rows(queries[MAIN:TOK]).astype(BF16)
         do_left = left_rows(dmixed[MAIN:TOK])
-        mixed = mixt_ref[w, :, MAIN:512].astype(F32).T[0:LEFT]
+        mixed = mixt_all[:, 512 * w + MAIN : 512 * (w + 1)].astype(F32).T[0:LEFT]
         dsum = jnp.sum((do_left * jnp.concatenate([mixed] * HEADS, axis=0)).T, axis=0, keepdims=True)
         do_left = do_left.astype(BF16)
         p = jnp.exp2(mm(k[w], q_left.T) - stat_left[w])
@@ -509,7 +517,7 @@
                 for j in (2 * pair, 2 * pair + 1):
                     dsums.append(
                         jnp.sum(
-                            mixt_ref[w, head_channels(g, j), 0:MAIN].astype(F32)
+                            mixt_all[head_channels(g, j), 512 * w : 512 * w + MAIN].astype(F32)
                             * dobd[w, head_channels(g, j), MAIN * j : MAIN * (j + 1)].astype(F32),
                             axis=0, keepdims=True,
                         )
@@ -644,19 +652,20 @@
             for s, (start, stop) in enumerate(SPLIT):
                 count = stop - start
                 kg = k[start:stop, channels_of(g)]
-                apart = pen[start:stop] > 0.5
+                apart = jnp.concatenate([pen[start:stop]] * 2, axis=1) > 0.5
                 sums_of, invs = [], []
-                for j in range(GROUP):
-                    lanes = slice(256 * j, 256 * (j + 1))
-                    scores = mm(kg, qbd[channels_of(g), 1024 * s + 256 * j : 1024 * s + 256 * (j + 1)])
+                for pair in range(2):
+                    lanes = slice(512 * pair, 512 * (pair + 1))
+                    scores = mm(kg, qbd[channels_of(g), 1024 * s + 512 * pair : 1024 * s + 512 * (pair + 1)])
                     scores = jnp.where(apart, MASKED, scores)
                     top = jnp.maximum(jnp.max(scores, axis=0, keepdims=True), MASKED)
                     e = jnp.exp2(scores - top)
                     e_s[s][0:count, lanes] = e.astype(BF16)
                     rest = jnp.exp2(MASKED - top)
-                    first = lax.broadcasted_iota(jnp.int32, (VIRTUAL, 256), 0) == 0
+                    first = lax.broadcasted_iota(jnp.int32, (VIRTUAL, 512), 0) == 0
                     e_s[s][count : count + VIRTUAL, lanes] = jnp.where(first, rest, 0.0).astype(BF16)
-                    invs.append(1.0 / (jnp.sum(e, axis=0, keepdims=True) + (TOK - count) * rest))
+                    inv = 1.0 / (jnp.sum(e, axis=0, keepdims=True) + (TOK - count) * rest)
+                    invs += [inv[:, 0:256], inv[:, 256:512]]
                 for j in range(GROUP):
                     lanes = slice(256 * j, 256 * (j + 1))
                     tokens = slice(256 * s, 256 * (s + 1))
@@ -676,15 +685,19 @@
                 turned = dopt[:, 256 * s : 256 * (s + 1)].T
                 qg = qn[start:stop, channels_of(g)]
                 for j in range(GROUP):
-                    lanes = slice(256 * j, 256 * (j + 1))
                     at = 1024 * s + 256 * j
                     do_rows[at : at + 256] = own_lanes(j, turned)
                     q_rows[at : at + count] = own_lanes(j, qg)
-                    dp = mm(v[start:stop, channels_of(g)], dobd[:, at : at + 256]) - sums_of[j]
+                for pair in range(2):
+                    lanes = slice(512 * pair, 512 * (pair + 1))
+                    at = 1024 * s + 512 * pair
+                    dsum = jnp.concatenate(sums_of[2 * pair : 2 * pair + 2], axis=1)
+                    dp = mm(v[start:stop, channels_of(g)], dobd[:, at : at + 512]) - dsum
                     ds = e_s[s][0:count, lanes].astype(F32) * jnp.where(apart, 0.0, dp)
-                    ds = ds.astype(BF16)
-                    ds_s[s][:, lanes] = ds
-                    dq = mm(kt[head_channels(g, j), 256 * s : 256 * s + count], ds)
+                    ds_s[s][:, lanes] = ds.astype(BF16)
+                for j in range(GROUP):
+                    lanes = slice(256 * j, 256 * (j + 1))
+                    dq = mm(kt[head_channels(g, j), 256 * s : 256 * s + count], ds_s[s][:, lanes])
                     dqt[HD * j : HD * (j + 1), 256 * s : 256 * (s + 1)] = (dq * HD ** (-0.5)).astype(BF16)
                 block = slice(1024 * s, 1024 * (s + 1))
                 dv = mm(e_s[s][...], do_rows[block])
@@ -819,8 +832,8 @@
         + [((both, 4, 4, 4, 4, 512), BF16)] * 3
         + [((both, 4, 4, 4, 512), BF16), ((both, 4, 4, 512), BF16)],
         vmem=46,
-        far=(len(args) - 1,),
-        semaphores=[(JOBS,), (both, 19), (both, 19)],
+        far=(5, len(args) - 1),
+        semaphores=[(JOBS,), (both, 19), (both, 19), (2,)],
         collective_id=3,
     )
 

time: 116 us -> 110 us (0.948)
  Pallas kernels: 113 us -> 107 us
    pallas_call x4, Pallas kernels: 113 us -> 107 us  [call(): pl.pallas_call(kernel, in_specs=[IN_HBM if i in far else IN_VMEM for i in...]
where the time goes in v11:
time: 110 us
  Pallas kernels  107 us (97%)
  local copies, waits for them, and re-layouts  2.62 us (2%)
    pallas_call x4, Pallas kernels, call(): pl.pallas_call(kernel, in_specs=[IN_HBM if i in far else IN_VMEM for i in...  107 us
    unnamed x24, local copies, waits for them, and re-layouts  2.62 us

profile of v11, /device:TPU:0, one launch (start us, length us, event | category | flops | bytes accessed | tf_op | source)
XLA Modules:
  0.0 110.2 jit_solution(15503401696710661728)
XLA Ops:
  0.6 0.0 copy-start.6
  0.6 0.7 copy-done.6
  1.3 0.0 copy-start.8
  1.3 0.7 copy-done.8
  2.0 25.7 %forward_first.1 = (bf16[2,512,512]{2,1,0:T(8,128)(2,1)}, f32[2,4,1,1536]{3,2,1,0:T(1,128)S(1)}, f32[2,1,128]{2,1,0:T(1,128)S(1)}, bf16[11,7,4,512]{3,2,1,0:T(4,...) custom-call(bf16[14,7,8,512]{3,2,1,0:T(8,128)(2,1)} %bitcast.7, ...), custom_call_target="tpu_custom_call" | custom-call | tf_op jit(solution)/shard_map/forward_first/pallas_call | solution.py:769
  27.8 0.0 copy-done.3
  27.8 0.0 copy-done.5
  27.8 0.0 copy-done.10
  27.8 0.0 copy-done.11
  27.8 0.0 copy-start
  27.8 0.0 copy-start.1
  27.8 0.0 copy-start.2
  27.8 0.0 copy-start.7
  27.8 0.0 copy-start.9
  27.9 34.2 %second_block.1 = (bf16[11,7,4,512]{3,2,1,0:T(4,128)(2,1)S(1)}, bf16[7,7,4,512]{3,2,1,0:T(4,128)(2,1)S(1)}, bf16[4,7,4,512]{3,2,1,0:T(4,128)(2,1)S(1)}, bf16[3,7...) custom-call(bf16[11,7,4,512]{3,2,1,0:T(4,128)(2,1)S(1)} %get-tuple-ele, ...), custom_call_target="tpu_custom_call" | custom-call | tf_op jit(solution)/shard_map/second_block/pallas_call | solution.py:769
  62.0 0.0 copy-done
  62.1 0.0 copy-done.1
  62.1 0.0 copy-done.2
  62.1 0.0 copy-done.7
  62.1 0.0 copy-done.9
  62.1 0.0 copy-start.4
  62.1 1.2 %copy-done.4 = bf16[2,512,512]{2,1,0:T(8,128)(2,1)S(1)} copy-done((bf16[2,512,512]{2,1,0:T(8,128)(2,1)S(1)}, bf16[2,512,512]{2,1,0:T(8,128)(2,1)}, u32[]{:S(2)}) %copy-start.4) | copy-done | bytes 1048600
  63.3 45.9 %backward_first.1 = (bf16[14,7,8,512]{3,2,1,0:T(8,128)(2,1)S(1)}, f32[4,1536]{1,0:T(4,128)S(1)}, f32[4,512]{1,0:T(4,128)S(1)}, f32[4,1536]{1,0:T(4,128)S(1)}, f32[4,512]{1,0:T(4,128)S(1)}) custom-call(bf16[14,7,8,512]{3,2,1,0:T(8,128)(2,1)S(1)} %bitcast.8, f32[1,512]{1,0:T(1,128)S(1)} %bitcast.10, f32[1,512]{1,0:T(1,128)S(1)} %bitcast.12, ...), custom_call_target="tpu_custom_call" | custom-call | tf_op jit(solution)/shard_map/backward_first/pallas_call | solution.py:769
  109.3 1.0 hand_on.1
  (4 shorter events, 0.0 us)
Async XLA Ops:
  0.6 0.7 copy-start.6
  1.3 0.7 copy-start.8
  2.0 25.8 %copy-start.3 = (bf16[512,1536]{1,0:T(8,128)(2,1)S(1)}, bf16[512,1536]{1,0:T(8,128)(2,1)}, u32[]{:S(2)}) copy-start(bf16[512,1536]{1,0:T(8,128)(2,1)} %wqkv_ref.2) | copy-start | bytes 4718596
  2.0 25.8 %copy-start.5 = (bf16[512,512]{1,0:T(8,128)(2,1)S(1)}, bf16[512,512]{1,0:T(8,128)(2,1)}, u32[]{:S(2)}) copy-start(bf16[512,512]{1,0:T(8,128)(2,1)} %wout_ref.2) | copy-start | bytes 1572868
  2.0 25.8 %copy-start.10 = (f32[512]{0:T(512)S(1)}, f32[512]{0:T(512)}, u32[]{:S(2)}) copy-start(f32[512]{0:T(512)} %param.16) | copy-start | bytes 6148
  2.0 25.8 %copy-start.11 = (f32[512]{0:T(512)S(1)}, f32[512]{0:T(512)}, u32[]{:S(2)}) copy-start(f32[512]{0:T(512)} %param.17) | copy-start | bytes 6148
  27.8 34.2 %copy-start = (bf16[512,1536]{1,0:T(8,128)(2,1)S(1)}, bf16[512,1536]{1,0:T(8,128)(2,1)}, u32[]{:S(2)}) copy-start(bf16[512,1536]{1,0:T(8,128)(2,1)} %wqkv_ref.3) | copy-start | bytes 4718596
  27.8 34.2 %copy-start.1 = (bf16[8,14,7,512]{3,0,2,1:T(8,128)(2,1)S(1)}, bf16[8,14,7,512]{3,0,2,1:T(8,128)(2,1)}, u32[]{:S(2)}) copy-start(bf16[8,14,7,512]{3,0,2,1:T(8,128)(2,1)} %param.10) | copy-start | bytes 2408452
  27.8 34.2 %copy-start.2 = (bf16[512,512]{1,0:T(8,128)(2,1)S(1)}, bf16[512,512]{1,0:T(8,128)(2,1)}, u32[]{:S(2)}) copy-start(bf16[512,512]{1,0:T(8,128)(2,1)} %wout_ref.3) | copy-start | bytes 1572868
  27.8 34.2 %copy-start.7 = (f32[512]{0:T(512)S(1)}, f32[512]{0:T(512)}, u32[]{:S(2)}) copy-start(f32[512]{0:T(512)} %param.12) | copy-start | bytes 6148
  27.8 34.2 %copy-start.9 = (f32[512]{0:T(512)S(1)}, f32[512]{0:T(512)}, u32[]{:S(2)}) copy-start(f32[512]{0:T(512)} %param.13) | copy-start | bytes 6148
  62.1 1.2 %copy-start.4 = (bf16[2,512,512]{2,1,0:T(8,128)(2,1)S(1)}, bf16[2,512,512]{2,1,0:T(8,128)(2,1)}, u32[]{:S(2)}) copy-start(bf16[2,512,512]{2,1,0:T(8,128)(2,1)} %get-tuple-element.34.mixt_far) | copy-start | bytes 3145732
